TPU v7x, 32 devices: a whole 2x2x4 slice. The times are simulated.
32 devices in a mesh: dp: 4 (over y, x), seq: 2 (over core), tensor: 4 (over z).
Axes of the slice: x: 2, y: 2, z: 4, core: 2. Of those that a mesh axis runs over, the one named last changes fastest.
Arguments:
- tokens: bfloat16 [4, 2048, 1024], P('dp', 'seq'), may hold values from -6 to 6
- cotangent: bfloat16 [4, 2048, 1024], P('dp', 'seq'), may hold values from -6 to 6
- segments: int32 [4, 2048], P('dp', 'seq'), may hold values from 0 to 3, as said below
- positions: int32 [4, 2048], P('dp', 'seq'), may hold values from 0 to 4095, as said below
- attn_gain: bfloat16 [2, 1024], replicated, may hold values from 0.25 to 1.75
- w_query: bfloat16 [2, 1024, 2048], P(None, None, 'tensor'), may hold values from -0.1875 to 0.1875
- key_projection: bfloat16 [2, 1024, 1024], P(None, None, 'tensor'), may hold values from -0.1875 to 0.1875
- value_projection: bfloat16 [2, 1024, 1024], P(None, None, 'tensor'), may hold values from -0.1875 to 0.1875
- query_gain: bfloat16 [2, 128], replicated, may hold values from 0.25 to 1.75
- key_gain: bfloat16 [2, 128], replicated, may hold values from 0.25 to 1.75
- w_output: bfloat16 [2, 2048, 1024], P(None, 'tensor'), may hold values from -0.5 to 0.5
- mlp_gain: bfloat16 [2, 1024], replicated, may hold values from 0.25 to 1.75
- w_gate: bfloat16 [2, 1024, 3072], P(None, None, 'tensor'), may hold values from -0.1875 to 0.1875
- w_up: bfloat16 [2, 1024, 3072], P(None, None, 'tensor'), may hold values from -0.1875 to 0.1875
- w_down: bfloat16 [2, 3072, 1024], P(None, 'tensor'), may hold values from -0.109375 to 0.109375
Outputs:
- output: bfloat16 [4, 2048, 1024], P('dp', 'seq')
- input_grad: float32 [4, 2048, 1024], P('dp', 'seq')
- grad_attn_gain: float32 [2, 1024], replicated
- grad_query: float32 [2, 1024, 2048], P(None, ('dp', 'seq'), 'tensor')
- grad_key: float32 [2, 1024, 1024], P(None, ('dp', 'seq'), 'tensor')
- grad_value: float32 [2, 1024, 1024], P(None, ('dp', 'seq'), 'tensor')
- grad_query_gain: float32 [2, 128], replicated
- grad_key_gain: float32 [2, 128], replicated
- grad_output: float32 [2, 2048, 1024], P(None, 'tensor', ('dp', 'seq'))
- grad_mlp_gain: float32 [2, 1024], replicated
- grad_gate: float32 [2, 1024, 3072], P(None, ('dp', 'seq'), 'tensor')
- grad_up: float32 [2, 1024, 3072], P(None, ('dp', 'seq'), 'tensor')
- grad_down: float32 [2, 3072, 1024], P(None, 'tensor', ('dp', 'seq'))
Inputs may be any that keep to these rules, and one draw needn't show every extreme that they name: `segments`: along each sequence the numbers start at 0 and never fall; each sequence holds 4 documents. Within a document the positions rise by one from token to token.
All inputs are finite; a program needn't handle non-finite values.
Results may differ from a plain program's by a relative error of at most 0.033.
Values may be sent and summed in bfloat16 or wider, within the bound.
A program may use at most 320 MiB of HBM per device.

v0:
```python
import jax
import jax.numpy as jnp
from jax import lax
from jax.sharding import PartitionSpec as P

HEAD_SIZE = 128
LAYER_COUNT = 2
WINDOW = 1024


EPS = 1e-06
THETA = 1000000.0
NEG_FILL = -1e30


def shifted(array, axis, by):
    devices = lax.axis_size(axis)
    pairs = [(i, i + by) for i in range(devices) if 0 <= i + by < devices]
    return lax.ppermute(array, axis, pairs)


def rope_tables(places):
    halves = HEAD_SIZE // 2
    frequency = THETA ** (-(jnp.arange(halves, dtype=jnp.float32) * 2.0) / HEAD_SIZE)
    angle = places.astype(jnp.float32)[..., None] * frequency
    cosine = jnp.cos(angle)
    sine_part = jnp.sin(angle)
    return (
        jnp.concatenate([cosine, cosine], -1)[..., None, :],
        jnp.concatenate([sine_part, sine_part], -1)[..., None, :],
    )


def apply_rotary(value_block, rotary_tables):
    cosine, sine_part = rotary_tables
    halves = value_block.shape[-1] // 2
    turned = jnp.concatenate([-value_block[..., halves:], value_block[..., :halves]], -1)
    return value_block * cosine + turned * sine_part


def rotate_back(grad, rotary_tables):
    cosine, sine_part = rotary_tables
    halves = grad.shape[-1] // 2
    scaled = grad * sine_part
    return grad * cosine + jnp.concatenate([scaled[..., halves:], -scaled[..., :halves]], -1)


def norm_forward(value_block, gain):
    inverse = lax.rsqrt(jnp.mean(value_block * value_block, -1, keepdims=True) + EPS)
    normed = value_block * inverse
    return (normed * gain, normed, inverse)


def norm_backward(grad, gain, normed, inverse):
    scaled = grad * gain
    inner = jnp.mean(scaled * normed, -1, keepdims=True)
    gain_grad = jnp.sum((grad * normed).reshape(-1, grad.shape[-1]), 0)
    return (inverse * (scaled - normed * inner), gain_grad)


def forward_layer(hidden, weights, rotary_tables, visible, reach, stretch):
    gain_a, w_q, key_weight, value_weight, query_norm_scale, gain_k, w_o, gain_m, w_g, w_u, w_d = (
        weights
    )
    seqs_here = visible.shape[0]
    rows = hidden.shape[0]
    scale = HEAD_SIZE ** (-0.5)
    attention_input, attn_hat, attn_inverse = norm_forward(hidden, gain_a.astype(jnp.float32))
    attn_low = attention_input.astype(jnp.bfloat16)
    query_unnormed = jnp.dot(attn_low, w_q, preferred_element_type=jnp.float32).reshape(
        seqs_here, stretch, -1, HEAD_SIZE
    )
    key_unnormed = jnp.dot(attn_low, key_weight, preferred_element_type=jnp.float32).reshape(
        seqs_here, stretch, -1, HEAD_SIZE
    )
    values_low = jnp.dot(attn_low, value_weight, preferred_element_type=jnp.float32).astype(
        jnp.bfloat16
    )
    key_heads = key_unnormed.shape[2]
    q_normed, q_hat, q_inverse = norm_forward(query_unnormed, query_norm_scale.astype(jnp.float32))
    k_normed, k_hat, k_inverse = norm_forward(key_unnormed, gain_k.astype(jnp.float32))
    queries_low = apply_rotary(q_normed, rotary_tables).astype(jnp.bfloat16)
    keys_low = (
        apply_rotary(k_normed, rotary_tables)
        .astype(jnp.bfloat16)
        .reshape(seqs_here, stretch, key_heads * HEAD_SIZE)
    )
    local_pair = jnp.stack(
        [keys_low, values_low.reshape(seqs_here, stretch, key_heads * HEAD_SIZE)]
    )
    earlier = [shifted(local_pair, "seq", back) for back in range(reach, 0, -1)]
    window_pair = jnp.concatenate(earlier + [local_pair], 2)
    span = window_pair.shape[2]
    key_window = window_pair[0].reshape(seqs_here, span, key_heads, HEAD_SIZE)
    value_window = window_pair[1].reshape(seqs_here, span, key_heads, HEAD_SIZE)
    grouped = queries_low.reshape(seqs_here, stretch, key_heads, -1, HEAD_SIZE)
    scores = (
        jnp.einsum("sqhgd,skhd->shgqk", grouped, key_window, preferred_element_type=jnp.float32)
        * scale
    )
    scores = jnp.where(visible[:, None, None], scores, NEG_FILL)
    peak = jnp.max(scores, -1, keepdims=True)
    expo = jnp.exp(scores - peak)
    totals = jnp.sum(expo, -1, keepdims=True)
    probs_low = (expo / totals).astype(jnp.bfloat16)
    log_total = peak + jnp.log(totals)
    context_low = (
        jnp.einsum("shgqk,skhd->sqhgd", probs_low, value_window, preferred_element_type=jnp.float32)
        .astype(jnp.bfloat16)
        .reshape(rows, -1)
    )
    attn_part = jnp.dot(context_low, w_o, preferred_element_type=jnp.float32)
    hidden_mid = hidden + lax.psum(attn_part.astype(jnp.bfloat16), "tensor").astype(jnp.float32)
    mlp_in, mlp_hat, mlp_inverse = norm_forward(hidden_mid, gain_m.astype(jnp.float32))
    mlp_low = mlp_in.astype(jnp.bfloat16)
    gate = jnp.dot(mlp_low, w_g, preferred_element_type=jnp.float32)
    up_branch = jnp.dot(mlp_low, w_u, preferred_element_type=jnp.float32)
    act_low = (jax.nn.silu(gate) * up_branch).astype(jnp.bfloat16)
    mlp_part = jnp.dot(act_low, w_d, preferred_element_type=jnp.float32)
    hidden_next = hidden_mid + lax.psum(mlp_part.astype(jnp.bfloat16), "tensor").astype(jnp.float32)
    saved = dict(
        attn_hat=attn_hat,
        attn_inverse=attn_inverse,
        attn_low=attn_low,
        q_hat=q_hat,
        q_inverse=q_inverse,
        k_hat=k_hat,
        k_inverse=k_inverse,
        grouped=grouped,
        key_window=key_window,
        value_window=value_window,
        log_total=log_total,
        context_low=context_low,
        mlp_hat=mlp_hat,
        mlp_inverse=mlp_inverse,
        mlp_low=mlp_low,
        gate=gate,
        up_branch=up_branch,
        act_low=act_low,
    )
    return (hidden_next, saved)


def backward_layer(grad, weights, saved, rotary_tables, visible, reach, stretch):
    gain_a, w_q, key_weight, value_weight, query_norm_scale, gain_k, w_o, gain_m, w_g, w_u, w_d = (
        weights
    )
    seqs_here = visible.shape[0]
    rows = grad.shape[0]
    scale = HEAD_SIZE ** (-0.5)
    grad_low = grad.astype(jnp.bfloat16)
    grad_down_turned = jnp.einsum(
        "rf,rd->df", saved["act_low"], grad_low, preferred_element_type=jnp.float32
    )
    d_act = jnp.einsum("rd,fd->rf", grad_low, w_d, preferred_element_type=jnp.float32)
    gate = saved["gate"]
    sigma = jax.nn.sigmoid(gate)
    d_gate = (d_act * saved["up_branch"] * sigma * (1.0 + gate * (1.0 - sigma))).astype(
        jnp.bfloat16
    )
    d_up = (d_act * gate * sigma).astype(jnp.bfloat16)
    grad_gate = jnp.einsum(
        "rd,rf->df", saved["mlp_low"], d_gate, preferred_element_type=jnp.float32
    )
    grad_up = jnp.einsum("rd,rf->df", saved["mlp_low"], d_up, preferred_element_type=jnp.float32)
    d_mlp_part = jnp.einsum(
        "rf,df->rd", d_gate, w_g, preferred_element_type=jnp.float32
    ) + jnp.einsum("rf,df->rd", d_up, w_u, preferred_element_type=jnp.float32)
    d_mlp_in = lax.psum(d_mlp_part.astype(jnp.bfloat16), "tensor").astype(jnp.float32)
    d_mid, grad_gain_m = norm_backward(
        d_mlp_in, gain_m.astype(jnp.float32), saved["mlp_hat"], saved["mlp_inverse"]
    )
    grad_mid = grad + d_mid
    mid_low = grad_mid.astype(jnp.bfloat16)
    grad_o_turned = jnp.einsum(
        "rc,rd->dc", saved["context_low"], mid_low, preferred_element_type=jnp.float32
    )
    grouped = saved["grouped"]
    key_window = saved["key_window"]
    value_window = saved["value_window"]
    key_heads = key_window.shape[2]
    d_context = jnp.einsum("rd,cd->rc", mid_low, w_o, preferred_element_type=jnp.float32)
    d_context = d_context.astype(jnp.bfloat16).reshape(grouped.shape)
    scores = (
        jnp.einsum("sqhgd,skhd->shgqk", grouped, key_window, preferred_element_type=jnp.float32)
        * scale
    )
    scores = jnp.where(visible[:, None, None], scores, NEG_FILL)
    probs = jnp.exp(scores - saved["log_total"])
    d_probs = jnp.einsum(
        "sqhgd,skhd->shgqk", d_context, value_window, preferred_element_type=jnp.float32
    )
    inner = jnp.sum(probs * d_probs, -1, keepdims=True)
    d_scores = (probs * (d_probs - inner)).astype(jnp.bfloat16)
    d_queries = (
        jnp.einsum("shgqk,skhd->sqhgd", d_scores, key_window, preferred_element_type=jnp.float32)
        * scale
    )
    d_key_window = (
        jnp.einsum("shgqk,sqhgd->skhd", d_scores, grouped, preferred_element_type=jnp.float32)
        * scale
    )
    d_value_window = jnp.einsum(
        "shgqk,sqhgd->skhd",
        probs.astype(jnp.bfloat16),
        d_context,
        preferred_element_type=jnp.float32,
    )
    span = key_window.shape[1]
    d_pair = jnp.stack([d_key_window, d_value_window]).reshape(
        2, seqs_here, span, key_heads * HEAD_SIZE
    )
    own_pair = d_pair[:, :, reach * stretch :]
    for back in range(1, reach + 1):
        piece = d_pair[:, :, (reach - back) * stretch : (reach - back + 1) * stretch]
        own_pair = own_pair + shifted(piece.astype(jnp.bfloat16), "seq", -back).astype(piece.dtype)
    d_keys = own_pair[0].reshape(seqs_here, stretch, key_heads, HEAD_SIZE)
    d_values_low = own_pair[1].astype(jnp.bfloat16).reshape(rows, -1)
    d_q_normed = rotate_back(d_queries.reshape(seqs_here, stretch, -1, HEAD_SIZE), rotary_tables)
    d_k_normed = rotate_back(d_keys, rotary_tables)
    d_q_raw, grad_gain_q = norm_backward(
        d_q_normed, query_norm_scale.astype(jnp.float32), saved["q_hat"], saved["q_inverse"]
    )
    d_k_raw, grad_gain_k = norm_backward(
        d_k_normed, gain_k.astype(jnp.float32), saved["k_hat"], saved["k_inverse"]
    )
    d_q_low = d_q_raw.astype(jnp.bfloat16).reshape(rows, -1)
    d_k_low = d_k_raw.astype(jnp.bfloat16).reshape(rows, -1)
    attn_low = saved["attn_low"]
    grad_q = jnp.einsum("rd,rc->dc", attn_low, d_q_low, preferred_element_type=jnp.float32)
    grad_k = jnp.einsum("rd,rc->dc", attn_low, d_k_low, preferred_element_type=jnp.float32)
    grad_v = jnp.einsum("rd,rc->dc", attn_low, d_values_low, preferred_element_type=jnp.float32)
    d_attn_part = (
        jnp.einsum("rc,dc->rd", d_q_low, w_q, preferred_element_type=jnp.float32)
        + jnp.einsum("rc,dc->rd", d_k_low, key_weight, preferred_element_type=jnp.float32)
        + jnp.einsum("rc,dc->rd", d_values_low, value_weight, preferred_element_type=jnp.float32)
    )
    d_attn_in, grad_gain_q, grad_gain_k = (
        lax.psum(d_attn_part.astype(jnp.bfloat16), "tensor").astype(jnp.float32),
        lax.psum(grad_gain_q.astype(jnp.bfloat16), "tensor").astype(jnp.float32),
        lax.psum(grad_gain_k.astype(jnp.bfloat16), "tensor").astype(jnp.float32),
    )
    d_hidden, grad_gain_a = norm_backward(
        d_attn_in, gain_a.astype(jnp.float32), saved["attn_hat"], saved["attn_inverse"]
    )
    gain_grads = (grad_gain_a, grad_gain_q, grad_gain_k, grad_gain_m)
    matrix_grads = (grad_q, grad_k, grad_v, grad_o_turned, grad_gate, grad_up, grad_down_turned)
    return (grad_mid + d_hidden, gain_grads, matrix_grads)


def reduce_grads(gain_grads, matrix_grads):
    gain_a, gain_q, gain_k, gain_m = gain_grads
    gain_a, gain_q, gain_k, gain_m = lax.psum((gain_a, gain_q, gain_k, gain_m), ("dp", "seq"))
    grad_q, grad_k, grad_v, grad_o_turned, grad_gate, grad_up, grad_down_turned = matrix_grads
    grad_q, grad_k, grad_v, grad_o_turned, grad_gate, grad_up, grad_down_turned = (
        lax.psum_scatter(
            grad_q.astype(jnp.bfloat16), ("dp", "seq"), scatter_dimension=0, tiled=True
        ).astype(jnp.float32),
        lax.psum_scatter(
            grad_k.astype(jnp.bfloat16), ("dp", "seq"), scatter_dimension=0, tiled=True
        ).astype(jnp.float32),
        lax.psum_scatter(
            grad_v.astype(jnp.bfloat16), ("dp", "seq"), scatter_dimension=0, tiled=True
        ).astype(jnp.float32),
        lax.psum_scatter(
            grad_o_turned.astype(jnp.bfloat16), ("dp", "seq"), scatter_dimension=0, tiled=True
        ).astype(jnp.float32),
        lax.psum_scatter(
            grad_gate.astype(jnp.bfloat16), ("dp", "seq"), scatter_dimension=0, tiled=True
        ).astype(jnp.float32),
        lax.psum_scatter(
            grad_up.astype(jnp.bfloat16), ("dp", "seq"), scatter_dimension=0, tiled=True
        ).astype(jnp.float32),
        lax.psum_scatter(
            grad_down_turned.astype(jnp.bfloat16), ("dp", "seq"), scatter_dimension=0, tiled=True
        ).astype(jnp.float32),
    )
    return [
        gain_a,
        grad_q,
        grad_k,
        grad_v,
        gain_q,
        gain_k,
        grad_o_turned.T,
        gain_m,
        grad_gate,
        grad_up,
        grad_down_turned.T,
    ]


def per_device(
    tokens,
    cotangent,
    segments,
    positions,
    attn_gain,
    w_query,
    key_projection,
    value_projection,
    query_gain,
    key_gain,
    w_output,
    mlp_gain,
    w_gate,
    w_up,
    w_down,
):
    seqs_here, stretch, width = tokens.shape
    rows = seqs_here * stretch
    seq_count = lax.axis_size("seq")
    place = lax.axis_index("seq")
    reach = min(seq_count - 1, (WINDOW + stretch - 2) // stretch)
    span = (reach + 1) * stretch
    every_doc = lax.all_gather(segments, "seq", axis=1, tiled=True)
    padded_docs = jnp.concatenate(
        [jnp.full((seqs_here, reach * stretch), -1, jnp.int32), every_doc], 1
    )
    key_docs = lax.dynamic_slice_in_dim(padded_docs, place * stretch, span, 1)
    query_index = place * stretch + jnp.arange(stretch, dtype=jnp.int32)
    key_index = (place - reach) * stretch + jnp.arange(span, dtype=jnp.int32)
    distance = query_index[:, None] - key_index[None, :]
    in_window = (distance >= 0) & (distance < WINDOW) & (key_index[None, :] >= 0)
    visible = in_window[None] & (segments[:, :, None] == key_docs[:, None, :])
    rotary_tables = rope_tables(positions)
    stacked = (
        attn_gain,
        w_query,
        key_projection,
        value_projection,
        query_gain,
        key_gain,
        w_output,
        mlp_gain,
        w_gate,
        w_up,
        w_down,
    )
    hidden = tokens.astype(jnp.float32).reshape(rows, width)
    saved_layers = []
    for layer_index in range(LAYER_COUNT):
        weights = tuple((w[layer_index] for w in stacked))
        hidden, saved = forward_layer(hidden, weights, rotary_tables, visible, reach, stretch)
        saved_layers.append(saved)
    output = hidden.astype(jnp.bfloat16).reshape(seqs_here, stretch, width)
    grad = cotangent.astype(jnp.float32).reshape(rows, width)
    reduced = [None] * LAYER_COUNT
    for layer_index in range(LAYER_COUNT - 1, -1, -1):
        weights = tuple((w[layer_index] for w in stacked))
        grad, gain_grads, matrix_grads = backward_layer(
            grad, weights, saved_layers[layer_index], rotary_tables, visible, reach, stretch
        )
        reduced[layer_index] = reduce_grads(gain_grads, matrix_grads)
    input_grad = grad.reshape(seqs_here, stretch, width)
    outs = [
        jnp.stack([reduced[layer_index][slot] for layer_index in range(LAYER_COUNT)])
        for slot in range(11)
    ]
    return (
        output,
        input_grad,
        outs[0],
        outs[1],
        outs[2],
        outs[3],
        outs[4],
        outs[5],
        outs[6],
        outs[7],
        outs[8],
        outs[9],
        outs[10],
    )


def solution(mesh):
    placed = (
        P("dp", "seq", None),
        P("dp", "seq", None),
        P("dp", "seq"),
        P("dp", "seq"),
        P(),
        P(None, None, "tensor"),
        P(None, None, "tensor"),
        P(None, None, "tensor"),
        P(),
        P(),
        P(None, "tensor", None),
        P(),
        P(None, None, "tensor"),
        P(None, None, "tensor"),
        P(None, "tensor", None),
    )
    return jax.shard_map(
        per_device,
        mesh=mesh,
        in_specs=placed,
        out_specs=(
            P("dp", "seq", None),
            P("dp", "seq", None),
            P(),
            P(None, ("dp", "seq"), "tensor"),
            P(None, ("dp", "seq"), "tensor"),
            P(None, ("dp", "seq"), "tensor"),
            P(),
            P(),
            P(None, "tensor", ("dp", "seq")),
            P(),
            P(None, ("dp", "seq"), "tensor"),
            P(None, ("dp", "seq"), "tensor"),
            P(None, "tensor", ("dp", "seq")),
        ),
        check_vma=False,
    )
```

profile of v0, /device:TPU:0, one launch (start us, length us, event | category | flops | bytes accessed | tf_op | source)
XLA Modules:
  0.0 1649.7 jit_solution(1598264823038468996)
XLA Ops:
  14.7 3.3 multiply_multiply_fusion.3
  27.6 3.3 collective-permute-start
  43.8 3.8 fusion.26
  50.1 14.2 fusion.215
  64.3 13.1 fusion.6
  77.4 14.1 fusion.115
  95.9 88.1 %all-reduce.12.cloned.1.call-done = bf16[1024,1024]{1,0:T(8,128)(2,1)} async-done(((bf16[1024,1024]{1,0:T(8,128)(2,1)}), bf16[1024,1024]{1,0:T(8,128)(2,1)}) %all-reduce.12.cloned.1.call-update) | async-done | bytes 2097168 | tf_op jit(solution)/shard_map/psum | solution.py:113
  191.0 3.6 multiply_convert_fusion.8
  199.5 85.1 %all-reduce.14.cloned.1.call-done = bf16[1024,1024]{1,0:T(8,128)(2,1)} async-done(((bf16[1024,1024]{1,0:T(8,128)(2,1)}), bf16[1024,1024]{1,0:T(8,128)(2,1)}) %all-reduce.14.cloned.1.call-update) | async-done | bytes 2097168 | tf_op jit(solution)/shard_map/psum | solution.py:120
  302.8 3.3 multiply_multiply_fusion.2
  323.6 14.1 fusion.216
  337.7 13.1 fusion.7
  350.8 14.0 fusion.118
  368.7 85.6 %all-reduce.16.cloned.1.call-done = bf16[1024,1024]{1,0:T(8,128)(2,1)} async-done(((bf16[1024,1024]{1,0:T(8,128)(2,1)}), bf16[1024,1024]{1,0:T(8,128)(2,1)}) %all-reduce.16.cloned.1.call-update) | async-done | bytes 2097168 | tf_op jit(solution)/shard_map/psum | solution.py:113
  454.3 3.5 multiply_reduce_fusion
  466.4 4.8 multiply_convert_fusion.5
  479.4 82.4 %all-reduce.18.cloned.1.call-done = bf16[1024,1024]{1,0:T(8,128)(2,1)} async-done(((bf16[1024,1024]{1,0:T(8,128)(2,1)}), bf16[1024,1024]{1,0:T(8,128)(2,1)}) %all-reduce.18.cloned.1.call-update) | async-done | bytes 2097168 | tf_op jit(solution)/shard_map/psum | solution.py:169
  561.9 4.8 fusion.57
  572.5 21.7 %fusion.3 = (f32[2,2,1024]{2,1,0:T(2,128)S(1)}, f32[2,2048,1024,2]{2,1,3,0:T(8,128)}) fusion(f32[1,2,2,1024,2048]{3,4,2,1,0:T(8,128)} %get-tuple-element.141, f32[2,2,1024]{2,1,0:T(2,128)S(1)} %log_add_fusion.1, bf16[2048,2,128,1]{0,2,3,1:T(8,128)(2,1)S(1)} %bitcast.645, bf16[1024,2,2,128]{0,3,2,1:T(8,128)(2,1)S(1)} %bitcast.626), kind=kOutput, calls=%fused_computation.9 | convolution fusion | flops 2172645376 | bytes 69238784 | tf_op jit(solution)/shard_map/sqhgd,skhd->shgqk/dot_general | solution.py:190
  594.2 13.8 fusion.14
  608.1 29.2 %fusion.16 = bf16[2,2,1024,2048]{2,3,1,0:T(8,128)(2,1)} fusion(f32[2,2048,1024,2]{2,1,3,0:T(8,128)} %get-tuple-element.143, f32[1,2,2,1024,2048]{3,4,2,1,0:T(8,128)} %get-tuple-element.141, f32[2,2,1024]{2,1,0:T(2,128)S(1)} %get-tuple-element.142, f32[2,2,1024]{2,1,0:T(2,128)S(1)} %log_add_fusion.1), kind=kLoop, calls=%fused_computation.26 | loop fusion | flops 33554432 | bytes 83918848 | tf_op jit(solution)/shard_map/reshape.86
  637.3 10.5 bitcast_multiply_fusion.15
  647.8 13.1 fusion.63
  682.9 5.7 multiply_reduce_fusion.10
  699.3 86.9 %all-reduce.20.cloned.1.call-done = bf16[1024,1024]{1,0:T(8,128)(2,1)} async-done(((bf16[1024,1024]{1,0:T(8,128)(2,1)}), bf16[1024,1024]{1,0:T(8,128)(2,1)}) %all-reduce.20.cloned.1.call-update) | async-done | bytes 2097168 | tf_op jit(solution)/shard_map/psum | solution.py:239
  786.2 4.9 fusion.58
  791.1 3.3 fusion.48
  797.7 3.5 multiply_convert_fusion.3
  809.0 4.4 fusion.112
  813.4 5.7 convolution_convert_fusion.4
  819.2 5.3 convolution_convert_fusion.5
  825.0 4.5 convolution_convert_fusion.6
  829.5 5.1 convolution_convert_fusion.7
  834.7 4.4 convolution_convert_fusion.8
  839.3 4.9 convolution_convert_fusion.9
  844.3 48.8 %all-reduce.22.cloned.1.call-done = bf16[1024,1024]{1,0:T(8,128)(2,1)} async-done(((bf16[1024,1024]{1,0:T(8,128)(2,1)}), bf16[1024,1024]{1,0:T(8,128)(2,1)}) %all-reduce.22.cloned.1.call-update) | async-done | bytes 2097168 | tf_op jit(solution)/shard_map/psum | solution.py:169
  893.1 4.1 fusion.59
  904.7 4.2 convolution_convert_fusion.11
  909.2 3.9 convolution_convert_fusion.13
  913.0 22.4 %fusion = (f32[2,2,1024]{2,1,0:T(2,128)S(1)}, f32[2,2048,1024,2]{2,1,3,0:T(8,128)}) fusion(f32[1,2,2,1024,2048]{3,4,2,1,0:T(8,128)} %get-tuple-element.137, f32[2,2,1024]{2,1,0:T(2,128)S(1)} %log_add_fusion, bf16[2048,2,128,1]{0,2,3,1:T(8,128)(2,1)S(1)} %bitcast.643, bf16[1024,2,2,128]{0,3,2,1:T(8,128)(2,1)S(1)} %bitcast.624), kind=kOutput, calls=%fused_computation.4 | convolution fusion | flops 2172645376 | bytes 69238784 | tf_op jit(solution)/shard_map/sqhgd,skhd->shgqk/dot_general | solution.py:190
  935.5 28.7 %fusion.17 = bf16[2,2,1024,2048]{2,3,1,0:T(8,128)(2,1)} fusion(f32[2,2048,1024,2]{2,1,3,0:T(8,128)} %get-tuple-element.147, f32[1,2,2,1024,2048]{3,4,2,1,0:T(8,128)} %get-tuple-element.137, f32[2,2,1024]{2,1,0:T(2,128)S(1)} %get-tuple-element.146, f32[2,2,1024]{2,1,0:T(2,128)S(1)} %log_add_fusion), kind=kLoop, calls=%fused_computation.27 | loop fusion | flops 33554432 | bytes 83918848 | tf_op jit(solution)/shard_map/reshape.106
  964.1 8.6 bitcast_multiply_fusion.13
  977.8 3.4 fusion.73
  984.7 15.9 fusion.11
  1000.9 13.2 fusion.62
  1027.3 5.3 convolution_convert_fusion.2
  1042.7 5.7 multiply_reduce_fusion.9
  1056.8 4.2 fusion.186
  1063.7 3.9 add_convert_fusion
  1087.8 12.9 reduce-scatter.33.cloned.1.call-done
  1100.7 41.6 %reduce-scatter.31.cloned.1.call-done = bf16[128,768]{1,0:T(8,128)(2,1)} async-done(((bf16[1024,768]{1,0:T(8,128)(2,1)}), bf16[128,768]{1,0:T(8,128)(2,1)}) %reduce-scatter.31.cloned.1.call-update) | async-done | bytes 196624 | tf_op jit(solution)/shard_map/reduce_scatter | solution.py:268
  1149.5 3.5 fusion.148
  1153.1 12.0 all-reduce.2
  1165.1 16.5 reduce-scatter.29.cloned.1.call-done
  1181.6 39.1 %reduce-scatter.27.cloned.1.call-done = bf16[128,512]{1,0:T(8,128)(2,1)} async-done(((bf16[1024,512]{1,0:T(8,128)(2,1)}), bf16[128,512]{1,0:T(8,128)(2,1)}) %reduce-scatter.27.cloned.1.call-update) | async-done | bytes 131088 | tf_op jit(solution)/shard_map/reduce_scatter | solution.py:265
  1222.6 37.0 %reduce-scatter.17.cloned.1.call-done = bf16[128,512]{1,0:T(8,128)(2,1)} async-done(((bf16[1024,512]{1,0:T(8,128)(2,1)}), bf16[128,512]{1,0:T(8,128)(2,1)}) %reduce-scatter.17.cloned.1.call-update) | async-done | bytes 131088 | tf_op jit(solution)/shard_map/reduce_scatter | solution.py:256
  1259.6 39.1 %reduce-scatter.15.cloned.1.call-done = bf16[128,512]{1,0:T(8,128)(2,1)} async-done(((bf16[1024,512]{1,0:T(8,128)(2,1)}), bf16[128,512]{1,0:T(8,128)(2,1)}) %reduce-scatter.15.cloned.1.call-update) | async-done | bytes 131088 | tf_op jit(solution)/shard_map/reduce_scatter | solution.py:256
  1300.5 35.3 %reduce-scatter.25.cloned.1.call-done = bf16[128,256]{1,0:T(8,128)(2,1)} async-done(((bf16[1024,256]{1,0:T(8,128)(2,1)}), bf16[128,256]{1,0:T(8,128)(2,1)}) %reduce-scatter.25.cloned.1.call-update) | async-done | bytes 65552 | tf_op jit(solution)/shard_map/reduce_scatter | solution.py:262
  1335.8 37.4 %reduce-scatter.23.cloned.1.call-done = bf16[128,256]{1,0:T(8,128)(2,1)} async-done(((bf16[1024,256]{1,0:T(8,128)(2,1)}), bf16[128,256]{1,0:T(8,128)(2,1)}) %reduce-scatter.23.cloned.1.call-update) | async-done | bytes 65552 | tf_op jit(solution)/shard_map/reduce_scatter | solution.py:262
  1374.8 35.6 %reduce-scatter.21.cloned.1.call-done = bf16[128,256]{1,0:T(8,128)(2,1)} async-done(((bf16[1024,256]{1,0:T(8,128)(2,1)}), bf16[128,256]{1,0:T(8,128)(2,1)}) %reduce-scatter.21.cloned.1.call-update) | async-done | bytes 65552 | tf_op jit(solution)/shard_map/reduce_scatter | solution.py:259
  1410.4 37.4 %reduce-scatter.19.cloned.1.call-done = bf16[128,256]{1,0:T(8,128)(2,1)} async-done(((bf16[1024,256]{1,0:T(8,128)(2,1)}), bf16[128,256]{1,0:T(8,128)(2,1)}) %reduce-scatter.19.cloned.1.call-update) | async-done | bytes 65552 | tf_op jit(solution)/shard_map/reduce_scatter | solution.py:259
  1449.4 156.8 %all-reduce.24.cloned.1.call-done = (bf16[1024,1024]{1,0:T(8,128)(2,1)}, bf16[1024,1024]{1,0:T(8,128)(2,1)}) async-done(((bf16[1024,1024]{1,0:T(8,128)(2,1)}, bf16[1024,1024]{1,0:T(8,128)(2,1)}), (bf16[1024,1024]{1,0:T(8,128)(2,1)}, bf16[1024,1024]{1,0:T(8,128)(2,1)})) %all-reduce.24.cloned.1.call-update) | async-done | bytes 4194320 | tf_op jit(solution)/shard_map/psum | solution.py:120
  1609.4 4.1 fusion.42
  1616.0 24.0 %all-reduce.1 = (f32[1,1024]{1,0:T(1,128)S(1)}, f32[1,1024]{1,0:T(1,128)S(1)}, f32[1,128]{1,0:T(1,128)S(1)}, f32[1,128]{1,0:T(1,128)S(1)}, f32[1,128]{1,0:T(1,12...) all-reduce(f32[1,1024]{1,0:T(1,128)S(1)} %bitcast.690, ...), channel_id=1, replica_groups=mesh['dp'=4,'seq'=2,'tensor'=4] {'dp','seq'}, use_global_device_ids=true, to_apply=%region_33.34 | all-reduce | flops 4608 | bytes 36864 | tf_op jit(solution)/shard_map/psum | solution.py:253
  (550 shorter events, 247.1 us)
Async XLA Ops:
  7.2 176.8 %all-reduce.12.cloned.1.call-start = ((), (), s32[]{:S(2)}) async-start(), calls=%async_computation.14 | async-start | bytes 4194304 | tf_op jit(solution)/shard_map/psum | solution.py:113
  8.1 22.9 %copy-start.125 = (f32[1,1024]{1,0:T(1,128)}, f32[1,1024]{1,0:T(1,128)S(1)}, u32[]{:S(2)}) copy-start(f32[1,1024]{1,0:T(1,128)S(1)} %get-tuple-element.131) | copy-start | bytes 12292
  8.1 279.7 %copy-start.119 = (f32[1,1024]{1,0:T(1,128)}, f32[1,1024]{1,0:T(1,128)S(1)}, u32[]{:S(2)}) copy-start(f32[1,1024]{1,0:T(1,128)S(1)} %get-tuple-element.130) | copy-start | bytes 12292
  10.2 20.8 %copy-start.123 = (f32[1024]{0:T(1024)}, f32[1024]{0:T(1024)S(1)}, u32[]{:S(2)}) copy-start(f32[1024]{0:T(1024)S(1)} %add_rsqrt_fusion.7) | copy-start | bytes 12292
  12.2 5.9 copy-start.19
  13.6 11.8 copy-start.107
  14.7 7.0 copy-start.137
  14.7 288.1 %copy-start.139 = (f32[128]{0:T(128)}, f32[128]{0:T(128)S(1)}, u32[]{:S(2)}) copy-start(f32[128]{0:T(128)S(1)} %get-tuple-element.134) | copy-start | bytes 1540
  21.7 290.0 %copy-start.135 = (f32[256]{0:T(256)}, f32[256]{0:T(256)S(1)}, u32[]{:S(2)}) copy-start(f32[256]{0:T(256)S(1)} %get-tuple-element.150) | copy-start | bytes 3076
  27.6 20.0 %collective-permute-start = (bf16[2,1,1024,256]{2,3,1,0:T(8,128)(2,1)}, bf16[2,1,1024,256]{2,3,1,0:T(8,128)(2,1)}, u32[]{:S(2)}, u32[]{:S(2)}) collective-permute-start(bf16[2,1,1024,256]{2,3,1,0:T(8,128)(2,1)} %pad_maximum_fusion.5), channel_id=1, source_target_pairs={{0,4},{1,5},{2,6},{3,7},{8,12},{9,13},{10,14},{11,15},{16,20},{17,... | collective-permute-start | bytes 3145736 | tf_op jit(solution)/shard_map/ppermute | solution.py:19
  35.2 5.5 copy-start.131
  35.3 5.5 copy-start.103
  43.7 6.3 copy-start.49
  50.0 14.3 copy-start.74
  50.1 27.4 %copy-start.68 = (bf16[1,1,2048,256]{2,3,1,0:T(8,128)(2,1)}, bf16[1,1,2048,256]{2,3,1,0:T(8,128)(2,1)S(1)}, u32[]{:S(2)}) copy-start(bf16[1,1,2048,256]{2,3,1,0:T(8,128)(2,1)S(1)} %get-tuple-element.117) | copy-start | bytes 3145732
  64.3 13.1 copy-start.111
  77.4 14.1 copy-start.113
  77.4 15.1 copy-start.154
  95.2 189.4 %all-reduce.14.cloned.1.call-start = ((), (), s32[]{:S(2)}) async-start(), calls=%async_computation.15 | async-start | bytes 4194304 | tf_op jit(solution)/shard_map/psum | solution.py:120
  95.9 90.6 %copy-start.121 = (f32[1,1024]{1,0:T(1,128)}, f32[1,1024]{1,0:T(1,128)S(1)}, u32[]{:S(2)}) copy-start(f32[1,1024]{1,0:T(1,128)S(1)} %get-tuple-element.129) | copy-start | bytes 12292
  198.9 255.4 %all-reduce.16.cloned.1.call-start = ((), (), s32[]{:S(2)}) async-start(), calls=%async_computation.16 | async-start | bytes 4194304 | tf_op jit(solution)/shard_map/psum | solution.py:113
  292.9 26.1 %copy-start.9 = (f32[1024,512]{0,1:T(8,128)}, f32[1024,512]{0,1:T(8,128)S(1)}, u32[]{:S(2)}) copy-start(f32[1024,512]{0,1:T(8,128)S(1)} %fusion.154) | copy-start | bytes 6291460
  301.8 9.9 copy-start.109
  315.4 4.5 collective-permute-start.1
  321.8 15.9 copy-start.75
  350.8 15.0 copy-start.155
  368.5 193.4 %all-reduce.18.cloned.1.call-start = ((), (), s32[]{:S(2)}) async-start(), calls=%async_computation.17 | async-start | bytes 4194304 | tf_op jit(solution)/shard_map/psum | solution.py:169
  476.2 310.0 %all-reduce.20.cloned.1.call-start = ((), (), s32[]{:S(2)}) async-start(), calls=%async_computation.18 | async-start | bytes 4194304 | tf_op jit(solution)/shard_map/psum | solution.py:239
  608.1 54.8 %copy-start.15 = (f32[2,128,2048,1]{2,1,3,0:T(8,128)}, f32[2,128,2048,1]{2,1,3,0:T(8,128)S(1)}, u32[]{:S(2)}) copy-start(f32[2,128,2048,1]{2,1,3,0:T(8,128)S(1)} %fusion.14) | copy-start | bytes 6291460
  664.3 7.3 collective-permute-start.2
  682.8 5.8 copy-start.39
  682.9 5.8 copy-start.41
  699.2 87.0 %copy-start.118 = (f32[1024]{0:T(1024)S(1)}, f32[1024]{0:T(1024)}, u32[]{:S(2)}) copy-start(f32[1024]{0:T(1024)} %copy-done.117) | copy-start | bytes 12292
  699.2 87.0 %copy-start.120 = (f32[1,1024]{1,0:T(1,128)S(1)}, f32[1,1024]{1,0:T(1,128)}, u32[]{:S(2)}) copy-start(f32[1,1024]{1,0:T(1,128)} %copy-done.119) | copy-start | bytes 12292
  699.3 193.8 %all-reduce.22.cloned.1.call-start = ((), (), s32[]{:S(2)}) async-start(), calls=%async_computation.19 | async-start | bytes 4194304 | tf_op jit(solution)/shard_map/psum | solution.py:169
  791.1 6.5 copy-start.167
  794.4 6.7 copy-start.28
  807.4 274.1 %reduce-scatter.41.cloned.1.call-start = ((), (), s32[]{:S(2)}) async-start(), calls=%async_computation.33 | async-start | bytes 1769472 | tf_op jit(solution)/shard_map/reduce_scatter | solution.py:274
  813.4 268.1 %reduce-scatter.39.cloned.1.call-start = ((), (), s32[]{:S(2)}) async-start(), calls=%async_computation.32 | async-start | bytes 1769472 | tf_op jit(solution)/shard_map/reduce_scatter | solution.py:274
  819.2 5.8 copy-start.91
  819.2 266.7 %reduce-scatter.37.cloned.1.call-start = ((), (), s32[]{:S(2)}) async-start(), calls=%async_computation.31 | async-start | bytes 1769472 | tf_op jit(solution)/shard_map/reduce_scatter | solution.py:271
  824.5 261.3 %reduce-scatter.35.cloned.1.call-start = ((), (), s32[]{:S(2)}) async-start(), calls=%async_computation.30 | async-start | bytes 1769472 | tf_op jit(solution)/shard_map/reduce_scatter | solution.py:271
  829.5 271.2 %reduce-scatter.33.cloned.1.call-start = ((), (), s32[]{:S(2)}) async-start(), calls=%async_computation.29 | async-start | bytes 1769472 | tf_op jit(solution)/shard_map/reduce_scatter | solution.py:268
  834.7 307.7 %reduce-scatter.31.cloned.1.call-start = ((), (), s32[]{:S(2)}) async-start(), calls=%async_computation.28 | async-start | bytes 1769472 | tf_op jit(solution)/shard_map/reduce_scatter | solution.py:268
  839.2 53.9 %copy-start.116 = (f32[1024]{0:T(1024)S(1)}, f32[1024]{0:T(1024)}, u32[]{:S(2)}) copy-start(f32[1024]{0:T(1024)} %copy-done.115) | copy-start | bytes 12292
  839.2 53.9 %copy-start.122 = (f32[1,1024]{1,0:T(1,128)S(1)}, f32[1,1024]{1,0:T(1,128)}, u32[]{:S(2)}) copy-start(f32[1,1024]{1,0:T(1,128)} %copy-done.121) | copy-start | bytes 12292
  839.2 342.4 %reduce-scatter.29.cloned.1.call-start = ((), (), s32[]{:S(2)}) async-start(), calls=%async_computation.27 | async-start | bytes 1179648 | tf_op jit(solution)/shard_map/reduce_scatter | solution.py:265
  839.2 53.8 %copy-start.1 = (bf16[1,1024,1024]{2,1,0:T(8,128)(2,1)S(1)}, bf16[1,1024,1024]{2,1,0:T(8,128)(2,1)}, u32[]{:S(2)}) copy-start(bf16[1,1024,1024]{2,1,0:T(8,128)(2,1)} %param.15) | copy-start | bytes 6291460
  844.2 376.4 %reduce-scatter.27.cloned.1.call-start = ((), (), s32[]{:S(2)}) async-start(), calls=%async_computation.26 | async-start | bytes 1179648 | tf_op jit(solution)/shard_map/reduce_scatter | solution.py:265
  897.2 5.0 copy-start.158
  904.5 355.1 %reduce-scatter.17.cloned.1.call-start = ((), (), s32[]{:S(2)}) async-start(), calls=%async_computation.21 | async-start | bytes 1179648 | tf_op jit(solution)/shard_map/reduce_scatter | solution.py:256
  908.9 389.8 %reduce-scatter.15.cloned.1.call-start = ((), (), s32[]{:S(2)}) async-start(), calls=%async_computation.20 | async-start | bytes 1179648 | tf_op jit(solution)/shard_map/reduce_scatter | solution.py:256
  913.0 22.4 %copy-start.33 = (bf16[1024,512]{0,1:T(8,128)(2,1)}, bf16[1024,512]{0,1:T(8,128)(2,1)S(1)}, u32[]{:S(2)}) copy-start(bf16[1024,512]{0,1:T(8,128)(2,1)S(1)} %convolution_convert_fusion.13) | copy-start | bytes 3145732
  1000.6 335.2 %reduce-scatter.25.cloned.1.call-start = ((), (), s32[]{:S(2)}) async-start(), calls=%async_computation.25 | async-start | bytes 589824 | tf_op jit(solution)/shard_map/reduce_scatter | solution.py:262
  1016.9 4.9 collective-permute-start.3
  1019.8 353.3 %reduce-scatter.23.cloned.1.call-start = ((), (), s32[]{:S(2)}) async-start(), calls=%async_computation.24 | async-start | bytes 589824 | tf_op jit(solution)/shard_map/reduce_scatter | solution.py:262
  1027.2 5.4 copy-start.85
  1027.2 383.2 %reduce-scatter.21.cloned.1.call-start = ((), (), s32[]{:S(2)}) async-start(), calls=%async_computation.23 | async-start | bytes 589824 | tf_op jit(solution)/shard_map/reduce_scatter | solution.py:259
  1027.3 5.3 copy-start.54
  1034.2 413.6 %reduce-scatter.19.cloned.1.call-start = ((), (), s32[]{:S(2)}) async-start(), calls=%async_computation.22 | async-start | bytes 589824 | tf_op jit(solution)/shard_map/reduce_scatter | solution.py:259
  1042.4 6.0 copy-start.44
  1042.4 6.0 copy-start.45
  1061.0 545.1 %all-reduce.24.cloned.1.call-start = ((), (), s32[]{:S(2)}) async-start(), calls=%async_computation.34 | async-start | bytes 8388608 | tf_op jit(solution)/shard_map/psum | solution.py:120
  1083.5 60.8 %copy-start.37 = (f32[1,1,1024,256]{2,3,1,0:T(8,128)S(1)}, f32[1,1,1024,256]{2,3,1,0:T(8,128)}, u32[]{:S(2)}) copy-start(f32[1,1,1024,256]{2,3,1,0:T(8,128)} %slice.249) | copy-start | bytes 3145732
  (129 other events, 318.6 us)
Sparse Core Ops, SparseCore 0:
  95.3 88.5 all-reduce.11
  199.1 85.4 all-reduce.13
  368.6 85.6 all-reduce.15
  476.4 85.4 all-reduce.17
  699.4 86.7 all-reduce.19
  807.5 85.4 all-reduce.21
  896.3 37.4 reduce-scatter.40
  937.1 38.4 reduce-scatter.38
  978.8 38.4 reduce-scatter.36
  1020.4 38.4 reduce-scatter.34
  1062.2 38.4 reduce-scatter.32
  1103.9 38.4 reduce-scatter.30
  1145.5 35.9 reduce-scatter.28
  1184.6 35.9 reduce-scatter.26
  1223.6 35.9 reduce-scatter.16
  1262.7 35.9 reduce-scatter.14
  1301.6 34.1 reduce-scatter.24
  1339.0 34.1 reduce-scatter.22
  1376.3 34.1 reduce-scatter.20
  1413.6 34.1 reduce-scatter.18
  1450.8 155.3 all-reduce.23
where the time goes:
time: 1660 us; the launch traced here: 1650 us
  waiting for transfers between devices  968 us (58%)
  matrix products  301 us (18%)
  other arithmetic  226 us (14%)
  local copies, waits for them, and re-layouts  87.6 us (5%)
  blocking collectives  38 us (2%)
  between operations  17 us (1%)
    psum x2, waiting for transfers between devices, forward_layer(): lax.psum(mlp_part.astype(jnp.bfloat16), 'tensor').astype(jnp.float32)  242 us
    psum x2, waiting for transfers between devices, forward_layer(): lax.psum(attn_part.astype(jnp.bfloat16), 'tensor').astype(jnp.float32)  174 us
    psum x2, waiting for transfers between devices, backward_layer(): lax.psum(d_mlp_part.astype(jnp.bfloat16), 'tensor').astype(jnp.float32)  131 us
    psum x1, waiting for transfers between devices, backward_layer(): lax.psum(d_attn_part.astype(jnp.bfloat16), 'tensor').astype(jnp.float32)  86.9 us
    reduce_scatter x2, waiting for transfers between devices, reduce_grads(): lax.psum_scatter(grad_q.astype(jnp.bfloat16), ('dp', 'seq'), scatter_dime...  76.1 us
    reduce_scatter x2, waiting for transfers between devices, reduce_grads(): lax.psum_scatter(grad_k.astype(jnp.bfloat16), ('dp', 'seq'), scatter_dime...  73 us
    reduce_scatter x2, waiting for transfers between devices, reduce_grads(): lax.psum_scatter(grad_v.astype(jnp.bfloat16), ('dp', 'seq'), scatter_dime...  72.7 us
    another operation x4, other arithmetic  61.9 us
  transfers between devices with their start and end apart: 25, of which 18 were waited for; matrix products, arithmetic and copies ran while one was open for 16% of the time, Pallas kernels for 0%

commit v1 on v0

--- a/solution.py
+++ b/solution.py
@@ -1,11 +1,431 @@
+import functools
+
 import jax
 import jax.numpy as jnp
 from jax import lax
+from jax.experimental import pallas as pl
+from jax.experimental.pallas import tpu as pltpu
 from jax.sharding import PartitionSpec as P
 
 HEAD_SIZE = 128
 LAYER_COUNT = 2
 WINDOW = 1024
+LOG2E = 1.4426950408889634
+SCALE = HEAD_SIZE ** (-0.5)
+MESH = pl.DeviceIdType.MESH
+
+NT = (((1,), (1,)), ((), ()))
+NN = (((1,), (0,)), ((), ()))
+TN = (((0,), (0,)), ((), ()))
+
+
+def dot(a, b, dims=NN):
+    return lax.dot_general(a, b, dims, preferred_element_type=jnp.float32)
+
+
+def attn_fwd_kernel(qb, kb, offset, first_ref, low_ref, q_ref, k_ref, v_ref, o_ref, of_ref, lse_ref):
+    step = pl.program_id(1)
+    heads = q_ref.shape[1] // HEAD_SIZE
+    q_start = step * qb + offset
+    queries = [q_ref[:, h * HEAD_SIZE:(h + 1) * HEAD_SIZE] for h in range(heads)]
+    q_index = q_start + lax.broadcasted_iota(jnp.int32, (qb, 1), 0)
+    low = low_ref[...]
+
+    def block(kk, carry):
+        start = pl.multiple_of(kk * kb, kb)
+        keys = k_ref[pl.ds(start, kb), :]
+        values = v_ref[pl.ds(start, kb), :]
+        key_index = start + lax.broadcasted_iota(jnp.int32, (qb, kb), 1)
+        mask = (key_index >= low) & (key_index <= q_index)
+        out = []
+        for h in range(heads):
+            acc, total = carry[h]
+            s = dot(queries[h], keys, NT) * (SCALE * LOG2E)
+            p = jnp.where(mask, jnp.exp2(s), 0.0)
+            part = p[:, :128]
+            for c in range(1, kb // 128):
+                part = part + p[:, c * 128:(c + 1) * 128]
+            out.append((acc + dot(p.astype(jnp.bfloat16), values), total + part))
+        return tuple(out)
+
+    zero = jnp.zeros((qb, HEAD_SIZE), jnp.float32)
+    first = first_ref[step] // kb
+    last = (q_start + qb - 1) // kb + 1
+    result = lax.fori_loop(first, last, block, tuple((zero, zero) for _ in range(heads)))
+    for h in range(heads):
+        acc, total = result[h]
+        total = jnp.sum(total, 1, keepdims=True)
+        o = acc / total
+        of_ref[:, h * HEAD_SIZE:(h + 1) * HEAD_SIZE] = o
+        o_ref[:, h * HEAD_SIZE:(h + 1) * HEAD_SIZE] = o.astype(jnp.bfloat16)
+        lse_ref[:, h:h + 1] = jnp.log2(total)
+
+
+def attn_fwd(q, k, v, first, low, offset, qb=256, kb=256):
+    rows, span = q.shape[0], k.shape[0]
+    kv_heads = k.shape[1] // HEAD_SIZE
+    group = q.shape[1] // k.shape[1]
+    qb = min(qb, rows)
+    width = group * HEAD_SIZE
+    return pl.pallas_call(
+        functools.partial(attn_fwd_kernel, qb, kb, offset),
+        grid_spec=pltpu.PrefetchScalarGridSpec(
+            num_scalar_prefetch=1,
+            grid=(kv_heads, rows // qb),
+            in_specs=[
+                pl.BlockSpec((qb, 1), lambda g, i, f: (i, 0)),
+                pl.BlockSpec((qb, width), lambda g, i, f: (i, g)),
+                pl.BlockSpec((span, HEAD_SIZE), lambda g, i, f: (0, g)),
+                pl.BlockSpec((span, HEAD_SIZE), lambda g, i, f: (0, g)),
+            ],
+            out_specs=[
+                pl.BlockSpec((qb, width), lambda g, i, f: (i, g)),
+                pl.BlockSpec((qb, width), lambda g, i, f: (i, g)),
+                pl.BlockSpec((None, qb, group), lambda g, i, f: (g, i, 0)),
+            ],
+        ),
+        out_shape=[
+            jax.ShapeDtypeStruct(q.shape, jnp.bfloat16),
+            jax.ShapeDtypeStruct(q.shape, jnp.float32),
+            jax.ShapeDtypeStruct((kv_heads, rows, group), jnp.float32),
+        ],
+        name="attn_fwd",
+        compiler_params=pltpu.CompilerParams(vmem_limit_bytes=32 << 20),
+    )(first, low, q, k, v)
+
+
+def attn_bwd_kernel(qb, kb, offset, first_ref, low_ref, lse_ref, delta_ref, q_ref, do_ref, k_ref, v_ref,
+                    dq_ref, dk_ref, dv_ref):
+    step = pl.program_id(1)
+    heads = q_ref.shape[1] // HEAD_SIZE
+    q_start = step * qb + offset
+
+    @pl.when(step == 0)
+    def _():
+        dk_ref[...] = jnp.zeros_like(dk_ref)
+        dv_ref[...] = jnp.zeros_like(dv_ref)
+
+    def stack(ref):
+        return jnp.concatenate([ref[:, h * HEAD_SIZE:(h + 1) * HEAD_SIZE] for h in range(heads)], 0)
+
+    queries = stack(q_ref)
+    d_out = stack(do_ref)
+    q_index = q_start + lax.broadcasted_iota(jnp.int32, (1, qb), 1)
+    low = low_ref[...]
+    lse = jnp.concatenate([lse_ref[h:h + 1, :] for h in range(heads)], 1)
+    delta = jnp.concatenate([delta_ref[h:h + 1, :] for h in range(heads)], 1)
+
+    def block(kk, dq):
+        start = pl.multiple_of(kk * kb, kb)
+        keys = k_ref[pl.ds(start, kb), :]
+        values = v_ref[pl.ds(start, kb), :]
+        key_index = start + lax.broadcasted_iota(jnp.int32, (kb, qb), 0)
+        mask = (key_index >= low) & (key_index <= q_index)
+        mask = jnp.concatenate([mask] * heads, 1)
+        s = dot(keys, queries, NT) * (SCALE * LOG2E) - lse
+        p = jnp.where(mask, jnp.exp2(s), 0.0)
+        dp = dot(values, d_out, NT)
+        ds = (p * (dp - delta)).astype(jnp.bfloat16)
+        dv_ref[pl.ds(start, kb), :] += dot(p.astype(jnp.bfloat16), d_out)
+        dk_ref[pl.ds(start, kb), :] += dot(ds, queries)
+        return dq + dot(ds, keys, TN)
+
+    first = first_ref[step] // kb
+    last = (q_start + qb - 1) // kb + 1
+    dq = lax.fori_loop(first, last, block, jnp.zeros((heads * qb, HEAD_SIZE), jnp.float32))
+    for h in range(heads):
+        dq_ref[:, h * HEAD_SIZE:(h + 1) * HEAD_SIZE] = dq[h * qb:(h + 1) * qb] * SCALE
+
+    @pl.when(step == pl.num_programs(1) - 1)
+    def _():
+        dk_ref[...] = dk_ref[...] * SCALE
+
+
+def attn_bwd(q, d_out, k, v, first, low_row, lse, delta, offset, qb=256, kb=256):
+    rows, span = q.shape[0], k.shape[0]
+    kv_heads = k.shape[1] // HEAD_SIZE
+    group = q.shape[1] // k.shape[1]
+    qb = min(qb, rows)
+    width = group * HEAD_SIZE
+    return pl.pallas_call(
+        functools.partial(attn_bwd_kernel, qb, kb, offset),
+        grid_spec=pltpu.PrefetchScalarGridSpec(
+            num_scalar_prefetch=1,
+            grid=(kv_heads, rows // qb),
+            in_specs=[
+                pl.BlockSpec((1, qb), lambda g, i, f: (0, i)),
+                pl.BlockSpec((None, group, qb), lambda g, i, f: (g, 0, i)),
+                pl.BlockSpec((None, group, qb), lambda g, i, f: (g, 0, i)),
+                pl.BlockSpec((qb, width), lambda g, i, f: (i, g)),
+                pl.BlockSpec((qb, width), lambda g, i, f: (i, g)),
+                pl.BlockSpec((span, HEAD_SIZE), lambda g, i, f: (0, g)),
+                pl.BlockSpec((span, HEAD_SIZE), lambda g, i, f: (0, g)),
+            ],
+            out_specs=[
+                pl.BlockSpec((qb, width), lambda g, i, f: (i, g)),
+                pl.BlockSpec((span, HEAD_SIZE), lambda g, i, f: (0, g)),
+                pl.BlockSpec((span, HEAD_SIZE), lambda g, i, f: (0, g)),
+            ],
+        ),
+        out_shape=[
+            jax.ShapeDtypeStruct(q.shape, jnp.float32),
+            jax.ShapeDtypeStruct(k.shape, jnp.float32),
+            jax.ShapeDtypeStruct(k.shape, jnp.float32),
+        ],
+        name="attn_bwd",
+        compiler_params=pltpu.CompilerParams(vmem_limit_bytes=32 << 20),
+    )(first, low_row, lse, delta, q, d_out, k, v)
+
+
+def attention_forward(queries, keys, values, low, offset):
+    seqs_here, stretch = low.shape
+    outs = []
+    for s in range(seqs_here):
+        here = queries[s * stretch : (s + 1) * stretch]
+        block = min(512, stretch)
+        outs.append(
+            attn_fwd(here, keys[s], values[s], low[s, ::block], low[s][:, None], offset, block, min(512, stretch))
+        )
+    low_out, full, lse = (jnp.concatenate(parts, 0) for parts in zip(*outs))
+    return low_out, full, lse.reshape((seqs_here,) + outs[0][2].shape)
+
+
+def attention_backward(queries, d_context, context, lse, keys, values, low, offset):
+    seqs_here, stretch = low.shape
+    product = d_context.astype(jnp.float32) * context
+    kv_heads, group = lse.shape[1], lse.shape[3]
+    delta = jnp.sum(product.reshape(seqs_here, stretch, kv_heads, group, HEAD_SIZE), -1)
+    outs = []
+    for s in range(seqs_here):
+        here = slice(s * stretch, (s + 1) * stretch)
+        block = min(512, stretch)
+        outs.append(
+            attn_bwd(
+                queries[here], d_context[here], keys[s], values[s], low[s, ::block], low[s][None],
+                lse[s].transpose(0, 2, 1), delta[s].transpose(1, 2, 0), offset, block, min(512, stretch),
+            )
+        )
+    d_queries, d_keys, d_values = zip(*outs)
+    return jnp.concatenate(d_queries, 0), jnp.stack(d_keys), jnp.stack(d_values)
+
+
+def line_sum_kernel(chunks, x_ref, o_ref, p_ref, land_ref, send_sem, land_sem, out_sem, total_sem):
+    n = lax.axis_size("tensor")
+    half = n // 2
+    z = lax.axis_index("tensor")
+    left = z < half
+    middle = (z == half - 1) | (z == half)
+    has_outer = (z > 0) & (z < n - 1)
+    inner = jnp.where(left, z + 1, z - 1)
+    outer = jnp.clip(jnp.where(left, z - 1, z + 1), 0, n - 1)
+    rows = x_ref.shape[0] // chunks
+    barrier = pltpu.get_barrier_semaphore()
+    pl.semaphore_signal(barrier, inc=1, device_id={"tensor": inner}, device_id_type=MESH)
+
+    @pl.when(has_outer)
+    def _():
+        pl.semaphore_signal(barrier, inc=1, device_id={"tensor": outer}, device_id_type=MESH)
+
+    pl.semaphore_wait(barrier, jnp.where(has_outer, 2, 1))
+    slot = jnp.where(middle, 1, 0)
+
+    def part(ref, c):
+        return ref.at[pl.ds(pl.multiple_of(c * rows, rows), rows)]
+
+    def inward(source, c):
+        return pltpu.make_async_remote_copy(
+            part(source, c), part(land_ref.at[slot], c), send_sem.at[c], land_sem.at[slot, c],
+            device_id={"tensor": inner}, device_id_type=MESH)
+
+    def landed(which, c):
+        return pltpu.make_async_remote_copy(
+            part(x_ref, c), part(land_ref.at[which], c), send_sem.at[c], land_sem.at[which, c],
+            device_id={"tensor": inner}, device_id_type=MESH)
+
+    def outward(c):
+        return pltpu.make_async_remote_copy(
+            part(o_ref, c), part(o_ref, c), out_sem.at[c], total_sem.at[c],
+            device_id={"tensor": outer}, device_id_type=MESH)
+
+    @pl.when(jnp.logical_not(has_outer))
+    def _():
+        @pl.loop(0, chunks)
+        def _(c):
+            inward(x_ref, c).start()
+
+    @pl.loop(0, chunks + 1)
+    def _(step):
+        @pl.when((step < chunks) & has_outer)
+        def _():
+            c = step
+            landed(0, c).wait_recv()
+            p_ref[pl.ds(pl.multiple_of(c * rows, rows), rows), :] = (
+                part(x_ref, c)[...].astype(jnp.float32) + part(land_ref.at[0], c)[...].astype(jnp.float32)
+            ).astype(jnp.bfloat16)
+            inward(p_ref, c).start()
+
+        @pl.when((step > 0) & middle)
+        def _():
+            c = step - 1
+            landed(1, c).wait_recv()
+
+            def finish(own):
+                o_ref[pl.ds(pl.multiple_of(c * rows, rows), rows), :] = (
+                    part(own, c)[...].astype(jnp.float32) + part(land_ref.at[1], c)[...].astype(jnp.float32)
+                ).astype(jnp.bfloat16)
+
+            @pl.when(has_outer)
+            def _():
+                finish(p_ref)
+                outward(c).start()
+
+            @pl.when(jnp.logical_not(has_outer))
+            def _():
+                finish(x_ref)
+
+    @pl.loop(0, chunks)
+    def _(c):
+        @pl.when(jnp.logical_not(middle))
+        def _():
+            outward(c).wait_recv()
+
+            @pl.when(has_outer)
+            def _():
+                outward(c).start()
+
+        inward(x_ref, c).wait_send()
+
+        @pl.when(has_outer)
+        def _():
+            outward(c).wait_send()
+
+
+def line_sum(x, collective_id, chunks=8):
+    n = lax.axis_size("tensor")
+    if n == 1:
+        return x
+    if n % 2:
+        return lax.psum(x, "tensor")
+    while x.shape[0] % (16 * chunks):
+        chunks //= 2
+    return pl.pallas_call(
+        functools.partial(line_sum_kernel, chunks),
+        out_shape=jax.ShapeDtypeStruct(x.shape, x.dtype),
+        in_specs=[pl.BlockSpec(memory_space=pltpu.VMEM)],
+        out_specs=pl.BlockSpec(memory_space=pltpu.VMEM),
+        scratch_shapes=[
+            pltpu.VMEM(x.shape, x.dtype),
+            pltpu.VMEM((2,) + x.shape, x.dtype),
+            pltpu.SemaphoreType.DMA((chunks,)),
+            pltpu.SemaphoreType.DMA((2, chunks)),
+            pltpu.SemaphoreType.DMA((chunks,)),
+            pltpu.SemaphoreType.DMA((chunks,)),
+        ],
+        name="line_sum",
+        compiler_params=pltpu.CompilerParams(
+            collective_id=collective_id, has_side_effects=True, vmem_limit_bytes=40 << 20),
+    )(x)
+
+
+def exchange_axes():
+    dp_bits = lax.axis_size("dp").bit_length() - 1
+    seq_bits = lax.axis_size("seq").bit_length() - 1
+    return [("dp", b) for b in reversed(range(dp_bits))] + [("seq", b) for b in reversed(range(seq_bits))]
+
+
+def scatter_kernel(orders, axes, *refs):
+    count = len(orders)
+    phases = len(axes)
+    in_refs = refs[:count]
+    out_refs = refs[count : 2 * count]
+    scratch = refs[2 * count :]
+    lands = [scratch[k * count : (k + 1) * count] for k in range(phases)]
+    sums = [scratch[(phases + k) * count : (phases + k + 1) * count] for k in range(phases - 1)]
+    send_sem, land_sem = scratch[-2:]
+    here = {"dp": lax.axis_index("dp"), "seq": lax.axis_index("seq")}
+
+    def bit(axis):
+        name, b = axis
+        return lax.rem(here[name] // (1 << b), 2)
+
+    def partner(axis):
+        name, b = axis
+        return {name: here[name] + (1 - 2 * bit(axis)) * (1 << b)}
+
+    barrier = pltpu.get_barrier_semaphore()
+    for axis in axes:
+        pl.semaphore_signal(barrier, inc=1, device_id=partner(axis), device_id_type=MESH)
+    pl.semaphore_wait(barrier, phases)
+
+    def view(ref, place, index):
+        return ref.at[(slice(None),) * place + (index,)]
+
+    def place_of(i, k):
+        left = [a for a in range(phases) if a not in orders[i][:k]]
+        return left.index(orders[i][k])
+
+    def source(i, k):
+        return in_refs[i] if k == 0 else sums[k - 1][i]
+
+    def copy(i, k):
+        axis = axes[orders[i][k]]
+        return pltpu.make_async_remote_copy(
+            view(source(i, k), place_of(i, k), 1 - bit(axis)), lands[k][i], send_sem.at[k, i],
+            land_sem.at[k, i], device_id=partner(axis), device_id_type=MESH)
+
+    for i in range(count):
+        copy(i, 0).start()
+    for k in range(phases):
+        for i in range(count):
+            copy(i, k).wait_recv()
+            axis = axes[orders[i][k]]
+            kept = view(source(i, k), place_of(i, k), bit(axis))
+            total = kept[...].astype(jnp.float32) + lands[k][i][...].astype(jnp.float32)
+            if k == phases - 1:
+                out_refs[i][...] = total
+            else:
+                sums[k][i][...] = total.astype(jnp.bfloat16)
+                copy(i, k + 1).start()
+    for k in range(phases):
+        for i in range(count):
+            copy(i, k).wait_send()
+
+
+def scatter_sums(arrays, collective_id):
+    dp, seq = lax.axis_size("dp"), lax.axis_size("seq")
+    if dp & (dp - 1) or seq & (seq - 1) or dp * seq == 1:
+        return [
+            lax.psum_scatter(a, ("dp", "seq"), scatter_dimension=0, tiled=True).astype(jnp.float32)
+            for a in arrays
+        ]
+    axes = exchange_axes()
+    phases = len(axes)
+    near = [k for k in range(phases) if axes[k][0] == "seq"][::-1]
+    far = [k for k in range(phases) if axes[k][0] == "dp"]
+    loads = [0, 0]
+    orders = []
+    for a in arrays:
+        side = 0 if loads[0] <= loads[1] else 1
+        loads[side] += a.shape[1]
+        orders.append(tuple(near + (far if side else far[::-1])))
+    blocks = [a.reshape((2,) * phases + (a.shape[0] // (dp * seq), a.shape[1])) for a in arrays]
+    tails = [b.shape[phases:] for b in blocks]
+    scratch = []
+    for k in range(phases):
+        scratch += [pltpu.VMEM((2,) * (phases - k - 1) + t, jnp.bfloat16) for t in tails]
+    for k in range(phases - 1):
+        scratch += [pltpu.VMEM((2,) * (phases - k - 1) + t, jnp.bfloat16) for t in tails]
+    scratch += [pltpu.SemaphoreType.DMA((phases, len(arrays)))] * 2
+    return pl.pallas_call(
+        functools.partial(scatter_kernel, orders, axes),
+        out_shape=[jax.ShapeDtypeStruct(t, jnp.float32) for t in tails],
+        in_specs=[pl.BlockSpec(memory_space=pltpu.VMEM)] * len(arrays),
+        out_specs=[pl.BlockSpec(memory_space=pltpu.VMEM)] * len(arrays),
+        scratch_shapes=scratch,
+        name="scatter_sums",
+        compiler_params=pltpu.CompilerParams(
+            collective_id=collective_id, has_side_effects=True, vmem_limit_bytes=50 << 20),
+    )(*blocks)
 
 
 EPS = 1e-06
@@ -58,7 +478,7 @@
     return (inverse * (scaled - normed * inner), gain_grad)
 
 
-def forward_layer(hidden, weights, rotary_tables, visible, reach, stretch):
+def forward_layer(hidden, weights, rotary_tables, visible, reach, stretch, ids):
     gain_a, w_q, key_weight, value_weight, query_norm_scale, gain_k, w_o, gain_m, w_g, w_u, w_d = (
         weights
     )
@@ -90,34 +510,19 @@
     )
     earlier = [shifted(local_pair, "seq", back) for back in range(reach, 0, -1)]
     window_pair = jnp.concatenate(earlier + [local_pair], 2)
-    span = window_pair.shape[2]
-    key_window = window_pair[0].reshape(seqs_here, span, key_heads, HEAD_SIZE)
-    value_window = window_pair[1].reshape(seqs_here, span, key_heads, HEAD_SIZE)
-    grouped = queries_low.reshape(seqs_here, stretch, key_heads, -1, HEAD_SIZE)
-    scores = (
-        jnp.einsum("sqhgd,skhd->shgqk", grouped, key_window, preferred_element_type=jnp.float32)
-        * scale
-    )
-    scores = jnp.where(visible[:, None, None], scores, NEG_FILL)
-    peak = jnp.max(scores, -1, keepdims=True)
-    expo = jnp.exp(scores - peak)
-    totals = jnp.sum(expo, -1, keepdims=True)
-    probs_low = (expo / totals).astype(jnp.bfloat16)
-    log_total = peak + jnp.log(totals)
-    context_low = (
-        jnp.einsum("shgqk,skhd->sqhgd", probs_low, value_window, preferred_element_type=jnp.float32)
-        .astype(jnp.bfloat16)
-        .reshape(rows, -1)
+    queries_flat = queries_low.reshape(rows, -1)
+    context_low, context, lse = attention_forward(
+        queries_flat, window_pair[0], window_pair[1], visible, reach * stretch
     )
     attn_part = jnp.dot(context_low, w_o, preferred_element_type=jnp.float32)
-    hidden_mid = hidden + lax.psum(attn_part.astype(jnp.bfloat16), "tensor").astype(jnp.float32)
+    hidden_mid = hidden + line_sum(attn_part.astype(jnp.bfloat16), ids + 0).astype(jnp.float32)
     mlp_in, mlp_hat, mlp_inverse = norm_forward(hidden_mid, gain_m.astype(jnp.float32))
     mlp_low = mlp_in.astype(jnp.bfloat16)
     gate = jnp.dot(mlp_low, w_g, preferred_element_type=jnp.float32)
     up_branch = jnp.dot(mlp_low, w_u, preferred_element_type=jnp.float32)
     act_low = (jax.nn.silu(gate) * up_branch).astype(jnp.bfloat16)
     mlp_part = jnp.dot(act_low, w_d, preferred_element_type=jnp.float32)
-    hidden_next = hidden_mid + lax.psum(mlp_part.astype(jnp.bfloat16), "tensor").astype(jnp.float32)
+    hidden_next = hidden_mid + line_sum(mlp_part.astype(jnp.bfloat16), ids + 1).astype(jnp.float32)
     saved = dict(
         attn_hat=attn_hat,
         attn_inverse=attn_inverse,
@@ -126,10 +531,10 @@
         q_inverse=q_inverse,
         k_hat=k_hat,
         k_inverse=k_inverse,
-        grouped=grouped,
-        key_window=key_window,
-        value_window=value_window,
-        log_total=log_total,
+        queries=queries_flat,
+        window_pair=window_pair,
+        lse=lse,
+        context=context,
         context_low=context_low,
         mlp_hat=mlp_hat,
         mlp_inverse=mlp_inverse,
@@ -141,7 +546,7 @@
     return (hidden_next, saved)
 
 
-def backward_layer(grad, weights, saved, rotary_tables, visible, reach, stretch):
+def backward_layer(grad, weights, saved, rotary_tables, visible, reach, stretch, ids):
     gain_a, w_q, key_weight, value_weight, query_norm_scale, gain_k, w_o, gain_m, w_g, w_u, w_d = (
         weights
     )
@@ -166,7 +571,7 @@
     d_mlp_part = jnp.einsum(
         "rf,df->rd", d_gate, w_g, preferred_element_type=jnp.float32
     ) + jnp.einsum("rf,df->rd", d_up, w_u, preferred_element_type=jnp.float32)
-    d_mlp_in = lax.psum(d_mlp_part.astype(jnp.bfloat16), "tensor").astype(jnp.float32)
+    d_mlp_in = line_sum(d_mlp_part.astype(jnp.bfloat16), ids + 2).astype(jnp.float32)
     d_mid, grad_gain_m = norm_backward(
         d_mlp_in, gain_m.astype(jnp.float32), saved["mlp_hat"], saved["mlp_inverse"]
     )
@@ -175,41 +580,15 @@
     grad_o_turned = jnp.einsum(
         "rc,rd->dc", saved["context_low"], mid_low, preferred_element_type=jnp.float32
     )
-    grouped = saved["grouped"]
-    key_window = saved["key_window"]
-    value_window = saved["value_window"]
-    key_heads = key_window.shape[2]
     d_context = jnp.einsum("rd,cd->rc", mid_low, w_o, preferred_element_type=jnp.float32)
-    d_context = d_context.astype(jnp.bfloat16).reshape(grouped.shape)
-    scores = (
-        jnp.einsum("sqhgd,skhd->shgqk", grouped, key_window, preferred_element_type=jnp.float32)
-        * scale
-    )
-    scores = jnp.where(visible[:, None, None], scores, NEG_FILL)
-    probs = jnp.exp(scores - saved["log_total"])
-    d_probs = jnp.einsum(
-        "sqhgd,skhd->shgqk", d_context, value_window, preferred_element_type=jnp.float32
-    )
-    inner = jnp.sum(probs * d_probs, -1, keepdims=True)
-    d_scores = (probs * (d_probs - inner)).astype(jnp.bfloat16)
-    d_queries = (
-        jnp.einsum("shgqk,skhd->sqhgd", d_scores, key_window, preferred_element_type=jnp.float32)
-        * scale
-    )
-    d_key_window = (
-        jnp.einsum("shgqk,sqhgd->skhd", d_scores, grouped, preferred_element_type=jnp.float32)
-        * scale
-    )
-    d_value_window = jnp.einsum(
-        "shgqk,sqhgd->skhd",
-        probs.astype(jnp.bfloat16),
-        d_context,
-        preferred_element_type=jnp.float32,
-    )
-    span = key_window.shape[1]
-    d_pair = jnp.stack([d_key_window, d_value_window]).reshape(
-        2, seqs_here, span, key_heads * HEAD_SIZE
-    )
+    d_context = d_context.astype(jnp.bfloat16)
+    key_window, value_window = saved["window_pair"]
+    key_heads = key_window.shape[2] // HEAD_SIZE
+    d_queries, d_key_window, d_value_window = attention_backward(
+        saved["queries"], d_context, saved["context"], saved["lse"], key_window, value_window,
+        visible, reach * stretch,
+    )
+    d_pair = jnp.stack([d_key_window, d_value_window])
     own_pair = d_pair[:, :, reach * stretch :]
     for back in range(1, reach + 1):
         piece = d_pair[:, :, (reach - back) * stretch : (reach - back + 1) * stretch]
@@ -236,7 +615,7 @@
         + jnp.einsum("rc,dc->rd", d_values_low, value_weight, preferred_element_type=jnp.float32)
     )
     d_attn_in, grad_gain_q, grad_gain_k = (
-        lax.psum(d_attn_part.astype(jnp.bfloat16), "tensor").astype(jnp.float32),
+        line_sum(d_attn_part.astype(jnp.bfloat16), ids + 3).astype(jnp.float32),
         lax.psum(grad_gain_q.astype(jnp.bfloat16), "tensor").astype(jnp.float32),
         lax.psum(grad_gain_k.astype(jnp.bfloat16), "tensor").astype(jnp.float32),
     )
@@ -248,32 +627,12 @@
     return (grad_mid + d_hidden, gain_grads, matrix_grads)
 
 
-def reduce_grads(gain_grads, matrix_grads):
+def reduce_grads(gain_grads, matrix_grads, ids):
     gain_a, gain_q, gain_k, gain_m = gain_grads
     gain_a, gain_q, gain_k, gain_m = lax.psum((gain_a, gain_q, gain_k, gain_m), ("dp", "seq"))
     grad_q, grad_k, grad_v, grad_o_turned, grad_gate, grad_up, grad_down_turned = matrix_grads
-    grad_q, grad_k, grad_v, grad_o_turned, grad_gate, grad_up, grad_down_turned = (
-        lax.psum_scatter(
-            grad_q.astype(jnp.bfloat16), ("dp", "seq"), scatter_dimension=0, tiled=True
-        ).astype(jnp.float32),
-        lax.psum_scatter(
-            grad_k.astype(jnp.bfloat16), ("dp", "seq"), scatter_dimension=0, tiled=True
-        ).astype(jnp.float32),
-        lax.psum_scatter(
-            grad_v.astype(jnp.bfloat16), ("dp", "seq"), scatter_dimension=0, tiled=True
-        ).astype(jnp.float32),
-        lax.psum_scatter(
-            grad_o_turned.astype(jnp.bfloat16), ("dp", "seq"), scatter_dimension=0, tiled=True
-        ).astype(jnp.float32),
-        lax.psum_scatter(
-            grad_gate.astype(jnp.bfloat16), ("dp", "seq"), scatter_dimension=0, tiled=True
-        ).astype(jnp.float32),
-        lax.psum_scatter(
-            grad_up.astype(jnp.bfloat16), ("dp", "seq"), scatter_dimension=0, tiled=True
-        ).astype(jnp.float32),
-        lax.psum_scatter(
-            grad_down_turned.astype(jnp.bfloat16), ("dp", "seq"), scatter_dimension=0, tiled=True
-        ).astype(jnp.float32),
+    grad_q, grad_k, grad_v, grad_o_turned, grad_gate, grad_up, grad_down_turned = scatter_sums(
+        [g.astype(jnp.bfloat16) for g in matrix_grads], ids
     )
     return [
         gain_a,
@@ -318,11 +677,10 @@
         [jnp.full((seqs_here, reach * stretch), -1, jnp.int32), every_doc], 1
     )
     key_docs = lax.dynamic_slice_in_dim(padded_docs, place * stretch, span, 1)
-    query_index = place * stretch + jnp.arange(stretch, dtype=jnp.int32)
-    key_index = (place - reach) * stretch + jnp.arange(span, dtype=jnp.int32)
-    distance = query_index[:, None] - key_index[None, :]
-    in_window = (distance >= 0) & (distance < WINDOW) & (key_index[None, :] >= 0)
-    visible = in_window[None] & (segments[:, :, None] == key_docs[:, None, :])
+    index = jnp.arange(stretch, dtype=jnp.int32)
+    doc_start = jnp.sum((key_docs[:, None, :] < segments[:, :, None]).astype(jnp.int32), 2)
+    low = jnp.maximum(doc_start, reach * stretch + index - (WINDOW - 1))
+    visible = low
     rotary_tables = rope_tables(positions)
     stacked = (
         attn_gain,
@@ -341,7 +699,7 @@
     saved_layers = []
     for layer_index in range(LAYER_COUNT):
         weights = tuple((w[layer_index] for w in stacked))
-        hidden, saved = forward_layer(hidden, weights, rotary_tables, visible, reach, stretch)
+        hidden, saved = forward_layer(hidden, weights, rotary_tables, visible, reach, stretch, 1 + 8 * layer_index)
         saved_layers.append(saved)
     output = hidden.astype(jnp.bfloat16).reshape(seqs_here, stretch, width)
     grad = cotangent.astype(jnp.float32).reshape(rows, width)
@@ -349,9 +707,10 @@
     for layer_index in range(LAYER_COUNT - 1, -1, -1):
         weights = tuple((w[layer_index] for w in stacked))
         grad, gain_grads, matrix_grads = backward_layer(
-            grad, weights, saved_layers[layer_index], rotary_tables, visible, reach, stretch
+            grad, weights, saved_layers[layer_index], rotary_tables, visible, reach, stretch,
+            1 + 8 * layer_index,
         )
-        reduced[layer_index] = reduce_grads(gain_grads, matrix_grads)
+        reduced[layer_index] = reduce_grads(gain_grads, matrix_grads, 5 + 8 * layer_index)
     input_grad = grad.reshape(seqs_here, stretch, width)
     outs = [
         jnp.stack([reduced[layer_index][slot] for layer_index in range(LAYER_COUNT)])

time: 1660 us -> 1080 us (0.65)
  waiting for transfers between devices: 968 us -> 0.01 us
  Pallas kernels: 0 us -> 625 us
  matrix products: 301 us -> 101 us
  other arithmetic: 226 us -> 129 us
  local copies, waits for them, and re-layouts: 87.6 us -> 171 us
    psum x7 -> x0, waiting for transfers between devices: 634 us -> none  [the longest x2 242 us: forward_layer(): lax.psum(mlp_part.astype(jnp.bfloat16), 'tensor').astype(jnp.float32)]
    pallas_call x0 -> x14, Pallas kernels: none -> 625 us  [the longest x8 490 us: line_sum(): pl.pallas_call(functools.partial(line_sum_kernel, chunks), out_shape=jax....]
    reduce_scatter x14 -> x0, waiting for transfers between devices: 332 us -> none  [the longest x2 76.1 us: reduce_grads(): lax.psum_scatter(grad_q.astype(jnp.bfloat16), ('dp', 'seq'), scatter_dime...]
    dot_general x12 -> x0, matrix products: 176 us -> none  [the longest x2 44.2 us: backward_layer(): jnp.einsum('sqhgd,skhd->shgqk', d_context, value_window, preferred_elemen...]
    another operation x4 -> x2, other arithmetic: 61.9 us -> 3.83 us
    reduce_sum x4 -> x3, other arithmetic: 37.5 us -> 10.7 us  [the longest x2 9.72 us: attention_backward(): jnp.sum(product.reshape(seqs_here, stretch, kv_heads, group, HEAD_SIZE), -1)]
    reshape x0 -> x8, local copies, waits for them, and re-layouts: none -> 19.3 us  [the longest x4 9.02 us: backward_layer(): d_queries.reshape(seqs_here, stretch, -1, HEAD_SIZE)]
    unnamed x338 -> x426, local copies, waits for them, and re-layouts: 45.3 us -> 54.2 us
  transfers between devices with their start and end apart: 25 -> 4, of which waited for: 18 -> 0; matrix products, arithmetic and copies ran while one was open for 16% -> 8% of each run, Pallas kernels for 0% -> 4%
where the time goes in v1:
time: 1080 us; the launch traced here: 1070 us
  Pallas kernels  625 us (58%)
  local copies, waits for them, and re-layouts  171 us (16%)
  other arithmetic  129 us (12%)
  matrix products  101 us (9%)
  blocking collectives  33.9 us (3%)
    pallas_call x8, Pallas kernels, line_sum(): pl.pallas_call(functools.partial(line_sum_kernel, chunks), out_shape=jax....  490 us
    pallas_call x2, Pallas kernels, scatter_sums(): pl.pallas_call(functools.partial(scatter_kernel, orders, axes), out_shape...  87.4 us
    unnamed x426, local copies, waits for them, and re-layouts  54.2 us
    pallas_call x2, Pallas kernels, attn_bwd(): pl.pallas_call(functools.partial(attn_bwd_kernel, qb, kb, offset), grid_s...  27.8 us
    psum x1, blocking collectives, reduce_grads(): lax.psum((gain_a, gain_q, gain_k, gain_m), ('dp', 'seq'))  22.4 us
  transfers between devices with their start and end apart: 4, of which 0 were waited for; matrix products, arithmetic and copies ran while one was open for 8% of the time, Pallas kernels for 4%

profile of v1, /device:TPU:0, one launch (start us, length us, event | category | flops | bytes accessed | tf_op | source)
XLA Modules:
  0.0 1072.1 jit_solution(12704610182489724351)
XLA Ops:
  19.2 3.5 collective-permute-start
  29.7 2.9 pad_maximum_fusion.2
  38.5 3.0 copy.181
  52.0 9.7 attn_fwd.2
  65.3 63.6 %line_sum.8 = bf16[1024,1024]{1,0:T(8,128)(2,1)S(1)} custom-call(bf16[1024,1024]{1,0:T(8,128)(2,1)S(1)} %convolution_convert_fusion.1.x_ref), custom_call_target="tpu_custom_call" | custom-call | tf_op jit(solution)/shard_map/line_sum/pallas_call | solution.py:311
  134.3 3.6 multiply_convert_fusion.8
  139.7 61.4 %line_sum.9 = bf16[1024,1024]{1,0:T(8,128)(2,1)S(1)} custom-call(bf16[1024,1024]{1,0:T(8,128)(2,1)S(1)} %convolution_convert_fusion.3.x_ref), custom_call_target="tpu_custom_call" | custom-call | tf_op jit(solution)/shard_map/line_sum/pallas_call | solution.py:311
  210.7 3.3 fusion.103
  214.0 2.7 fusion.125
  222.7 2.8 fusion.150
  226.6 3.0 collective-permute-start.1
  232.6 2.9 copy.133
  242.8 2.9 copy.183
  246.0 2.7 reshape.1326
  251.1 4.5 fusion.50.q_ref
  258.1 9.6 attn_fwd.3
  271.0 62.7 %line_sum.10 = bf16[1024,1024]{1,0:T(8,128)(2,1)S(1)} custom-call(bf16[1024,1024]{1,0:T(8,128)(2,1)S(1)} %convolution_convert_fusion.x_ref), custom_call_target="tpu_custom_call" | custom-call | tf_op jit(solution)/shard_map/line_sum/pallas_call | solution.py:311
  341.4 5.0 multiply_convert_fusion.5
  346.4 3.8 fusion.73
  352.0 59.6 %line_sum.12 = bf16[1024,1024]{1,0:T(8,128)(2,1)S(1)} custom-call(bf16[1024,1024]{1,0:T(8,128)(2,1)S(1)} %add_convert_fusion.3.x_ref), custom_call_target="tpu_custom_call" | custom-call | tf_op jit(solution)/shard_map/line_sum/pallas_call | solution.py:311
  415.7 60.8 %line_sum.11 = bf16[1024,1024]{1,0:T(8,128)(2,1)S(1)} custom-call(bf16[1024,1024]{1,0:T(8,128)(2,1)S(1)} %convolution_convert_fusion.2.x_ref), custom_call_target="tpu_custom_call" | custom-call | tf_op jit(solution)/shard_map/line_sum/pallas_call | solution.py:311
  476.5 2.7 fusion.24
  483.5 3.0 fusion.87
  488.2 3.5 reshape.1304
  491.8 5.4 reduce_sum.259
  503.9 13.9 %attn_bwd.2 = (f32[1024,512]{1,0:T(8,128)S(1)}, f32[2048,256]{1,0:T(8,128)S(1)}, f32[2048,256]{1,0:T(8,128)S(1)}) custom-call(s32[2]{0:T(128)S(1)} %bitcast.521, s32[1,1024]{1,0:T(1,128)S(1)} %add_maximum_fusion.1.low_ref, f32[2,2,1024]{2,1,0:T(2,128)S(1)} %bitcast.518, f32[2,2,1024]{2,1,0:T(2,128)S(1)} %bitcast.516, bf16[1024,512]{1,0:T(8,128)(2,1)S(1)} %fusion.50.q_ref, ...), custom_call_target="tpu_custom_call" | custom-call | tf_op jit(solution)/shard_map/attn_bwd/pallas_call | solution.py:150
  521.8 3.1 copy.189
  531.8 3.0 copy.185
  534.7 2.8 fusion.56
  540.2 4.0 fusion.46
  547.4 2.9 copy.165
  552.0 2.6 reshape.1325
  554.7 2.6 copy.160
  557.3 5.3 convolution_convert_fusion.5
  562.5 3.1 convolution_convert_fusion.4
  569.1 2.7 fusion.152
  589.3 59.3 %line_sum.13 = bf16[1024,1024]{1,0:T(8,128)(2,1)S(1)} custom-call(bf16[1024,1024]{1,0:T(8,128)(2,1)S(1)} %add_convert_fusion.2.x_ref), custom_call_target="tpu_custom_call" | custom-call | tf_op jit(solution)/shard_map/line_sum/pallas_call | solution.py:311
  653.6 5.0 multiply_convert_fusion.3
  663.0 62.7 %line_sum.14 = bf16[1024,1024]{1,0:T(8,128)(2,1)S(1)} custom-call(bf16[1024,1024]{1,0:T(8,128)(2,1)S(1)} %add_convert_fusion.1.x_ref), custom_call_target="tpu_custom_call" | custom-call | tf_op jit(solution)/shard_map/line_sum/pallas_call | solution.py:311
  733.5 3.0 convolution_convert_fusion.6
  736.5 3.0 convolution_convert_fusion.8
  751.3 2.7 reshape.1306
  754.0 4.3 reduce_sum.264
  763.4 13.9 %attn_bwd.3 = (f32[1024,512]{1,0:T(8,128)S(1)}, f32[2048,256]{1,0:T(8,128)S(1)}, f32[2048,256]{1,0:T(8,128)S(1)}) custom-call(s32[2]{0:T(128)S(1)} %bitcast.522, s32[1,1024]{1,0:T(1,128)S(1)} %add_maximum_fusion.1.low_ref, f32[2,2,1024]{2,1,0:T(2,128)S(1)} %bitcast.515, f32[2,2,1024]{2,1,0:T(2,128)S(1)} %bitcast.517, bf16[1024,512]{1,0:T(8,128)(2,1)S(1)} %copy-done.3, ...), custom_call_target="tpu_custom_call" | custom-call | tf_op jit(solution)/shard_map/attn_bwd/pallas_call | solution.py:150
  789.1 2.8 copy.161
  791.9 5.0 pad_maximum_fusion.5
  797.2 2.9 copy.187
  801.7 4.6 fusion.43
  811.6 48.1 %scatter_sums.3 = (f32[128,512]{1,0:T(8,128)S(1)}, f32[128,256]{1,0:T(8,128)S(1)}, f32[128,256]{1,0:T(8,128)S(1)}, f32[128,512]{1,0:T(8,128)S(1)}, f32[128,768]{...) custom-call(bf16[2,2,2,128,512]{4,3,2,1,0:T(8,128)(2,1)S(1)} %bitcast.495, ...), custom_call_target="tpu_custom_call" | custom-call | tf_op jit(solution)/shard_map/scatter_sums/pallas_call | solution.py:419
  859.8 5.3 convolution_convert_fusion.7
  865.4 5.4 fusion.58
  874.9 2.6 copy.192
  882.2 3.3 pad_maximum_fusion.11
  891.0 2.6 copy.188
  895.9 2.7 fusion.106
  900.0 2.7 fusion.162
  902.7 2.7 fusion.159
  905.4 39.2 %scatter_sums.2 = (f32[128,512]{1,0:T(8,128)S(1)}, f32[128,256]{1,0:T(8,128)S(1)}, f32[128,256]{1,0:T(8,128)S(1)}, f32[128,512]{1,0:T(8,128)S(1)}, f32[128,768]{...) custom-call(bf16[2,2,2,128,512]{4,3,2,1,0:T(8,128)(2,1)S(1)} %bitcast.496, ...), custom_call_target="tpu_custom_call" | custom-call | tf_op jit(solution)/shard_map/scatter_sums/pallas_call | solution.py:419
  950.8 4.0 fusion.119
  954.8 9.5 all-reduce.2
  966.5 5.3 add_convert_fusion.x_ref
  971.8 60.3 %line_sum.15 = bf16[1024,1024]{1,0:T(8,128)(2,1)S(1)} custom-call(bf16[1024,1024]{1,0:T(8,128)(2,1)S(1)} %add_convert_fusion.x_ref), custom_call_target="tpu_custom_call" | custom-call | tf_op jit(solution)/shard_map/line_sum/pallas_call | solution.py:311
  1037.8 4.8 fusion.15
  1044.6 22.4 %all-reduce.1 = (f32[1,1024]{1,0:T(1,128)S(1)}, f32[1,1024]{1,0:T(1,128)S(1)}, f32[1,128]{1,0:T(1,128)S(1)}, f32[1,128]{1,0:T(1,128)S(1)}, f32[1,128]{1,0:T(1,12...) all-reduce(f32[1,1024]{1,0:T(1,128)S(1)} %bitcast.608, ...), channel_id=1, replica_groups=mesh['dp'=4,'seq'=2,'tensor'=4] {'dp','seq'}, use_global_device_ids=true, to_apply=%region_22.23 | all-reduce | flops 4608 | bytes 36864 | tf_op jit(solution)/shard_map/psum | solution.py:632
  (611 shorter events, 243.5 us)
Async XLA Ops:
  1.5 21.2 %copy-start.165 = (f32[1,1024]{1,0:T(1,128)}, f32[1,1024]{1,0:T(1,128)S(1)}, u32[]{:S(2)}) copy-start(f32[1,1024]{1,0:T(1,128)S(1)} %get-tuple-element.185) | copy-start | bytes 12292
  3.6 19.1 %copy-start.163 = (f32[1024]{0:T(1024)}, f32[1024]{0:T(1024)S(1)}, u32[]{:S(2)}) copy-start(f32[1024]{0:T(1024)S(1)} %add_rsqrt_fusion.7) | copy-start | bytes 12292
  7.1 6.0 copy-start.178
  18.2 6.0 copy-start.127
  18.2 4.6 copy-start.140
  19.2 30.8 %collective-permute-start = (bf16[2,1,1024,256]{3,2,1,0:T(8,128)(2,1)}, bf16[2,1,1024,256]{3,2,1,0:T(8,128)(2,1)}, u32[]{:S(2)}, u32[]{:S(2)}) collective-permute-start(bf16[2,1,1024,256]{3,2,1,0:T(8,128)(2,1)} %pad_maximum_fusion.7), channel_id=1, source_target_pairs={{0,4},{1,5},{2,6},{3,7},{8,12},{9,13},{10,14},{11,15},{16,20},{17,... | collective-permute-start | bytes 3145736 | tf_op jit(solution)/shard_map/ppermute | solution.py:439
  24.9 7.7 copy-start.153
  24.9 21.4 %copy-start.169 = (f32[512]{0:T(512)}, f32[512]{0:T(512)S(1)}, u32[]{:S(2)}) copy-start(f32[512]{0:T(512)S(1)} %broadcast_bitcast_fusion.1) | copy-start | bytes 6148
  38.5 4.2 copy-start.72
  44.1 85.6 %copy-start.161 = (f32[1,1024]{1,0:T(1,128)}, f32[1,1024]{1,0:T(1,128)S(1)}, u32[]{:S(2)}) copy-start(f32[1,1024]{1,0:T(1,128)S(1)} %get-tuple-element.183) | copy-start | bytes 12292
  44.2 7.8 copy-start.20
  52.0 11.1 %copy-start.4 = (bf16[2048,256]{1,0:T(8,128)(2,1)}, bf16[2048,256]{1,0:T(8,128)(2,1)S(1)}, u32[]{:S(2)}) copy-start(bf16[2048,256]{1,0:T(8,128)(2,1)S(1)} %get-tuple-element.164.v_ref) | copy-start | bytes 3145732
  52.0 11.1 %copy-start.6 = (bf16[2048,256]{1,0:T(8,128)(2,1)}, bf16[2048,256]{1,0:T(8,128)(2,1)S(1)}, u32[]{:S(2)}) copy-start(bf16[2048,256]{1,0:T(8,128)(2,1)S(1)} %get-tuple-element.165.k_ref) | copy-start | bytes 3145732
  52.0 12.1 %copy-start.200 = (bf16[2,512,1024]{2,1,0:T(8,128)(2,1)S(1)}, bf16[2,512,1024]{2,1,0:T(8,128)(2,1)}, u32[]{:S(2)}) copy-start(bf16[2,512,1024]{2,1,0:T(8,128)(2,1)} %param.25) | copy-start | bytes 6291460
  65.3 63.6 %copy-start.51 = (bf16[1,1024,1024]{2,1,0:T(8,128)(2,1)S(1)}, bf16[1,1024,1024]{2,1,0:T(8,128)(2,1)}, u32[]{:S(2)}) copy-start(bf16[1,1024,1024]{2,1,0:T(8,128)(2,1)} %param.15) | copy-start | bytes 6291460
  225.5 4.3 copy-start.129
  226.6 29.1 %collective-permute-start.1 = (bf16[2,1,1024,256]{3,2,1,0:T(8,128)(2,1)}, bf16[2,1,1024,256]{3,2,1,0:T(8,128)(2,1)}, u32[]{:S(2)}, u32[]{:S(2)}) collective-permute-start(bf16[2,1,1024,256]{3,2,1,0:T(8,128)(2,1)} %pad_maximum_fusion.9), channel_id=1, source_target_pairs={{0,4},{1,5},{2,6},{3,7},{8,12},{9,13},{10,14},{11,15},{16,20},{17,... | collective-permute-start | bytes 3145736 | tf_op jit(solution)/shard_map/ppermute | solution.py:439
  250.8 4.9 copy-start.85
  251.1 4.5 copy-start.130
  251.1 4.6 copy-start.150
  257.2 10.5 copy-start.10
  257.2 12.5 %copy-start.201 = (bf16[2,512,1024]{2,1,0:T(8,128)(2,1)S(1)}, bf16[2,512,1024]{2,1,0:T(8,128)(2,1)}, u32[]{:S(2)}) copy-start(bf16[2,512,1024]{2,1,0:T(8,128)(2,1)} %param.25) | copy-start | bytes 6291460
  271.0 62.7 %copy-start.57 = (f32[1024,1024]{1,0:T(8,128)S(1)}, f32[1024,1024]{1,0:T(8,128)}, u32[]{:S(2)}) copy-start(f32[1024,1024]{1,0:T(8,128)} %copy-done.56) | copy-start | bytes 12582916
  481.3 5.3 copy-start.24
  527.2 4.3 copy-start.99
  527.2 4.3 copy-start.101
  534.7 5.4 copy-start.61
  534.7 5.4 copy-start.73
  537.5 28.2 %collective-permute-start.2 = (bf16[2,1,1024,256]{3,2,1,0:T(8,128)(2,1)}, bf16[2,1,1024,256]{3,2,1,0:T(8,128)(2,1)}, u32[]{:S(2)}, u32[]{:S(2)}) collective-permute-start(bf16[2,1,1024,256]{3,2,1,0:T(8,128)(2,1)} %fusion.56), channel_id=1, source_target_pairs={{4,0},{5,1},{6,2},{7,3},{12,8},{13,9},{14,10},{15,11},{20,16},{21,... | collective-permute-start | bytes 3145736 | tf_op jit(solution)/shard_map/ppermute | solution.py:439
  540.2 5.0 copy-start.115
  557.3 5.3 copy-start.146
  557.3 5.3 copy-start.206
  576.7 6.1 copy-start.65
  589.3 59.3 %copy-start.58 = (f32[1024,1024]{1,0:T(8,128)S(1)}, f32[1024,1024]{1,0:T(8,128)}, u32[]{:S(2)}) copy-start(f32[1024,1024]{1,0:T(8,128)} %copy-done.56) | copy-start | bytes 12582916
  653.6 5.0 copy-start.196
  663.0 62.8 %copy-start.52 = (bf16[1,1024,1024]{2,1,0:T(8,128)(2,1)S(1)}, bf16[1,1024,1024]{2,1,0:T(8,128)(2,1)}, u32[]{:S(2)}) copy-start(bf16[1,1024,1024]{2,1,0:T(8,128)(2,1)} %param.15) | copy-start | bytes 6291460
  663.0 62.8 %copy-start.160 = (f32[1024]{0:T(1024)S(1)}, f32[1024]{0:T(1024)}, u32[]{:S(2)}) copy-start(f32[1024]{0:T(1024)} %copy-done.159) | copy-start | bytes 12292
  663.0 62.8 %copy-start.162 = (f32[1,1024]{1,0:T(1,128)S(1)}, f32[1,1024]{1,0:T(1,128)}, u32[]{:S(2)}) copy-start(f32[1,1024]{1,0:T(1,128)} %copy-done.161) | copy-start | bytes 12292
  731.3 18.3 %copy-start.22 = (bf16[1024,512]{1,0:T(8,128)(2,1)}, bf16[1024,512]{1,0:T(8,128)(2,1)S(1)}, u32[]{:S(2)}) copy-start(bf16[1024,512]{1,0:T(8,128)(2,1)S(1)} %convolution_convert_fusion.13.do_ref) | copy-start | bytes 3145732
  744.9 4.6 copy-start.27
  754.0 5.7 copy-start.3
  801.7 4.6 copy-start.53
  801.7 4.6 copy-start.164
  801.7 4.7 copy-start.166
  810.0 60.7 %collective-permute-start.3 = (bf16[2,1,1024,256]{3,2,1,0:T(8,128)(2,1)}, bf16[2,1,1024,256]{3,2,1,0:T(8,128)(2,1)}, u32[]{:S(2)}, u32[]{:S(2)}) collective-permute-start(bf16[2,1,1024,256]{3,2,1,0:T(8,128)(2,1)} %fusion.55), channel_id=1, source_target_pairs={{4,0},{5,1},{6,2},{7,3},{12,8},{13,9},{14,10},{15,11},{20,16},{21,... | collective-permute-start | bytes 3145736 | tf_op jit(solution)/shard_map/ppermute | solution.py:439
  859.7 5.4 copy-start.34
  859.7 5.4 copy-start.40
  859.7 5.4 copy-start.42
  859.7 5.4 copy-start.108
  859.7 5.4 copy-start.109
  859.7 5.4 copy-start.110
  859.7 5.4 copy-start.111
  859.8 5.6 copy-start.112
  859.8 5.6 copy-start.157
  859.8 5.6 copy-start.158
  889.9 6.0 copy-start.175
  947.5 7.3 copy-start.44
  971.8 60.3 %copy-start.55 = (bf16[1,1024,1024]{2,1,0:T(8,128)(2,1)S(1)}, bf16[1,1024,1024]{2,1,0:T(8,128)(2,1)}, u32[]{:S(2)}) copy-start(bf16[1,1024,1024]{2,1,0:T(8,128)(2,1)} %param.15) | copy-start | bytes 6291460
  1037.8 4.9 copy-start.33
  1042.6 26.1 %copy-start.43 = (f32[128,256]{1,0:T(8,128)S(1)}, f32[128,256]{1,0:T(8,128)}, u32[]{:S(2)}) copy-start(f32[128,256]{1,0:T(8,128)} %copy-done.42) | copy-start | bytes 393220
  1042.7 26.1 %copy-start.47 = (f32[128,256]{1,0:T(8,128)S(1)}, f32[128,256]{1,0:T(8,128)}, u32[]{:S(2)}) copy-start(f32[128,256]{1,0:T(8,128)} %copy-done.46) | copy-start | bytes 393220
  1042.7 26.8 %copy-start.41 = (f32[128,256]{1,0:T(8,128)S(1)}, f32[128,256]{1,0:T(8,128)}, u32[]{:S(2)}) copy-start(f32[128,256]{1,0:T(8,128)} %copy-done.40) | copy-start | bytes 393220
  1042.7 26.8 %copy-start.45 = (f32[128,256]{1,0:T(8,128)S(1)}, f32[128,256]{1,0:T(8,128)}, u32[]{:S(2)}) copy-start(f32[128,256]{1,0:T(8,128)} %copy-done.44) | copy-start | bytes 393220
  1042.7 27.5 %copy-start.37 = (f32[128,512]{1,0:T(8,128)S(1)}, f32[128,512]{1,0:T(8,128)}, u32[]{:S(2)}) copy-start(f32[128,512]{1,0:T(8,128)} %copy-done.36) | copy-start | bytes 786436
  (152 other events, 329.5 us)

commit v2 on v0

v2 whole, which is shorter than its diff:
```python
import functools
import types

import jax
import jax.numpy as jnp
from jax import lax
from jax.experimental import pallas as pl
from jax.experimental.pallas import tpu as pltpu
from jax.sharding import PartitionSpec as P

HEAD = 128
LAYER_COUNT = 2
WINDOW = 1024
EPS = 1e-06
THETA = 1000000.0
LOG2E = 1.4426950408889634
SCALE = HEAD ** (-0.5)
CHUNK = 128
PIECES = 2
MESH = pl.DeviceIdType.MESH
BF = jnp.bfloat16
F32 = jnp.float32

NT = (((1,), (1,)), ((), ()))
NN = (((1,), (0,)), ((), ()))
TN = (((0,), (0,)), ((), ()))


def dot(a, b, dims=NN):
    return lax.dot_general(a, b, dims, preferred_element_type=F32)


def attn_fwd_kernel(qb, kb, offset, stretch, first_ref, low_ref, q_ref, k_ref, v_ref, o_ref, lse_ref):
    step = pl.program_id(2)
    heads = q_ref.shape[1] // HEAD
    q_start = step * qb + offset
    queries = [q_ref[:, h * HEAD : (h + 1) * HEAD] for h in range(heads)]
    q_index = q_start + lax.broadcasted_iota(jnp.int32, (qb, 1), 0)
    low = low_ref[...]

    def block(kk, carry):
        start = kk * kb
        place = (start // stretch, pl.ds(pl.multiple_of(lax.rem(start, stretch), kb), kb))
        keys = k_ref[place]
        values = v_ref[place]
        key_index = start + lax.broadcasted_iota(jnp.int32, (qb, kb), 1)
        mask = (key_index >= low) & (key_index <= q_index)
        out = []
        for h in range(heads):
            acc, total = carry[h]
            s = dot(queries[h], keys, NT) * (SCALE * LOG2E)
            p = jnp.where(mask, jnp.exp2(s), 0.0)
            part = p[:, :HEAD]
            for c in range(1, kb // HEAD):
                part = part + p[:, c * HEAD : (c + 1) * HEAD]
            out.append((acc + dot(p.astype(BF), values), total + part))
        return tuple(out)

    zero = jnp.zeros((qb, HEAD), F32)
    first = first_ref[pl.program_id(0) * pl.num_programs(2) + step] // kb
    last = (q_start + qb - 1) // kb + 1
    result = lax.fori_loop(first, last, block, tuple((zero, zero) for _ in range(heads)))
    for h in range(heads):
        acc, total = result[h]
        o_ref[:, h * HEAD : (h + 1) * HEAD] = (acc / jnp.sum(total, 1, keepdims=True)).astype(BF)
        lse_ref[h : h + 1, :] = jnp.log2(jnp.sum(total.T, 0, keepdims=True))


def attn_fwd(q, window, first, low, stretch, qb=512, kb=512):
    rows = q.shape[0]
    reach = window.shape[0] - 1
    kv_heads = window.shape[2] // (2 * HEAD)
    width = q.shape[1] // kv_heads
    group = width // HEAD
    steps = stretch // qb
    return pl.pallas_call(
        functools.partial(attn_fwd_kernel, qb, kb, reach * stretch, stretch),
        grid_spec=pltpu.PrefetchScalarGridSpec(
            num_scalar_prefetch=1,
            grid=(rows // stretch, kv_heads, steps),
            in_specs=[
                pl.BlockSpec((qb, 1), lambda s, g, i, f: (s * steps + i, 0)),
                pl.BlockSpec((qb, width), lambda s, g, i, f: (s * steps + i, g)),
                pl.BlockSpec((reach + 1, stretch, HEAD), lambda s, g, i, f: (0, s, g)),
                pl.BlockSpec((reach + 1, stretch, HEAD), lambda s, g, i, f: (0, s, kv_heads + g)),
            ],
            out_specs=[
                pl.BlockSpec((qb, width), lambda s, g, i, f: (s * steps + i, g)),
                pl.BlockSpec((None, group, qb), lambda s, g, i, f: (g, 0, s * steps + i)),
            ],
        ),
        out_shape=[
            jax.ShapeDtypeStruct(q.shape, BF),
            jax.ShapeDtypeStruct((kv_heads, group, rows), F32),
        ],
        name=attn_fwd.__name__,
        compiler_params=pltpu.CompilerParams(vmem_limit_bytes=62 << 20),
    )(first, low[:, None], q, window, window)


def attn_bwd_kernel(qb, kb, offset, stretch, first_ref, low_ref, lse_ref, q_ref, do_ref, o_ref, k_ref, v_ref,
                    dq_ref, own_ref, prev_ref, dk_ref, dv_ref):
    step = pl.program_id(2)
    heads = q_ref.shape[1] // HEAD
    q_start = step * qb + offset

    @pl.when(step == 0)
    def _():
        dk_ref[...] = jnp.zeros_like(dk_ref)
        dv_ref[...] = jnp.zeros_like(dv_ref)

    def stack(ref):
        return jnp.concatenate([ref[:, h * HEAD : (h + 1) * HEAD] for h in range(heads)], 0)

    queries = stack(q_ref)
    d_out = stack(do_ref)
    q_index = q_start + lax.broadcasted_iota(jnp.int32, (1, qb), 1)
    low = low_ref[...]
    lse = jnp.concatenate([lse_ref[h : h + 1, :] for h in range(heads)], 1)
    product = d_out.astype(F32) * stack(o_ref).astype(F32)
    delta = jnp.sum(product.T, 0, keepdims=True)

    def block(kk, dq):
        start = kk * kb
        place = (start // stretch, pl.ds(pl.multiple_of(lax.rem(start, stretch), kb), kb))
        here = pl.ds(pl.multiple_of(start, kb), kb)
        keys = k_ref[place]
        values = v_ref[place]
        key_index = start + lax.broadcasted_iota(jnp.int32, (kb, qb), 0)
        mask = (key_index >= low) & (key_index <= q_index)
        mask = jnp.concatenate([mask] * heads, 1)
        s = dot(keys, queries, NT) * (SCALE * LOG2E) - lse
        p = jnp.where(mask, jnp.exp2(s), 0.0)
        dp = dot(values, d_out, NT)
        ds = (p * (dp - delta)).astype(BF)
        dv_ref[here, :] += dot(p.astype(BF), d_out)
        dk_ref[here, :] += dot(ds, queries)
        return dq + dot(ds, keys, TN)

    first = first_ref[pl.program_id(0) * pl.num_programs(2) + step] // kb
    last = (q_start + qb - 1) // kb + 1
    dq = lax.fori_loop(first, last, block, jnp.zeros((heads * qb, HEAD), F32))
    for h in range(heads):
        dq_ref[:, h * HEAD : (h + 1) * HEAD] = dq[h * qb : (h + 1) * qb] * SCALE

    @pl.when(step == pl.num_programs(2) - 1)
    def _():
        own_ref[0] = dk_ref[offset:, :] * SCALE
        own_ref[1] = dv_ref[offset:, :]
        for j in range(offset // stretch):
            prev_ref[j, 0] = (dk_ref[j * stretch : (j + 1) * stretch, :] * SCALE).astype(BF)
            prev_ref[j, 1] = dv_ref[j * stretch : (j + 1) * stretch, :].astype(BF)


def attn_bwd(q, d_out, o, window, first, low, lse, stretch, qb=512, kb=512):
    rows = q.shape[0]
    reach = window.shape[0] - 1
    kv_heads = window.shape[2] // (2 * HEAD)
    width = q.shape[1] // kv_heads
    group = width // HEAD
    steps = stretch // qb
    span = (reach + 1) * stretch
    held = max(reach, 1)
    row_spec = pl.BlockSpec((qb, width), lambda s, g, i, f: (s * steps + i, g))
    return pl.pallas_call(
        functools.partial(attn_bwd_kernel, qb, kb, reach * stretch, stretch),
        grid_spec=pltpu.PrefetchScalarGridSpec(
            num_scalar_prefetch=1,
            grid=(rows // stretch, kv_heads, steps),
            in_specs=[
                pl.BlockSpec((1, qb), lambda s, g, i, f: (0, s * steps + i)),
                pl.BlockSpec((None, group, qb), lambda s, g, i, f: (g, 0, s * steps + i)),
                row_spec,
                row_spec,
                row_spec,
                pl.BlockSpec((reach + 1, stretch, HEAD), lambda s, g, i, f: (0, s, g)),
                pl.BlockSpec((reach + 1, stretch, HEAD), lambda s, g, i, f: (0, s, kv_heads + g)),
            ],
            out_specs=[
                row_spec,
                pl.BlockSpec((2, stretch, HEAD), lambda s, g, i, f: (0, s, g)),
                pl.BlockSpec((held, 2, stretch, HEAD), lambda s, g, i, f: (0, 0, s, g)),
            ],
            scratch_shapes=[pltpu.VMEM((span, HEAD), F32), pltpu.VMEM((span, HEAD), F32)],
        ),
        out_shape=[
            jax.ShapeDtypeStruct(q.shape, F32),
            jax.ShapeDtypeStruct((2, rows, kv_heads * HEAD), F32),
            jax.ShapeDtypeStruct((held, 2, rows, kv_heads * HEAD), BF),
        ],
        name=attn_bwd.__name__,
        cost_estimate=pl.CostEstimate(flops=3 * 10**10, bytes_accessed=12 * 2**20, transcendentals=4 * 2**20),
        compiler_params=pltpu.CompilerParams(vmem_limit_bytes=62 << 20),
    )(first, low[None], lse, q, d_out, o, window, window)


def chunk_index(schedule, s):
    rate, lag, count = schedule
    return jnp.clip((s - lag) // rate, 0, count - 1)


def rows_spec(schedule, shape):
    return pl.BlockSpec((shape[0] // schedule[2], shape[1]), lambda s: (chunk_index(schedule, s), 0))


WHOLE, HBM = object(), object()
MLP_WEIGHTS = ("w_gate", "w_up", "w_down")
QKV_WEIGHTS = ("w_q", "w_k", "w_v")
GRAD_OPERANDS = ("d_gate_all", "d_up_all", "context_all", "act_all")


def of_layer(array, layer):
    shape = array.shape[1:]
    zeros = (0,) * len(shape)
    return array, pl.BlockSpec((None,) + shape, lambda s: (layer,) + zeros, pipeline_mode=pl.Buffered(1))


class Late:
    def __init__(self, layer=None):
        self.layer = layer

    def shape(self, array):
        return array.shape if self.layer is None else array.shape[1:]

    def copy(self, source, held, sem):
        return pltpu.make_async_copy(source if self.layer is None else source.at[self.layer], held, sem)


def step_kernel(owner, body, steps, ins, outs, scratch, collective_id, vmem=62):
    def spec(shape, where, is_in):
        if isinstance(where, pl.BlockSpec):
            return where
        if where is HBM or isinstance(where, Late):
            return pl.BlockSpec(memory_space=pl.ANY)
        if where is WHOLE:
            zeros = (0,) * len(shape)
            if is_in:
                return pl.BlockSpec(shape, lambda s: zeros, pipeline_mode=pl.Buffered(1))
            return pl.BlockSpec(memory_space=pltpu.VMEM)
        return rows_spec(where, shape)

    late = {name: where for name, (_, where) in ins.items() if isinstance(where, Late)}
    held = {name: pltpu.VMEM(where.shape(ins[name][0]), ins[name][0].dtype) for name, where in late.items()}
    flat, tree = jax.tree.flatten((scratch, held, {name: pltpu.SemaphoreType.DMA(()) for name in late}))

    def kernel(*refs):
        named = dict(zip(ins, refs))
        named.update(zip(outs, refs[len(ins) :]))
        own, held_refs, sems = jax.tree.unflatten(tree, refs[len(ins) + len(outs) :])
        copies = {name: where.copy(named[name], held_refs[name], sems[name]) for name, where in late.items()}
        for name, ref in own.items():
            named[name] = types.SimpleNamespace(**ref) if isinstance(ref, dict) else ref
        named.update(held_refs)
        s = pl.program_id(0)

        @pl.when(s == 0)
        def _():
            for copy in copies.values():
                copy.start()

        def arrived(step, *names):
            @pl.when(s == step)
            def _():
                for name in names:
                    copies[name].wait()

        body(types.SimpleNamespace(arrived=arrived, **named), s)

    results = pl.pallas_call(
        kernel,
        grid=(steps,),
        in_specs=[spec(a.shape, w, True) for a, w in ins.values()],
        out_specs=[spec(shape, w, False) for shape, _, w in outs.values()],
        out_shape=[jax.ShapeDtypeStruct(shape, dtype) for shape, dtype, _ in outs.values()],
        scratch_shapes=flat,
        name=owner.__name__,
        compiler_params=pltpu.CompilerParams(
            collective_id=collective_id, has_side_effects=True, vmem_limit_bytes=vmem << 20
        ),
    )(*[a for a, _ in ins.values()])
    return types.SimpleNamespace(**dict(zip(outs, results)))


def at_chunk(s, schedule, work):
    rate, lag, count = schedule
    moved = s - lag
    here = (moved >= 0) & (moved < rate * count)
    if rate > 1:
        here = here & (lax.rem(moved, rate) == 0)

    @pl.when(here)
    def _():
        work(moved // rate if rate > 1 else moved)


def enter(devices):
    barrier = pltpu.get_barrier_semaphore()
    count = 0
    for device, exists in devices:
        if exists is True:
            pl.semaphore_signal(barrier, inc=1, device_id=device, device_id_type=MESH)
            count = count + 1
        else:

            @pl.when(exists)
            def _():
                pl.semaphore_signal(barrier, inc=1, device_id=device, device_id_type=MESH)

            count = count + jnp.where(exists, 1, 0)
    pl.semaphore_wait(barrier, count)


class LineSum:
    def __init__(self, refs, x=None):
        self.x, self.land = refs.x if x is None else x, refs.land
        self.send_sem, self.land_sem, self.out_sem = refs.send, refs.arrive, refs.out
        self.pieces = self.send_sem.shape[0]
        self.rows = self.x.shape[0] // self.pieces
        n = lax.axis_size("tensor")
        z = lax.axis_index("tensor")
        half = n // 2
        self.middle = (z == half - 1) | (z == half)
        self.has_outer = (z > 0) & (z < n - 1)
        self.inner = jnp.where(z < half, z + 1, z - 1)
        self.outer = jnp.clip(jnp.where(z < half, z - 1, z + 1), 0, n - 1)
        self.slot = jnp.where(self.middle, 1, 0)

    @staticmethod
    def scratch(rows, width, pieces):
        return dict(
            x=pltpu.VMEM((rows, width), BF),
            land=pltpu.VMEM((2, rows, width), BF),
            send=pltpu.SemaphoreType.DMA((pieces,)),
            arrive=pltpu.SemaphoreType.DMA((2, pieces)),
            out=pltpu.SemaphoreType.DMA((pieces,)),
        )

    def neighbours(self):
        return [({"tensor": self.inner}, True), ({"tensor": self.outer}, self.has_outer)]

    def at(self, j, rows=None):
        rows = rows or self.rows
        return pl.ds(pl.multiple_of(j * rows, rows), rows)

    def inward(self, source, j, slot):
        return pltpu.make_async_remote_copy(
            source.at[self.at(j)], self.land.at[slot, self.at(j)], self.send_sem.at[j], self.land_sem.at[slot, j],
            device_id={"tensor": self.inner}, device_id_type=MESH)

    def outward(self, j):
        return pltpu.make_async_remote_copy(
            self.land.at[1, self.at(j)], self.land.at[1, self.at(j)], self.out_sem.at[j], self.land_sem.at[1, j],
            device_id={"tensor": self.outer}, device_id_type=MESH)

    def put(self, c, value):
        rows = value.shape[0]
        self.x[self.at(c, rows), :] = value.astype(BF)
        self.push(c, rows)

    def push(self, c, rows):
        @pl.when(jnp.logical_not(self.has_outer))
        def _():
            for i in range(rows // self.rows):
                self.inward(self.x, c * (rows // self.rows) + i, self.slot).start()

    def add(self, j, source, slot):
        self.land[slot, self.at(j), :] = (
            source[self.at(j), :].astype(F32) + self.land[slot, self.at(j), :].astype(F32)
        ).astype(BF)

    def relay(self, j):
        @pl.when(self.has_outer)
        def _():
            self.inward(self.x, j, 0).wait_recv()
            self.add(j, self.x, 0)
            self.inward(self.land.at[0], j, self.slot).start()

    def meet(self, j):
        @pl.when(self.middle)
        def _():
            self.inward(self.x, j, 1).wait_recv()

            @pl.when(self.has_outer)
            def _():
                self.add(j, self.land.at[0], 1)
                self.outward(j).start()

            @pl.when(jnp.logical_not(self.has_outer))
            def _():
                self.add(j, self.x, 1)

    def total(self, c, rows):
        @pl.when(jnp.logical_not(self.middle))
        def _():
            for i in range(rows // self.rows):
                j = c * (rows // self.rows) + i
                self.inward(self.x, j, 1).wait_recv()

                @pl.when(self.has_outer)
                def _():
                    self.outward(j).start()

        return self.land[1, self.at(c, rows), :].astype(F32)

    def finish(self):
        @pl.when(self.has_outer)
        def _():
            @pl.loop(0, self.pieces)
            def _(j):
                self.inward(self.land.at[0], j, self.slot).wait_send()
                self.outward(j).wait_send()

        @pl.when(jnp.logical_not(self.has_outer))
        def _():
            @pl.loop(0, self.pieces)
            def _(j):
                self.inward(self.x, j, self.slot).wait_send()


class Spread(LineSum):
    @staticmethod
    def scratch(rows, width, pieces):
        return dict(
            land=pltpu.VMEM((2, rows, width), BF),
            send=pltpu.SemaphoreType.DMA((pieces,)),
            arrive=pltpu.SemaphoreType.DMA((2, pieces)),
            out=pltpu.SemaphoreType.DMA((pieces,)),
        )

    def start(self):
        @pl.when(self.middle)
        def _():
            @pl.loop(0, self.pieces)
            def _(j):
                self.land[1, self.at(j), :] = self.x[self.at(j), :]

                @pl.when(self.has_outer)
                def _():
                    self.outward(j).start()

    def finish(self):
        @pl.when(self.has_outer)
        def _():
            @pl.loop(0, self.pieces)
            def _(j):
                self.outward(j).wait_send()


class KeyValueSend:
    def __init__(self, refs, reach):
        self.held, self.window = refs.kv.held, refs.window
        self.copy_sem, self.send_sem, self.land_sem = refs.kv.copy, refs.kv.send, refs.kv.land
        self.chunks = self.copy_sem.shape[0]
        self.rows = self.held.shape[0] // self.chunks
        self.reach = reach
        self.place = lax.axis_index("seq")
        self.count = lax.axis_size("seq")

    @staticmethod
    def scratch(rows, width, chunks, reach):
        held = max(reach, 1)
        return dict(
            held=pltpu.VMEM((rows, width), BF),
            copy=pltpu.SemaphoreType.DMA((chunks,)),
            send=pltpu.SemaphoreType.DMA((held, chunks)),
            land=pltpu.SemaphoreType.DMA((held, chunks)),
        )

    def neighbours(self):
        found = []
        for back in range(1, self.reach + 1):
            found.append(({"seq": jnp.minimum(self.place + back, self.count - 1)}, self.place + back < self.count))
            found.append(({"seq": jnp.maximum(self.place - back, 0)}, self.place >= back))
        return found

    def at(self, c):
        return pl.ds(pl.multiple_of(c * self.rows, self.rows), self.rows)

    def own(self, c):
        return pltpu.make_async_copy(self.held.at[self.at(c)], self.window.at[self.reach, self.at(c)], self.copy_sem.at[c])

    def remote(self, back, c):
        return pltpu.make_async_remote_copy(
            self.held.at[self.at(c)], self.window.at[self.reach - back, self.at(c)],
            self.send_sem.at[back - 1, c], self.land_sem.at[back - 1, c],
            device_id={"seq": jnp.minimum(self.place + back, self.count - 1)}, device_id_type=MESH)

    def send(self, c):
        self.own(c).start()
        for back in range(1, self.reach + 1):

            @pl.when(self.place + back < self.count)
            def _():
                self.remote(back, c).start()

    def finish(self):
        @pl.loop(0, self.chunks)
        def _(c):
            self.own(c).wait()
            for back in range(1, self.reach + 1):

                @pl.when(self.place + back < self.count)
                def _():
                    self.remote(back, c).wait_send()

                @pl.when(self.place >= back)
                def _():
                    self.remote(back, c).wait_recv()


class KeyValueReturn:
    def __init__(self, refs, reach):
        self.prev, self.land = refs.d_prev, refs.kr.land
        self.send_sem, self.land_sem = refs.kr.send, refs.kr.arrive
        self.chunks = self.send_sem.shape[1]
        self.rows = self.land.shape[2] // self.chunks
        self.reach = reach
        self.place = lax.axis_index("seq")
        self.count = lax.axis_size("seq")

    @staticmethod
    def scratch(rows, width, chunks, reach):
        held = max(reach, 1)
        return dict(
            land=pltpu.VMEM((held, 2, rows, width), BF),
            send=pltpu.SemaphoreType.DMA((held, chunks)),
            arrive=pltpu.SemaphoreType.DMA((held, chunks)),
        )

    neighbours = KeyValueSend.neighbours
    at = KeyValueSend.at

    def copy(self, back, c):
        return pltpu.make_async_remote_copy(
            self.prev.at[self.reach - back, :, self.at(c)], self.land.at[back - 1, :, self.at(c)],
            self.send_sem.at[back - 1, c], self.land_sem.at[back - 1, c],
            device_id={"seq": jnp.maximum(self.place - back, 0)}, device_id_type=MESH)

    def start(self):
        for back in range(1, self.reach + 1):

            @pl.when(self.place >= back)
            def _():
                @pl.loop(0, self.chunks)
                def _(c):
                    self.copy(back, c).start()

    def add(self, own, c):
        for back in range(1, self.reach + 1):
            exists = self.place + back < self.count

            @pl.when(exists)
            def _():
                self.copy(back, c).wait_recv()

            own = own + jnp.where(exists, self.land[back - 1, :, self.at(c), :].astype(F32), 0.0)
        return own

    def finish(self):
        for back in range(1, self.reach + 1):

            @pl.when(self.place >= back)
            def _():
                @pl.loop(0, self.chunks)
                def _(c):
                    self.copy(back, c).wait_send()


def device_bit(axis):
    name, b = axis
    return lax.rem(lax.axis_index(name) // (1 << b), 2)


def device_partner(axis):
    name, b = axis
    return {name: lax.axis_index(name) + (1 - 2 * device_bit(axis)) * (1 << b)}


def bits_of(name):
    return lax.axis_size(name).bit_length() - 1


def block_axes():
    return [(name, b) for name in ("dp", "seq") for b in reversed(range(bits_of(name)))]


class Scatter:
    def __init__(self, refs, swapped):
        self.axes = block_axes()
        phases = len(self.axes)
        near = [k for k in range(phases) if self.axes[k][0] == "seq"][::-1]
        far = [k for k in range(phases) if self.axes[k][0] == "dp"]
        self.order = near + (far if swapped else far[::-1])
        self.buffer, self.lands = refs.held, refs.lands
        self.send_sem, self.land_sem = refs.send, refs.arrive

    @staticmethod
    def scratch(rows, width):
        phases = len(block_axes())
        return dict(
            held=pltpu.VMEM((2,) * phases + (rows, width), BF),
            lands=[pltpu.VMEM((2,) * (phases - k - 1) + (rows, width), BF) for k in range(phases)],
            send=pltpu.SemaphoreType.DMA((phases,)),
            arrive=pltpu.SemaphoreType.DMA((phases,)),
        )

    def neighbours(self):
        return [(device_partner(axis), True) for axis in self.axes]

    def put(self, block, columns, value):
        phases = len(self.axes)
        place = tuple(lax.rem(block // (1 << (phases - 1 - k)), 2) for k in range(phases))
        self.buffer[place + (slice(None), columns)] = value.astype(BF)

    def view(self, k, mine):
        index = [slice(None)] * len(self.axes)
        for earlier in self.order[:k]:
            index[earlier] = device_bit(self.axes[earlier])
        bit = device_bit(self.axes[self.order[k]])
        index[self.order[k]] = bit if mine else 1 - bit
        return tuple(index)

    def copy(self, k):
        return pltpu.make_async_remote_copy(
            self.buffer.at[self.view(k, False)], self.lands[k], self.send_sem.at[k], self.land_sem.at[k],
            device_id=device_partner(self.axes[self.order[k]]), device_id_type=MESH)

    def send(self, k):
        self.copy(k).start()

    def fold(self, k, store=None):
        self.copy(k).wait_recv()
        index = self.view(k, True)
        free = [i for i, v in enumerate(index) if isinstance(v, slice)]
        for j in range(1 << len(free)):
            place = [(j >> (len(free) - 1 - i)) & 1 for i in range(len(free))]
            here = list(index)
            for i, axis in enumerate(free):
                here[axis] = place[i]
            here = tuple(here)
            total = self.buffer[here].astype(F32) + self.lands[k][tuple(place)].astype(F32)
            if store is None:
                self.buffer[here] = total.astype(BF)
            else:
                store(total)

    def finish(self):
        for k in range(len(self.axes)):
            self.copy(k).wait_send()


class Butterfly:
    def __init__(self, refs):
        self.axes = [(name, b) for name in ("seq", "dp", "tensor") for b in range(bits_of(name))]
        self.held, self.land = refs.held, refs.land
        self.send_sem, self.land_sem = refs.send, refs.arrive

    @staticmethod
    def scratch(shape):
        phases = bits_of("seq") + bits_of("dp") + bits_of("tensor")
        return dict(
            held=pltpu.VMEM((phases + 1,) + shape, F32),
            land=pltpu.VMEM((phases,) + shape, F32),
            send=pltpu.SemaphoreType.DMA((phases,)),
            arrive=pltpu.SemaphoreType.DMA((phases,)),
        )

    def neighbours(self):
        return [(device_partner(axis), True) for axis in self.axes]

    def copy(self, k):
        return pltpu.make_async_remote_copy(
            self.held.at[k], self.land.at[k], self.send_sem.at[k], self.land_sem.at[k],
            device_id=device_partner(self.axes[k]), device_id_type=MESH)

    def put(self, value):
        self.held[0] = value
        self.copy(0).start()

    def fold(self, k):
        self.copy(k).wait_recv()
        self.held[k + 1] = self.held[k] + self.land[k]
        if k + 1 < len(self.axes):
            self.copy(k + 1).start()

    def total(self):
        return self.held[len(self.axes)]

    def finish(self):
        for k in range(len(self.axes)):
            self.copy(k).wait_send()


def norm_parts(value):
    inverse = lax.rsqrt(jnp.mean(value * value, -1, keepdims=True) + EPS)
    return value * inverse, inverse


def norm_back(grad, gain, hat, inverse):
    scaled = grad * gain
    inner = jnp.mean(scaled * hat, -1, keepdims=True)
    return inverse * (scaled - hat * inner)


def row_sums(value):
    return jnp.sum(value, 0, keepdims=True)


def heads_of(value):
    return [value[:, h * HEAD : (h + 1) * HEAD] for h in range(value.shape[1] // HEAD)]


def rope(value, cosine, signed_sine):
    return value * cosine + pltpu.roll(value, HEAD // 2, 1) * signed_sine


def rope_back(grad, cosine, signed_sine):
    return grad * cosine - pltpu.roll(grad, HEAD // 2, 1) * signed_sine


def project(r, hidden, kv, c):
    hat, _ = norm_parts(hidden)
    low = (hat * r.attn_gain[...].astype(F32)).astype(BF)
    r.attn_low[...] = low
    q_raw = dot(low, r.w_q[...])
    k_raw = dot(low, r.w_k[...])
    values = dot(low, r.w_v[...])
    r.q_raw[...] = q_raw
    r.k_raw[...] = k_raw
    cosine, sine = r.cosine[...], r.sine[...]

    def turned(raw, gain):
        return jnp.concatenate(
            [rope(norm_parts(u)[0] * gain, cosine, sine).astype(BF) for u in heads_of(raw)], 1)

    r.queries[...] = turned(q_raw, r.q_gain[...].astype(F32))
    kv.held[kv.at(c), :] = jnp.concatenate([turned(k_raw, r.k_gain[...].astype(F32)), values.astype(BF)], 1)
    kv.send(c)


def project_outs(rows, width, w, reach, when):
    q_width, k_width = w.w_q.shape[2], w.w_k.shape[2]
    return dict(
        attn_low=((rows, width), BF, when),
        q_raw=((rows, q_width), F32, when),
        k_raw=((rows, k_width), F32, when),
        queries=((rows, q_width), BF, when),
        window=((reach + 1, rows, k_width + w.w_v.shape[2]), BF, HBM),
    )


def project_ins(w, layer, tables, when, late):
    def weight(array):
        return (array, Late(layer)) if late else of_layer(array, layer)

    return dict(
        attn_gain=of_layer(w.attn_gain, layer),
        w_q=weight(w.w_q),
        w_k=weight(w.w_k),
        w_v=weight(w.w_v),
        q_gain=of_layer(w.q_gain, layer),
        k_gain=of_layer(w.k_gain, layer),
        cosine=(tables[0], when),
        sine=(tables[1], when),
    )


def mlp_gates(r, low):
    gate = dot(low, r.w_gate[...])
    up = dot(low, r.w_up[...])
    sigma = jax.nn.sigmoid(gate)
    return gate, up, sigma


def mlp_back(r, g_low, gate, up, sigma):
    d_act = dot(g_low, r.w_down[...], NT)
    d_gate = (d_act * up * sigma * (1.0 + gate * (1.0 - sigma))).astype(BF)
    d_up = (d_act * gate * sigma).astype(BF)
    return d_gate, d_up, dot(d_gate, r.w_gate[...], NT) + dot(d_up, r.w_up[...], NT)


def first_projection(hidden, w, tables, reach, chunks, collective_id):
    rows, width = hidden.shape
    when = (1, 0, chunks)
    kv_width = w.w_k.shape[2] + w.w_v.shape[2]

    def body(r, s):
        kv = KeyValueSend(r, reach)

        @pl.when(s == 0)
        def _():
            enter(kv.neighbours())

        project(r, r.hidden[...].astype(F32), kv, s)

        @pl.when(s == chunks - 1)
        def _():
            kv.finish()

    return step_kernel(
        first_projection, body, chunks,
        dict(hidden=(hidden, when)) | project_ins(w, 0, tables, when, False),
        project_outs(rows, width, w, reach, when),
        dict(kv=KeyValueSend.scratch(rows, kv_width, chunks, reach)), collective_id)


def between_forward(context, hidden, w, layer, tables, reach, chunks, collective_id):
    rows, width = hidden.shape
    kv_width = w.w_k.shape[2] + w.w_v.shape[2]
    ff = w.w_gate.shape[2]
    pieces = chunks * PIECES
    first, second, third = (PIECES, 0, chunks), (PIECES, 4, chunks), (PIECES, 8, chunks)
    steps = PIECES * (chunks - 1) + third[1] + 1
    chunk = rows // chunks

    def body(r, s):
        kv = KeyValueSend(r, reach)
        attn, mlp = LineSum(r.attn), LineSum(r.mlp)

        @pl.when(s == 0)
        def _():
            enter(attn.neighbours() + kv.neighbours())

        def send_attn(c):
            attn.put(c, dot(r.context[...], r.w_o[...]))

        def feed_forward(c):
            middle = r.hidden[...].astype(F32) + attn.total(c, chunk)
            r.hidden_mid[...] = middle
            r.mid_held[attn.at(c, chunk), :] = middle
            hat, _ = norm_parts(middle)
            low = (hat * r.mlp_gain[...].astype(F32)).astype(BF)
            r.mlp_low[...] = low
            gate, up, sigma = mlp_gates(r, low)
            r.gate[...] = gate
            r.up[...] = up
            act = (gate * sigma * up).astype(BF)
            r.act[...] = act
            mlp.put(c, dot(act, r.w_down[...]))

        def next_layer(c):
            hidden_next = r.mid_held[mlp.at(c, chunk), :] + mlp.total(c, chunk)
            r.hidden_next[...] = hidden_next
            project(r, hidden_next, kv, c)

        at_chunk(s, first, send_attn)
        at_chunk(s, (1, 1, pieces), attn.relay)
        at_chunk(s, (1, 2, pieces), attn.meet)
        r.arrived(second[1], *MLP_WEIGHTS)
        at_chunk(s, second, feed_forward)
        at_chunk(s, (1, 6, pieces), mlp.relay)
        at_chunk(s, (1, 7, pieces), mlp.meet)
        r.arrived(third[1], *QKV_WEIGHTS)
        at_chunk(s, third, next_layer)

        @pl.when(s == steps - 1)
        def _():
            attn.finish()
            mlp.finish()
            kv.finish()

    return step_kernel(
        between_forward, body, steps,
        dict(
            context=(context, first),
            w_o=of_layer(w.w_o, layer),
            hidden=(hidden, second),
            mlp_gain=of_layer(w.mlp_gain, layer),
            w_gate=(w.w_gate, Late(layer)),
            w_up=(w.w_up, Late(layer)),
            w_down=(w.w_down, Late(layer)),
        )
        | project_ins(w, layer + 1, tables, third, True),
        dict(
            hidden_mid=((rows, width), F32, second),
            mlp_low=((rows, width), BF, second),
            gate=((rows, ff), F32, second),
            up=((rows, ff), F32, second),
            act=((rows, ff), BF, second),
            hidden_next=((rows, width), F32, third),
        )
        | project_outs(rows, width, w, reach, third),
        dict(
            attn=LineSum.scratch(rows, width, pieces),
            mlp=LineSum.scratch(rows, width, pieces),
            kv=KeyValueSend.scratch(rows, kv_width, chunks, reach),
            mid_held=pltpu.VMEM((rows, width), F32),
        ),
        collective_id)


def turn_around(context, hidden, cotangent, w, layer, chunks, collective_id):
    rows, width = hidden.shape
    ff = w.w_gate.shape[2]
    pieces = chunks * PIECES
    first, second, third = (PIECES, 0, chunks), (PIECES, 6, chunks), (PIECES, 12, chunks)
    steps = PIECES * (chunks - 1) + third[1] + 1
    chunk = rows // chunks

    def body(r, s):
        attn, back = LineSum(r.attn), LineSum(r.back)

        @pl.when(s == 0)
        def _():
            enter(attn.neighbours())
            r.gain_grad[...] = jnp.zeros_like(r.gain_grad)

        def send_attn(c):
            attn.put(c, dot(r.context[...], r.w_o[...]))

        def feed_forward(c):
            middle = r.hidden[...] + attn.total(c, chunk)
            r.hidden_mid[...] = middle
            r.mid_held[attn.at(c, chunk), :] = middle
            hat, _ = norm_parts(middle)
            low = (hat * r.mlp_gain[...].astype(F32)).astype(BF)
            r.mlp_low[...] = low
            gate, up, sigma = mlp_gates(r, low)
            d_gate, d_up, part = mlp_back(r, r.cotangent[...], gate, up, sigma)
            back.put(c, part)
            r.d_gate[...] = d_gate
            r.d_up[...] = d_up
            act = (gate * sigma * up).astype(BF)
            r.act[...] = act
            r.mlp_part[...] = dot(act, r.w_down[...]).astype(BF)

        def middle_grad(c):
            hat, inverse = norm_parts(r.mid_held[back.at(c, chunk), :])
            d_in = back.total(c, chunk)
            r.gain_grad[0:1, :] += row_sums(d_in * hat)
            g_mid = r.cotangent_late[...].astype(F32) + norm_back(d_in, r.mlp_gain[...].astype(F32), hat, inverse)
            r.g_mid[...] = g_mid
            mid_low = g_mid.astype(BF)
            r.mid_low[...] = mid_low
            r.d_context[...] = dot(mid_low, r.w_o[...], NT).astype(BF)

        at_chunk(s, first, send_attn)
        at_chunk(s, (1, 3, pieces), attn.relay)
        at_chunk(s, (1, 4, pieces), attn.meet)
        r.arrived(second[1], *MLP_WEIGHTS)
        at_chunk(s, second, feed_forward)
        at_chunk(s, (1, 9, pieces), back.relay)
        at_chunk(s, (1, 10, pieces), back.meet)
        at_chunk(s, third, middle_grad)

        @pl.when(s == steps - 1)
        def _():
            attn.finish()
            back.finish()

    return step_kernel(
        turn_around, body, steps,
        dict(
            context=(context, first),
            w_o=of_layer(w.w_o, layer),
            hidden=(hidden, second),
            cotangent=(cotangent, second),
            cotangent_late=(cotangent, third),
            mlp_gain=of_layer(w.mlp_gain, layer),
            w_gate=(w.w_gate, Late(layer)),
            w_up=(w.w_up, Late(layer)),
            w_down=(w.w_down, Late(layer)),
        ),
        dict(
            mlp_low=((rows, width), BF, second),
            act=((rows, ff), BF, second),
            hidden_mid=((rows, width), F32, second),
            mlp_part=((rows, width), BF, second),
            d_gate=((rows, ff), BF, second),
            d_up=((rows, ff), BF, second),
            g_mid=((rows, width), F32, third),
            mid_low=((rows, width), BF, third),
            d_context=(context.shape, BF, third),
            gain_grad=((8, width), F32, WHOLE),
        ),
        dict(
            attn=LineSum.scratch(rows, width, pieces),
            back=LineSum.scratch(rows, width, pieces),
            mid_held=pltpu.VMEM((rows, width), F32),
        ),
        collective_id)


def attention_grads(r, back, line, c):
    cosine, sine = r.cosine[...], r.sine[...]
    both = back.add(r.d_own[...], c)

    def raw_back(grads, raws, gain):
        lows, gains = [], 0.0
        for grad, raw in zip(heads_of(grads), heads_of(raws)):
            grad = rope_back(grad, cosine, sine)
            hat, inverse = norm_parts(raw)
            gains = gains + row_sums(grad * hat)
            lows.append(norm_back(grad, gain, hat, inverse).astype(BF))
        return jnp.concatenate(lows, 1), gains

    d_q, q_gain = raw_back(r.d_q[...], r.q_raw[...], r.q_gain[...].astype(F32))
    d_k, k_gain = raw_back(both[0], r.k_raw[...], r.k_gain[...].astype(F32))
    d_v = both[1].astype(BF)
    r.head_gain[0:1, 0:HEAD] += q_gain
    r.head_gain[0:1, HEAD : 2 * HEAD] += k_gain
    r.d_held[line.at(c, d_q.shape[0]), :] = jnp.concatenate([d_q, d_k, d_v], 1)
    part = dot(d_q, r.w_q[...], NT) + dot(d_k, r.w_k[...], NT) + dot(d_v, r.w_v[...], NT)
    line.put(c, part)
    return part


class WeightGrads:
    def __init__(self, r, plan):
        self.r = r
        self.plan = plan
        self.slabs = plan.slabs[2]
        self.late = Scatter(r.sc_q, False), Scatter(r.sc_kv, True)
        self.early = Scatter(r.sc_a, False), Scatter(r.sc_b, True)
        self.blocks = 1 << len(block_axes())

    @staticmethod
    def scratch(rows, width, q_width, k_width, ff):
        per = width // (1 << len(block_axes()))
        return dict(
            sc_a=Scatter.scratch(per, ff + q_width),
            sc_b=Scatter.scratch(per, 2 * ff),
            sc_q=Scatter.scratch(per, q_width),
            sc_kv=Scatter.scratch(per, 2 * k_width),
            d_held=pltpu.VMEM((rows, q_width + 2 * k_width), BF),
        )

    def neighbours(self):
        return self.late[0].neighbours()

    def put(self, scatter, slab, columns, value):
        per = self.blocks // self.slabs
        rows = value.shape[0] // per
        for j in range(per):
            scatter.put(slab * per + j, columns, value[j * rows : (j + 1) * rows])

    def mlp_slab(self, slab):
        r = self.r
        ff = r.d_gate_all.shape[1]
        q_width = r.context_all.shape[1]
        mlp_low = r.mlp_low_slab[...]
        self.put(self.early[0], slab, slice(0, ff), dot(mlp_low, r.d_gate_all[...], TN))
        self.put(self.early[0], slab, slice(ff, ff + q_width), dot(r.mid_low_slab[...], r.context_all[...], TN))
        self.put(self.early[1], slab, slice(0, ff), dot(mlp_low, r.d_up_all[...], TN))
        self.put(self.early[1], slab, slice(ff, 2 * ff), dot(r.g_low_slab[...], r.act_all[...], TN))

    def qkv_slabs(self, begin, end):
        r = self.r
        slab_width = r.attn_low_all.shape[1] // self.slabs
        q_width = r.d_q.shape[1]

        @pl.loop(begin, end)
        def _(slab):
            columns = pl.ds(pl.multiple_of(slab * slab_width, slab_width), slab_width)
            value = dot(r.attn_low_all[:, columns], r.d_held[...], TN)
            self.put(self.late[0], slab, slice(None), value[:, :q_width])
            self.put(self.late[1], slab, slice(None), value[:, q_width:])

    def each(self, scatters, work):
        for scatter in scatters:
            work(scatter)

    def store(self):
        r = self.r
        last = len(block_axes()) - 1
        ff = r.d_gate_all.shape[1]
        k_width = r.k_raw.shape[1]

        def store_a(total):
            r.grad_gate[...] = total[:, :ff]
            r.grad_o[...] = total[:, ff:]

        def store_b(total):
            r.grad_up[...] = total[:, :ff]
            r.grad_down[...] = total[:, ff:]

        def store_q(total):
            r.grad_q[...] = total

        def store_kv(total):
            r.grad_k[...] = total[:, :k_width]
            r.grad_v[...] = total[:, k_width:]

        self.early[0].fold(last, store_a)
        self.early[1].fold(last, store_b)
        self.late[0].fold(last, store_q)
        self.late[1].fold(last, store_kv)

    def late_slabs(self, s):
        for i in range(2):
            self.r.arrived(self.plan.late_slabs[0], "attn_low_all") if i == 0 else None

            @pl.when(s == self.plan.late_slabs[i])
            def _():
                self.qkv_slabs(i * self.slabs // 2, (i + 1) * self.slabs // 2)

        @pl.when(s == self.plan.late_slabs[1])
        def _():
            self.each(self.late, lambda scatter: scatter.send(0))

    def run(self, s):
        rate, lag, count = self.plan.slabs
        self.r.arrived(lag, *GRAD_OPERANDS)
        at_chunk(s, self.plan.slabs, self.mlp_slab)

        @pl.when(s == lag + rate * (count - 1))
        def _():
            self.each(self.early, lambda scatter: scatter.send(0))

        for k in range(len(block_axes()) - 1):

            def move(scatter):
                scatter.fold(k)
                scatter.send(k + 1)

            @pl.when(s == self.plan.early(k))
            def _():
                self.each(self.early, move)

            @pl.when(s == self.plan.late(k))
            def _():
                self.each(self.late, move)

    def finish(self):
        self.each(self.early + self.late, lambda scatter: scatter.finish())


def slab_count(chunks):
    return min(4, max(1, chunks // 2))


def grads_ins(a, rows, width, when):
    slab = pl.BlockSpec((rows, width // when[2]), lambda s: (0, chunk_index(when, s)))
    return dict(
        mlp_low_slab=(a.mlp_low, slab),
        mid_low_slab=(a.mid_low, slab),
        g_low_slab=(a.g_low, slab),
        attn_low_all=(a.attn_low, Late()),
        d_gate_all=(a.d_gate, Late()),
        d_up_all=(a.d_up, Late()),
        context_all=(a.context, Late()),
        act_all=(a.act, Late()),
    )


def grads_outs(width, q_width, k_width, ff):
    per = width // (1 << len(block_axes()))
    return dict(
        grad_q=((per, q_width), F32, WHOLE),
        grad_k=((per, k_width), F32, WHOLE),
        grad_v=((per, k_width), F32, WHOLE),
        grad_o=((per, q_width), F32, WHOLE),
        grad_gate=((per, ff), F32, WHOLE),
        grad_up=((per, ff), F32, WHOLE),
        grad_down=((per, ff), F32, WHOLE),
    )


def attention_grads_ins(a, w, layer, tables, when):
    rows, k_width = a.k_raw.shape
    own = pl.BlockSpec((2, rows // when[2], k_width), lambda s: (0, chunk_index(when, s), 0))
    return dict(
        d_q=(a.d_q, when),
        d_own=(a.d_own, own),
        d_prev=(a.d_prev, HBM),
        q_raw=(a.q_raw, when),
        k_raw=(a.k_raw, when),
        cosine=(tables[0], when),
        sine=(tables[1], when),
        w_q=of_layer(w.w_q, layer),
        w_k=of_layer(w.w_k, layer),
        w_v=of_layer(w.w_v, layer),
        q_gain=of_layer(w.q_gain, layer),
        k_gain=of_layer(w.k_gain, layer),
        attn_gain=of_layer(w.attn_gain, layer),
    )


def between_backward(a, below, g_mid, w, layer, tables, reach, chunks, collective_id):
    rows, width = g_mid.shape
    q_width, k_width, ff = w.w_q.shape[2], w.w_k.shape[2], w.w_gate.shape[2]
    pieces = chunks * PIECES
    first, second, third = (PIECES, 0, chunks), (PIECES, 4, chunks), (PIECES, 10, chunks)
    steps = PIECES * (chunks - 1) + third[1] + 1
    chunk = rows // chunks
    after = PIECES * (chunks - 1) + 1
    plan = types.SimpleNamespace(
        slabs=(PIECES, 4, slab_count(chunks)),
        early=lambda k: min(after - 2 + 6 * k, steps - 2),
        late_slabs=(after, after + 2),
        late=lambda k: min(after + 5 + 2 * k, steps - 2),
    )

    def body(r, s):
        back = KeyValueReturn(r, reach)
        attn, mlp = LineSum(r.attn), LineSum(r.mlp)
        grads = WeightGrads(r, plan)

        @pl.when(s == 0)
        def _():
            enter(attn.neighbours() + back.neighbours() + grads.neighbours())
            back.start()
            r.gain_grad[...] = jnp.zeros_like(r.gain_grad)
            r.head_gain[...] = jnp.zeros_like(r.head_gain)

        def send_attn(c):
            attention_grads(r, back, attn, c)

        def feed_forward(c):
            hat, inverse = norm_parts(r.hidden[...])
            d_in = attn.total(c, chunk)
            r.gain_grad[0:1, :] += row_sums(d_in * hat)
            g = r.g_above[...] + norm_back(d_in, r.attn_gain[...].astype(F32), hat, inverse)
            r.g_held[lax.rem(c, 4)] = g
            g_low = g.astype(BF)
            r.g_low[...] = g_low
            gate = r.gate[...]
            d_gate, d_up, part = mlp_back(r, g_low, gate, r.up[...], jax.nn.sigmoid(gate))
            r.d_gate[...] = d_gate
            r.d_up[...] = d_up
            mlp.put(c, part)

        def middle_grad(c):
            hat, inverse = norm_parts(r.hidden_mid[...])
            d_in = mlp.total(c, chunk)
            r.gain_grad[1:2, :] += row_sums(d_in * hat)
            g_mid = r.g_held[lax.rem(c, 4)] + norm_back(d_in, r.mlp_gain[...].astype(F32), hat, inverse)
            r.g_mid[...] = g_mid
            mid_low = g_mid.astype(BF)
            r.mid_low[...] = mid_low
            r.d_context[...] = dot(mid_low, r.w_o[...], NT).astype(BF)

        at_chunk(s, first, send_attn)
        grads.late_slabs(s)
        at_chunk(s, (1, 2, pieces), attn.relay)
        at_chunk(s, (1, 3, pieces), attn.meet)
        r.arrived(second[1], *MLP_WEIGHTS)
        at_chunk(s, second, feed_forward)
        at_chunk(s, (1, 7, pieces), mlp.relay)
        at_chunk(s, (1, 8, pieces), mlp.meet)
        r.arrived(third[1], "w_o")
        at_chunk(s, third, middle_grad)
        grads.run(s)

        @pl.when(s == steps - 1)
        def _():
            grads.store()
            attn.finish()
            mlp.finish()
            back.finish()
            grads.finish()

    return step_kernel(
        between_backward, body, steps,
        attention_grads_ins(a, w, layer, tables, first)
        | grads_ins(a, rows, width, plan.slabs)
        | dict(
            hidden=(a.hidden, second),
            g_above=(g_mid, second),
            gate=(below.gate, second),
            up=(below.up, second),
            hidden_mid=(below.hidden_mid, third),
            mlp_gain=of_layer(w.mlp_gain, layer - 1),
            w_gate=(w.w_gate, Late(layer - 1)),
            w_up=(w.w_up, Late(layer - 1)),
            w_down=(w.w_down, Late(layer - 1)),
            w_o=(w.w_o, Late(layer - 1)),
        ),
        dict(
            g_low=((rows, width), BF, second),
            d_gate=((rows, ff), BF, second),
            d_up=((rows, ff), BF, second),
            g_mid=((rows, width), F32, third),
            mid_low=((rows, width), BF, third),
            d_context=((rows, q_width), BF, third),
            gain_grad=((8, width), F32, WHOLE),
            head_gain=((8, 2 * HEAD), F32, WHOLE),
        )
        | grads_outs(width, q_width, k_width, ff),
        dict(
            attn=LineSum.scratch(rows, width, pieces),
            mlp=LineSum.scratch(rows, width, pieces),
            kr=KeyValueReturn.scratch(rows, k_width, chunks, reach),
            **WeightGrads.scratch(rows, width, q_width, k_width, ff),
            g_held=pltpu.VMEM((4, rows // chunks, width), F32),
        ),
        collective_id)


def last_backward(a, top, top_total, g_mid, gain_parts, w, tables, reach, chunks, collective_id):
    rows, width = g_mid.shape
    q_width, k_width, ff = w.w_q.shape[2], w.w_k.shape[2], w.w_gate.shape[2]
    layer = 0
    pieces = chunks * PIECES
    pairs = max(1, chunks // 2)
    half = rows // 2
    half_pieces = pieces // 2
    first, second, third = (PIECES, 0, pairs), (PIECES, 8, chunks), (PIECES, 5, chunks)
    steps = PIECES * (chunks - 1) + second[1] + 1
    chunk = rows // chunks
    after = PIECES * pairs
    plan = types.SimpleNamespace(
        slabs=(PIECES, 1, slab_count(chunks)),
        early=lambda k: min(after + 1 + 4 * k, steps - 2),
        late_slabs=(after, after + 1),
        late=lambda k: min(after + 5 + 5 * k, steps - 2),
    )

    def body(r, s):
        back = KeyValueReturn(r, reach)
        attn, upper, lower = LineSum(r.attn), LineSum(r.upper, r.upper_part), Spread(r.lower, r.lower_total)
        grads = WeightGrads(r, plan)
        sums = Butterfly(r.sums)

        @pl.when(s == 0)
        def _():
            enter(attn.neighbours() + back.neighbours() + sums.neighbours())
            back.start()
            lower.start()
            r.head_gain[...] = jnp.zeros_like(r.head_gain)
            r.gain_held[...] = jnp.zeros_like(r.gain_held)

        def send_attn(c):
            part = attention_grads(r, back, attn, c)
            hat, _ = norm_parts(r.hidden[...].astype(F32))
            r.gain_held[...] += row_sums(part * hat)

        def give_output(c):
            @pl.when(c < chunks // 2)
            def _():
                r.output[...] = (r.hidden_mid[...] + lower.total(c, chunk)).astype(BF)

            @pl.when(c >= chunks // 2)
            def _():
                r.output[...] = (r.hidden_mid[...] + upper.total(c - chunks // 2, chunk)).astype(BF)

        def push_upper(j):
            upper.push(j, 2 * upper.rows)

        def give_input(c):
            hat, inverse = norm_parts(r.hidden_late[...].astype(F32))
            r.input_grad[...] = r.g_above[...] + norm_back(attn.total(c, chunk), r.attn_gain[...].astype(F32), hat, inverse)

        at_chunk(s, (1, 0, half_pieces // 2), push_upper)
        at_chunk(s, first, send_attn)
        grads.late_slabs(s)
        at_chunk(s, (1, 3, half_pieces), upper.relay)
        at_chunk(s, (1, 3, pieces), attn.relay)
        at_chunk(s, (1, 5, half_pieces), upper.meet)
        at_chunk(s, (1, 5, pieces), attn.meet)
        at_chunk(s, third, give_output)
        at_chunk(s, second, give_input)
        grads.run(s)

        @pl.when(s == after)
        def _():
            row = lax.broadcasted_iota(jnp.int32, (8, width), 0)
            pad = jnp.zeros((1, width - 2 * HEAD), F32)
            heads = jnp.concatenate([r.head_gain[0:1, :], pad], 1)
            packet = r.gain_parts[...] + jnp.where(row == 0, r.gain_held[...], 0.0) + jnp.where(row == 4, heads, 0.0)
            sums.put(packet)

        for k in range(len(sums.axes)):

            @pl.when(s == min(after + 2 + 2 * k, steps - 1))
            def _():
                sums.fold(k)

        @pl.when(s == steps - 1)
        def _():
            grads.store()
            r.gains[...] = sums.total()
            attn.finish()
            upper.finish()
            lower.finish()
            back.finish()
            grads.finish()
            sums.finish()

    return step_kernel(
        last_backward, body, steps,
        attention_grads_ins(a, w, layer, tables, first)
        | grads_ins(a, rows, width, plan.slabs)
        | dict(
            hidden=(a.hidden, first),
            hidden_late=(a.hidden, second),
            g_above=(g_mid, second),
            gain_parts=(gain_parts, WHOLE),
            upper_part=(top.mlp_part, pl.BlockSpec((half, width), lambda s: (1, 0), pipeline_mode=pl.Buffered(1))),
            lower_total=(top_total, WHOLE),
            hidden_mid=(top.hidden_mid, third),
        ),
        dict(
            input_grad=((rows, width), F32, second),
            output=((rows, width), BF, third),
            gains=((8, width), F32, WHOLE),
        )
        | grads_outs(width, q_width, k_width, ff),
        dict(
            attn=LineSum.scratch(rows, width, pieces),
            upper=Spread.scratch(half, width, half_pieces),
            lower=Spread.scratch(half, width, half_pieces),
            kr=KeyValueReturn.scratch(rows, k_width, pairs, reach),
            **WeightGrads.scratch(rows, width, q_width, k_width, ff),
            sums=Butterfly.scratch((8, width)),
            head_gain=pltpu.VMEM((8, 2 * HEAD), F32),
            gain_held=pltpu.VMEM((1, width), F32),
        ),
        collective_id)


def shifted(array, axis, by):
    devices = lax.axis_size(axis)
    pairs = [(i, i + by) for i in range(devices) if 0 <= i + by < devices]
    return lax.ppermute(array, axis, pairs)


def middle_sum(part):
    n = lax.axis_size("tensor")
    half = n // 2
    total = part
    for hop in range(half - 1):
        moved = lax.ppermute(total, "tensor", [(hop, hop + 1), (n - 1 - hop, n - 2 - hop)])
        total = (part.astype(F32) + moved.astype(F32)).astype(BF)
    if n > 1:
        moved = lax.ppermute(total, "tensor", [(half - 1, half), (half, half - 1)])
        total = (total.astype(F32) + moved.astype(F32)).astype(BF)
    return total


def rope_tables(places):
    halves = HEAD // 2
    frequency = THETA ** (-(jnp.arange(halves, dtype=F32) * 2.0) / HEAD)
    angle = places.astype(F32)[:, None] * frequency
    cosine, sine = jnp.cos(angle), jnp.sin(angle)
    return jnp.concatenate([cosine, cosine], -1), jnp.concatenate([-sine, sine], -1)


def lowest_keys(segments, reach):
    seqs_here, stretch = segments.shape
    place = lax.axis_index("seq")
    docs = [segments]
    for back in range(1, reach + 1):
        docs.insert(0, jnp.where(place >= back, shifted(segments, "seq", back), -1))
    docs = jnp.concatenate(docs, 1)
    start = jnp.sum((docs < 0).astype(jnp.int32), 1, keepdims=True)
    low = jnp.broadcast_to(start, segments.shape)
    for d in range(1, 4):
        start = jnp.sum((docs < d).astype(jnp.int32), 1, keepdims=True)
        low = jnp.where(segments >= d, start, low)
    index = jnp.arange(stretch, dtype=jnp.int32)
    return jnp.maximum(low, reach * stretch + index - (WINDOW - 1)).reshape(-1)


def per_device(
    tokens, cotangent, segments, positions, attn_gain, w_query, key_projection, value_projection, query_gain, key_gain,
    w_output, mlp_gain, w_gate, w_up, w_down,
):
    seqs_here, stretch, width = tokens.shape
    rows = seqs_here * stretch
    reach = min(lax.axis_size("seq") - 1, (WINDOW + stretch - 2) // stretch)
    chunks = rows // min(CHUNK, stretch)

    w = types.SimpleNamespace(
        attn_gain=attn_gain[:, None], mlp_gain=mlp_gain[:, None], q_gain=query_gain[:, None], k_gain=key_gain[:, None],
        w_q=w_query, w_k=key_projection, w_v=value_projection, w_o=w_output, w_gate=w_gate, w_up=w_up, w_down=w_down,
    )
    tables = rope_tables(positions.reshape(rows))
    low = lowest_keys(segments, reach)
    block = min(512, stretch)
    first = low[::block]
    tokens = tokens.reshape(rows, width)
    cotangent = cotangent.reshape(rows, width)

    a0 = first_projection(tokens, w, tables, reach, chunks, 1)
    a0.hidden = tokens
    a0.context, a0.lse = attn_fwd(a0.queries, a0.window, first, low, stretch, block, block)
    mid = between_forward(a0.context, tokens, w, 0, tables, reach, chunks, 2)
    a1 = types.SimpleNamespace(
        attn_low=mid.attn_low, q_raw=mid.q_raw, k_raw=mid.k_raw, queries=mid.queries, window=mid.window,
        hidden=mid.hidden_next)
    a1.context, a1.lse = attn_fwd(a1.queries, a1.window, first, low, stretch, block, block)
    turn = turn_around(a1.context, a1.hidden, cotangent, w, 1, chunks, 3)
    top_total = middle_sum(turn.mlp_part[: rows // 2])
    a1.mlp_low, a1.act, a1.d_gate, a1.d_up = turn.mlp_low, turn.act, turn.d_gate, turn.d_up
    a1.mid_low, a1.g_low = turn.mid_low, cotangent
    a1.d_q, a1.d_own, a1.d_prev = attn_bwd(
        a1.queries, turn.d_context, a1.context, a1.window, first, low, a1.lse, stretch, block, block)
    down = between_backward(a1, mid, turn.g_mid, w, 1, tables, reach, chunks, 4)
    a0.mlp_low, a0.act, a0.d_gate, a0.d_up = mid.mlp_low, mid.act, down.d_gate, down.d_up
    a0.mid_low, a0.g_low = down.mid_low, down.g_low
    a0.d_q, a0.d_own, a0.d_prev = attn_bwd(
        a0.queries, down.d_context, a0.context, a0.window, first, low, a0.lse, stretch, block, block)

    once = lax.axis_index("tensor") == 0
    shared = jnp.concatenate([
        jnp.zeros((1, width), F32), down.gain_grad[0:1], down.gain_grad[1:2], turn.gain_grad[0:1],
        jnp.zeros((4, width), F32)], 0)
    heads = jnp.pad(down.head_gain[0:1], ((4, 3), (2 * HEAD, width - 4 * HEAD)))
    gain_parts = jnp.where(once, shared, 0.0) + heads
    end = last_backward(a0, turn, top_total, down.g_mid, gain_parts, w, tables, reach, chunks, 5)
    gains = end.gains

    def both(pick, turned=False):
        lower, upper = pick(end), pick(down)
        return jnp.stack([lower.T, upper.T] if turned else [lower, upper])

    head_rows = gains[4, : 4 * HEAD].reshape(2, 2, HEAD)
    shape = (seqs_here, stretch, width)
    return (
        end.output.reshape(shape), end.input_grad.reshape(shape), gains[0:2], both(lambda k: k.grad_q), both(lambda k: k.grad_k),
        both(lambda k: k.grad_v), head_rows[:, 0], head_rows[:, 1], both(lambda k: k.grad_o, True), gains[2:4], both(lambda k: k.grad_gate),
        both(lambda k: k.grad_up), both(lambda k: k.grad_down, True),
    )


def solution(mesh):
    placed = (
        P("dp", "seq", None), P("dp", "seq", None), P("dp", "seq"), P("dp", "seq"), P(), P(None, None, "tensor"),
        P(None, None, "tensor"), P(None, None, "tensor"), P(), P(), P(None, "tensor", None), P(),
        P(None, None, "tensor"), P(None, None, "tensor"), P(None, "tensor", None),
    )
    by_rows = P(None, ("dp", "seq"), "tensor")
    by_columns = P(None, "tensor", ("dp", "seq"))
    return jax.shard_map(
        per_device,
        mesh=mesh,
        in_specs=placed,
        out_specs=(
            P("dp", "seq", None), P("dp", "seq", None), P(), by_rows, by_rows, by_rows, P(), P(), by_columns, P(),
            by_rows, by_rows, by_columns,
        ),
        check_vma=False,
    )
```

time: 1660 us -> 589 us (0.35)
  waiting for transfers between devices: 968 us -> 0.01 us
  Pallas kernels: 0 us -> 535 us
  matrix products: 301 us -> 0 us
  other arithmetic: 226 us -> 20.2 us
  local copies, waits for them, and re-layouts: 87.6 us -> 17.5 us
  blocking collectives: 38 us -> 0 us
    psum x7 -> x0, waiting for transfers between devices: 634 us -> none  [the longest x2 242 us: forward_layer(): lax.psum(mlp_part.astype(jnp.bfloat16), 'tensor').astype(jnp.float32)]
    pallas_call x0 -> x9, Pallas kernels: none -> 535 us  [the longest x5 477 us: step_kernel(): pl.pallas_call(kernel, grid=(steps,), in_specs=[spec(a.shape, w, True) fo...]
    reduce_scatter x14 -> x0, waiting for transfers between devices: 332 us -> none  [the longest x2 76.1 us: reduce_grads(): lax.psum_scatter(grad_q.astype(jnp.bfloat16), ('dp', 'seq'), scatter_dime...]
    dot_general x54 -> x0, matrix products: 301 us -> none  [the longest x2 44.2 us: backward_layer(): jnp.einsum('sqhgd,skhd->shgqk', d_context, value_window, preferred_elemen...]
    reduce_sum x19 -> x1, other arithmetic: 73.4 us -> 0.7 us  [lowest_keys(): start = jnp.sum((docs < d).astype(jnp.int32), 1, keepdims=True)]
    another operation x21 -> x8, other arithmetic: 78.3 us -> 7.77 us  [the longest x7 5.17 us: both(): return jnp.stack([lower.T, upper.T] if turned else [lower, upper])]
    unnamed x338 -> x46, local copies, waits for them, and re-layouts: 45.3 us -> 7.18 us
    psum x2 -> x0, blocking collectives: 36 us -> none  [the longest x1 24 us: reduce_grads(): lax.psum((gain_a, gain_q, gain_k, gain_m), ('dp', 'seq'))]
  transfers between devices with their start and end apart: 25 -> 3, of which waited for: 18 -> 0; matrix products, arithmetic and copies ran while one was open for 16% -> 2% of each run, Pallas kernels for 0% -> 31%
where the time goes in v2:
time: 589 us; the launch traced here: 580 us
  Pallas kernels  535 us (91%)
  other arithmetic  20.2 us (3%)
  local copies, waits for them, and re-layouts  17.5 us (3%)
  starting transfers between devices  6.27 us (1%)
    pallas_call x5, Pallas kernels, step_kernel(): pl.pallas_call(kernel, grid=(steps,), in_specs=[spec(a.shape, w, True) fo...  477 us
    pallas_call x2, Pallas kernels, attn_bwd(): pl.pallas_call(functools.partial(attn_bwd_kernel, qb, kb, reach * stretch...  34 us
    pallas_call x2, Pallas kernels, attn_fwd(): pl.pallas_call(functools.partial(attn_fwd_kernel, qb, kb, reach * stretch...  23.6 us
  transfers between devices with their start and end apart: 3, of which 0 were waited for; matrix products, arithmetic and copies ran while one was open for 2% of the time, Pallas kernels for 31%

profile of v2, /device:TPU:0, one launch (start us, length us, event | category | flops | bytes accessed | tf_op | source)
XLA Modules:
  0.0 579.9 jit_solution(14065840274607273675)
XLA Ops:
  0.6 2.4 collective-permute-start
  3.0 0.7 convert_element_type.78
  3.7 0.0 copy-start.17
  3.7 1.9 fusion
  5.6 1.3 pad_maximum_fusion.3
  7.0 0.1 pad.22.clone
  7.0 0.0 copy-done.19
  7.0 0.6 copy.33.refs_5_.refs_11_.refs_10_
  7.6 0.0 copy-done.20
  7.6 0.6 copy.34.refs_6_.refs_12_.refs_11_
  8.2 0.0 copy-done.16
  8.2 0.6 copy.32.refs_1_.refs_7_.refs_12_
  8.8 0.0 copy-done.17
  8.8 0.6 copy.36.refs_3_.refs_5_.refs_26_
  9.4 11.9 %first_projection.1 = (bf16[1024,1024]{1,0:T(8,128)(2,1)}, f32[1024,512]{1,0:T(8,128)}, f32[1024,256]{1,0:T(8,128)}, bf16[1024,512]{1,0:T(8,128)(2,1)}, bf16[2,1024,512]{2,1,0:T(8,128)(2,1)}) custom-call(bf16[1024,1024]{1,0:T(8,128)(2,1)} %bitcast.42, bf16[2,1,1024]{2,1,0:T(2,128)(2,1)} %copy.32.refs_1_.refs_7_.refs_12_, bf16[2,1024,512]{2,1,0:T(8,128)(2,1)} %refs_7_.5, ...), custom_call_target="tpu_custom_call" | custom-call | tf_op jit(solution)/shard_map/first_projection/pallas_call | solution.py:269
  21.3 0.0 collective-permute-done
  21.4 0.0 copy-done.15
  21.4 0.7 fusion.2
  22.1 2.6 fusion.6.low_ref
  24.7 0.0 copy-start.18
  24.7 2.6 fusion.9
  27.3 0.6 slice.32.first_ref
  27.9 1.0 copy.35.low_ref
  28.9 11.8 %attn_fwd.2 = (bf16[1024,512]{1,0:T(8,128)(2,1)}, f32[2,2,1024]{2,1,0:T(2,128)}) custom-call(s32[2]{0:T(128)} %slice.32.first_ref, s32[1024,1]{1,0:T(8,128)} %copy.35.low_ref, bf16[1024,512]{1,0:T(8,128)(2,1)} %get-tuple-element.74.q_ref, bf16[2,1024,512]{2,1,0:T(8,128)(2,1)} %get-tuple-element.75.k_ref.v_ref, ...), custom_call_target="tpu_custom_call" | custom-call | tf_op jit(solution)/shard_map/attn_fwd/pallas_call | solution.py:76
  40.7 0.0 copy-done.18
  40.7 118.5 %between_forward.1 = (f32[1024,1024]{1,0:T(8,128)}, bf16[1024,1024]{1,0:T(8,128)(2,1)}, f32[1024,768]{1,0:T(8,128)}, f32[1024,768]{1,0:T(8,128)}, bf16[1024,768]...) custom-call(bf16[1024,512]{1,0:T(8,128)(2,1)} %get-tuple-element.77., ...), custom_call_target="tpu_custom_call" | custom-call | tf_op jit(solution)/shard_map/between_forward/pallas_call | solution.py:269
  159.3 11.8 %attn_fwd.3 = (bf16[1024,512]{1,0:T(8,128)(2,1)}, f32[2,2,1024]{2,1,0:T(2,128)}) custom-call(s32[2]{0:T(128)} %slice.32.first_ref, s32[1024,1]{1,0:T(8,128)} %copy.35.low_ref, bf16[1024,512]{1,0:T(8,128)(2,1)} %get-tuple-element.78.q_ref, bf16[2,1024,512]{2,1,0:T(8,128)(2,1)} %get-tuple-element.79.k_ref.v_ref, ...), custom_call_target="tpu_custom_call" | custom-call | tf_op jit(solution)/shard_map/attn_fwd/pallas_call | solution.py:76
  171.1 112.3 %turn_around.1 = (bf16[1024,1024]{1,0:T(8,128)(2,1)}, bf16[1024,768]{1,0:T(8,128)(2,1)}, f32[1024,1024]{1,0:T(8,128)}, bf16[1024,1024]{1,0:T(8,128)(2,1)}, bf16[...) custom-call(bf16[1024,512]{1,0:T(8,128)(2,1)} %get-tuple-element.81., ...), custom_call_target="tpu_custom_call" | custom-call | tf_op jit(solution)/shard_map/turn_around/pallas_call | solution.py:269
  283.3 1.3 slice.36
  284.6 2.3 collective-permute-start.1
  286.9 17.0 %attn_bwd.2 = (f32[1024,512]{1,0:T(8,128)}, f32[2,1024,256]{2,1,0:T(8,128)}, bf16[1,2,1024,256]{3,2,1,0:T(8,128)(2,1)}) custom-call(s32[2]{0:T(128)} %slice.32.first_ref, s32[1,1024]{1,0:T(1,128)} %copy-done.18, f32[2,2,1024]{2,1,0:T(2,128)} %get-tuple-element.80.lse_ref, bf16[1024,512]{1,0:T(8,128)(2,1)} %get-tuple-element.78.q_ref, ...), custom_call_target="tpu_custom_call" | custom-call | flops 30000001024 | bytes 12582912 | tf_op jit(solution)/shard_map/attn_bwd/pallas_call | solution.py:165
  303.9 131.1 %between_backward.1 = (bf16[1024,1024]{1,0:T(8,128)(2,1)}, bf16[1024,768]{1,0:T(8,128)(2,1)}, bf16[1024,768]{1,0:T(8,128)(2,1)}, f32[1024,1024]{1,0:T(8,128)}, b...) custom-call(f32[1024,512]{1,0:T(8,128)} %get-tuple-element.84.refs_0, ...), custom_call_target="tpu_custom_call" | custom-call | tf_op jit(solution)/shard_map/between_backward/pallas_call | solution.py:269
  435.0 0.0 collective-permute-done.1
  435.0 1.9 add_convert_fusion.1
  437.0 1.6 collective-permute-start.2
  438.6 17.0 %attn_bwd.3 = (f32[1024,512]{1,0:T(8,128)}, f32[2,1024,256]{2,1,0:T(8,128)}, bf16[1,2,1024,256]{3,2,1,0:T(8,128)(2,1)}) custom-call(s32[2]{0:T(128)} %slice.32.first_ref, s32[1,1024]{1,0:T(1,128)} %copy-done.18, f32[2,2,1024]{2,1,0:T(2,128)} %get-tuple-element.76.lse_ref, bf16[1024,512]{1,0:T(8,128)(2,1)} %get-tuple-element.74.q_ref, ...), custom_call_target="tpu_custom_call" | custom-call | flops 30000001024 | bytes 12582912 | tf_op jit(solution)/shard_map/attn_bwd/pallas_call | solution.py:165
  455.7 0.8 slice.34
  456.4 0.7 slice.35
  457.1 0.8 slice.33
  457.9 0.7 fusion.1.refs_24_
  458.6 0.0 collective-permute-done.2
  458.6 2.6 add_convert_fusion.refs_26_
  461.2 103.1 %last_backward.1 = (f32[1024,1024]{1,0:T(8,128)}, bf16[1024,1024]{1,0:T(8,128)(2,1)}, f32[8,1024]{1,0:T(8,128)}, f32[128,512]{1,0:T(8,128)}, f32[128,256]{1,0:T(...) custom-call(f32[1024,512]{1,0:T(8,128)} %get-tuple-element.100.refs_, ...), custom_call_target="tpu_custom_call" | custom-call | tf_op jit(solution)/shard_map/last_backward/pallas_call | solution.py:269
  564.3 0.0 copy-start.4
  564.3 0.0 copy-start.7
  564.3 0.8 slice.38
  565.1 1.4 fusion.7
  566.5 0.6 fusion.8
  567.1 0.0 copy-done.9
  567.1 1.0 pad_maximum_fusion.6
  568.1 1.0 copy.51
  569.1 0.0 copy-start.8
  569.1 0.0 copy-start.10
  569.1 0.1 pad_maximum_fusion.2
  569.2 1.1 copy.52
  570.4 0.7 pad_maximum_fusion.7
  571.1 0.0 copy-done.13
  571.1 0.7 pad_maximum_fusion.8
  571.8 0.8 pad_maximum_fusion.5
  572.7 0.9 pad_maximum_fusion
  573.6 0.9 pad_maximum_fusion.1
  574.5 1.3 copy.57
  575.9 1.6 copy-done
  577.5 2.0 copy.58
  (31 shorter events, 0.1 us)
Async XLA Ops:
  0.6 20.7 %collective-permute-start = (s32[1,1024]{1,0:T(1,128)}, s32[1,1024]{1,0:T(1,128)S(1)}, u32[]{:S(2)}, u32[]{:S(2)}) collective-permute-start(s32[1,1024]{1,0:T(1,128)} %param.17), channel_id=1, source_target_pairs={{0,4},{1,5},{2,6},{3,7},{8,12},{9,13},{10,14},{11,15},{16,20},{17,... | collective-permute-start | bytes 12296 | tf_op jit(solution)/shard_map/ppermute | solution.py:1415
  3.7 3.3 copy-start.19
  3.7 3.9 copy-start.20
  3.7 4.5 copy-start.16
  3.7 5.1 copy-start.17
  9.4 12.0 %copy-start.15 = (s32[1,1024]{1,0:T(1,128)S(1)}, s32[1,1024]{1,0:T(1,128)}, u32[]{:S(2)}) copy-start(s32[1,1024]{1,0:T(1,128)} %param.17) | copy-start | bytes 12292
  24.7 16.0 %copy-start.18 = (s32[1,1024]{1,0:T(1,128)}, s32[1,1024]{1,0:T(1,128)S(1)}, u32[]{:S(2)}) copy-start(s32[1,1024]{1,0:T(1,128)S(1)} %fusion.6.low_ref) | copy-start | bytes 12292
  284.6 150.4 %collective-permute-start.1 = (bf16[512,1024]{1,0:T(8,128)(2,1)S(1)}, bf16[512,1024]{1,0:T(8,128)(2,1)}, u32[]{:S(2)}, u32[]{:S(2)}) collective-permute-start(bf16[512,1024]{1,0:T(8,128)(2,1)S(1)} %slice.36), channel_id=1, source_target_pairs={{0,1},{3,2},{4,5},{7,6},{8,9},{11,10},{12,13},{15,14},{16,17},{19,... | collective-permute-start | bytes 3145736 | tf_op jit(solution)/shard_map/ppermute | solution.py:1423
  437.0 21.6 %collective-permute-start.2 = (bf16[512,1024]{1,0:T(8,128)(2,1)S(1)}, bf16[512,1024]{1,0:T(8,128)(2,1)}, u32[]{:S(2)}, u32[]{:S(2)}) collective-permute-start(bf16[512,1024]{1,0:T(8,128)(2,1)S(1)} %add_convert_fusion.1), channel_id=1, source_target_pairs={{1,2},{2,1},{5,6},{6,5},{9,10},{10,9},{13,14},{14,13},{17,18},{18,... | collective-permute-start | bytes 3145736 | tf_op jit(solution)/shard_map/ppermute | solution.py:1426
  461.2 105.9 %copy-start.9 = (f32[128,512]{1,0:T(8,128)S(1)}, f32[128,512]{1,0:T(8,128)}, u32[]{:S(2)}) copy-start(f32[128,512]{1,0:T(8,128)} %get-tuple-element.128) | copy-start | bytes 786436
  564.3 4.8 copy-start.4
  564.3 4.8 copy-start.7
  568.1 2.3 copy-start.12
  568.1 2.3 copy-start.14
  569.1 2.0 copy-start.11
  569.1 2.0 copy-start.13
  569.1 2.7 copy-start.8
  569.1 2.7 copy-start.10
  569.2 3.5 copy-start.3
  569.2 3.5 copy-start.6
  570.4 3.2 copy-start.2
  570.4 3.2 copy-start.5
  571.8 2.7 copy-start.1
  574.5 2.9 copy-start

commit v3 on v2

--- a/solution.py
+++ b/solution.py
@@ -30,79 +30,16 @@
     return lax.dot_general(a, b, dims, preferred_element_type=F32)
 
 
-def attn_fwd_kernel(qb, kb, offset, stretch, first_ref, low_ref, q_ref, k_ref, v_ref, o_ref, lse_ref):
+def attn_bwd_kernel(offset, low_ref, lse_ref, q_ref, do_ref, o_ref, k_ref, v_ref, dq_ref, own_ref, prev_ref,
+                    dk_ref, dv_ref):
     step = pl.program_id(2)
+    qb = q_ref.shape[0]
     heads = q_ref.shape[1] // HEAD
+    span = k_ref.shape[0]
+    length = min(WINDOW + qb, span)
     q_start = step * qb + offset
-    queries = [q_ref[:, h * HEAD : (h + 1) * HEAD] for h in range(heads)]
-    q_index = q_start + lax.broadcasted_iota(jnp.int32, (qb, 1), 0)
-    low = low_ref[...]
-
-    def block(kk, carry):
-        start = kk * kb
-        place = (start // stretch, pl.ds(pl.multiple_of(lax.rem(start, stretch), kb), kb))
-        keys = k_ref[place]
-        values = v_ref[place]
-        key_index = start + lax.broadcasted_iota(jnp.int32, (qb, kb), 1)
-        mask = (key_index >= low) & (key_index <= q_index)
-        out = []
-        for h in range(heads):
-            acc, total = carry[h]
-            s = dot(queries[h], keys, NT) * (SCALE * LOG2E)
-            p = jnp.where(mask, jnp.exp2(s), 0.0)
-            part = p[:, :HEAD]
-            for c in range(1, kb // HEAD):
-                part = part + p[:, c * HEAD : (c + 1) * HEAD]
-            out.append((acc + dot(p.astype(BF), values), total + part))
-        return tuple(out)
-
-    zero = jnp.zeros((qb, HEAD), F32)
-    first = first_ref[pl.program_id(0) * pl.num_programs(2) + step] // kb
-    last = (q_start + qb - 1) // kb + 1
-    result = lax.fori_loop(first, last, block, tuple((zero, zero) for _ in range(heads)))
-    for h in range(heads):
-        acc, total = result[h]
-        o_ref[:, h * HEAD : (h + 1) * HEAD] = (acc / jnp.sum(total, 1, keepdims=True)).astype(BF)
-        lse_ref[h : h + 1, :] = jnp.log2(jnp.sum(total.T, 0, keepdims=True))
-
-
-def attn_fwd(q, window, first, low, stretch, qb=512, kb=512):
-    rows = q.shape[0]
-    reach = window.shape[0] - 1
-    kv_heads = window.shape[2] // (2 * HEAD)
-    width = q.shape[1] // kv_heads
-    group = width // HEAD
-    steps = stretch // qb
-    return pl.pallas_call(
-        functools.partial(attn_fwd_kernel, qb, kb, reach * stretch, stretch),
-        grid_spec=pltpu.PrefetchScalarGridSpec(
-            num_scalar_prefetch=1,
-            grid=(rows // stretch, kv_heads, steps),
-            in_specs=[
-                pl.BlockSpec((qb, 1), lambda s, g, i, f: (s * steps + i, 0)),
-                pl.BlockSpec((qb, width), lambda s, g, i, f: (s * steps + i, g)),
-                pl.BlockSpec((reach + 1, stretch, HEAD), lambda s, g, i, f: (0, s, g)),
-                pl.BlockSpec((reach + 1, stretch, HEAD), lambda s, g, i, f: (0, s, kv_heads + g)),
-            ],
-            out_specs=[
-                pl.BlockSpec((qb, width), lambda s, g, i, f: (s * steps + i, g)),
-                pl.BlockSpec((None, group, qb), lambda s, g, i, f: (g, 0, s * steps + i)),
-            ],
-        ),
-        out_shape=[
-            jax.ShapeDtypeStruct(q.shape, BF),
-            jax.ShapeDtypeStruct((kv_heads, group, rows), F32),
-        ],
-        name=attn_fwd.__name__,
-        compiler_params=pltpu.CompilerParams(vmem_limit_bytes=62 << 20),
-    )(first, low[:, None], q, window, window)
-
-
-def attn_bwd_kernel(qb, kb, offset, stretch, first_ref, low_ref, lse_ref, q_ref, do_ref, o_ref, k_ref, v_ref,
-                    dq_ref, own_ref, prev_ref, dk_ref, dv_ref):
-    step = pl.program_id(2)
-    heads = q_ref.shape[1] // HEAD
-    q_start = step * qb + offset
+    start = jnp.clip(q_start + qb - length, 0, span - length)
+    here = pl.ds(pl.multiple_of(start, HEAD), length)
 
     @pl.when(step == 0)
     def _():
@@ -114,84 +51,72 @@
 
     queries = stack(q_ref)
     d_out = stack(do_ref)
-    q_index = q_start + lax.broadcasted_iota(jnp.int32, (1, qb), 1)
-    low = low_ref[...]
     lse = jnp.concatenate([lse_ref[h : h + 1, :] for h in range(heads)], 1)
     product = d_out.astype(F32) * stack(o_ref).astype(F32)
     delta = jnp.sum(product.T, 0, keepdims=True)
-
-    def block(kk, dq):
-        start = kk * kb
-        place = (start // stretch, pl.ds(pl.multiple_of(lax.rem(start, stretch), kb), kb))
-        here = pl.ds(pl.multiple_of(start, kb), kb)
-        keys = k_ref[place]
-        values = v_ref[place]
-        key_index = start + lax.broadcasted_iota(jnp.int32, (kb, qb), 0)
-        mask = (key_index >= low) & (key_index <= q_index)
-        mask = jnp.concatenate([mask] * heads, 1)
-        s = dot(keys, queries, NT) * (SCALE * LOG2E) - lse
-        p = jnp.where(mask, jnp.exp2(s), 0.0)
-        dp = dot(values, d_out, NT)
-        ds = (p * (dp - delta)).astype(BF)
-        dv_ref[here, :] += dot(p.astype(BF), d_out)
-        dk_ref[here, :] += dot(ds, queries)
-        return dq + dot(ds, keys, TN)
-
-    first = first_ref[pl.program_id(0) * pl.num_programs(2) + step] // kb
-    last = (q_start + qb - 1) // kb + 1
-    dq = lax.fori_loop(first, last, block, jnp.zeros((heads * qb, HEAD), F32))
+    keys = k_ref[here, :]
+    values = v_ref[here, :]
+    key_index = start + lax.broadcasted_iota(jnp.int32, (length, qb), 0)
+    q_index = q_start + lax.broadcasted_iota(jnp.int32, (1, qb), 1)
+    mask = (key_index >= low_ref[...]) & (key_index <= q_index)
+    mask = jnp.concatenate([mask] * heads, 1)
+    s = dot(keys, queries, NT) * (SCALE * LOG2E) - lse
+    p = jnp.where(mask, jnp.exp2(s), 0.0)
+    ds = (p * (dot(values, d_out, NT) - delta)).astype(BF)
+    dv_ref[here, :] += dot(p.astype(BF), d_out)
+    dk_ref[here, :] += dot(ds, queries)
+    dq = dot(ds, keys, TN) * SCALE
     for h in range(heads):
-        dq_ref[:, h * HEAD : (h + 1) * HEAD] = dq[h * qb : (h + 1) * qb] * SCALE
+        dq_ref[:, h * HEAD : (h + 1) * HEAD] = dq[h * qb : (h + 1) * qb]
 
     @pl.when(step == pl.num_programs(2) - 1)
     def _():
         own_ref[0] = dk_ref[offset:, :] * SCALE
         own_ref[1] = dv_ref[offset:, :]
+        stretch = own_ref.shape[1]
         for j in range(offset // stretch):
             prev_ref[j, 0] = (dk_ref[j * stretch : (j + 1) * stretch, :] * SCALE).astype(BF)
             prev_ref[j, 1] = dv_ref[j * stretch : (j + 1) * stretch, :].astype(BF)
 
 
-def attn_bwd(q, d_out, o, window, first, low, lse, stretch, qb=512, kb=512):
+def attn_bwd(q, d_out, o, window, low, lse, stretch):
     rows = q.shape[0]
-    reach = window.shape[0] - 1
-    kv_heads = window.shape[2] // (2 * HEAD)
+    kv_heads = window.shape[1] // (2 * HEAD)
     width = q.shape[1] // kv_heads
     group = width // HEAD
+    qb = min(2 * CHUNK, stretch)
     steps = stretch // qb
-    span = (reach + 1) * stretch
+    span = window.shape[0] // (rows // stretch)
+    reach = span // stretch - 1
     held = max(reach, 1)
-    row_spec = pl.BlockSpec((qb, width), lambda s, g, i, f: (s * steps + i, g))
+    row_spec = pl.BlockSpec((qb, width), lambda s, g, i: (s * steps + i, g))
     return pl.pallas_call(
-        functools.partial(attn_bwd_kernel, qb, kb, reach * stretch, stretch),
-        grid_spec=pltpu.PrefetchScalarGridSpec(
-            num_scalar_prefetch=1,
-            grid=(rows // stretch, kv_heads, steps),
-            in_specs=[
-                pl.BlockSpec((1, qb), lambda s, g, i, f: (0, s * steps + i)),
-                pl.BlockSpec((None, group, qb), lambda s, g, i, f: (g, 0, s * steps + i)),
-                row_spec,
-                row_spec,
-                row_spec,
-                pl.BlockSpec((reach + 1, stretch, HEAD), lambda s, g, i, f: (0, s, g)),
-                pl.BlockSpec((reach + 1, stretch, HEAD), lambda s, g, i, f: (0, s, kv_heads + g)),
-            ],
-            out_specs=[
-                row_spec,
-                pl.BlockSpec((2, stretch, HEAD), lambda s, g, i, f: (0, s, g)),
-                pl.BlockSpec((held, 2, stretch, HEAD), lambda s, g, i, f: (0, 0, s, g)),
-            ],
-            scratch_shapes=[pltpu.VMEM((span, HEAD), F32), pltpu.VMEM((span, HEAD), F32)],
-        ),
+        functools.partial(attn_bwd_kernel, reach * stretch),
+        grid=(rows // stretch, kv_heads, steps),
+        in_specs=[
+            pl.BlockSpec((1, qb), lambda s, g, i: (0, s * steps + i)),
+            pl.BlockSpec((None, group, qb), lambda s, g, i: (g, 0, s * steps + i)),
+            row_spec,
+            row_spec,
+            row_spec,
+            pl.BlockSpec((span, HEAD), lambda s, g, i: (s, g)),
+            pl.BlockSpec((span, HEAD), lambda s, g, i: (s, kv_heads + g)),
+        ],
+        out_specs=[
+            row_spec,
+            pl.BlockSpec((2, stretch, HEAD), lambda s, g, i: (0, s, g)),
+            pl.BlockSpec((held, 2, stretch, HEAD), lambda s, g, i: (0, 0, s, g)),
+        ],
         out_shape=[
             jax.ShapeDtypeStruct(q.shape, F32),
             jax.ShapeDtypeStruct((2, rows, kv_heads * HEAD), F32),
             jax.ShapeDtypeStruct((held, 2, rows, kv_heads * HEAD), BF),
         ],
+        scratch_shapes=[pltpu.VMEM((span, HEAD), F32), pltpu.VMEM((span, HEAD), F32)],
         name=attn_bwd.__name__,
         cost_estimate=pl.CostEstimate(flops=3 * 10**10, bytes_accessed=12 * 2**20, transcendentals=4 * 2**20),
         compiler_params=pltpu.CompilerParams(vmem_limit_bytes=62 << 20),
-    )(first, low[None], lse, q, d_out, o, window, window)
+    )(low, lse, q, d_out, o, window, window)
 
 
 def chunk_index(schedule, s):
@@ -213,6 +138,11 @@
     shape = array.shape[1:]
     zeros = (0,) * len(shape)
     return array, pl.BlockSpec((None,) + shape, lambda s: (layer,) + zeros, pipeline_mode=pl.Buffered(1))
+
+
+class Row:
+    def __init__(self, layer):
+        self.layer = layer
 
 
 class Late:
@@ -232,7 +162,7 @@
             return where
         if where is HBM or isinstance(where, Late):
             return pl.BlockSpec(memory_space=pl.ANY)
-        if where is WHOLE:
+        if where is WHOLE or isinstance(where, Row):
             zeros = (0,) * len(shape)
             if is_in:
                 return pl.BlockSpec(shape, lambda s: zeros, pipeline_mode=pl.Buffered(1))
@@ -251,6 +181,9 @@
         for name, ref in own.items():
             named[name] = types.SimpleNamespace(**ref) if isinstance(ref, dict) else ref
         named.update(held_refs)
+        for name, (_, where) in ins.items():
+            if isinstance(where, Row):
+                named[name] = named[name].at[where.layer : where.layer + 1]
         s = pl.program_id(0)
 
         @pl.when(s == 0)
@@ -427,12 +360,14 @@
             out=pltpu.SemaphoreType.DMA((pieces,)),
         )
 
-    def start(self):
+    def start(self, other):
         @pl.when(self.middle)
         def _():
             @pl.loop(0, self.pieces)
             def _(j):
-                self.land[1, self.at(j), :] = self.x[self.at(j), :]
+                self.land[1, self.at(j), :] = (
+                    self.x[self.at(j), :].astype(F32) + other[self.at(j), :].astype(F32)
+                ).astype(BF)
 
                 @pl.when(self.has_outer)
                 def _():
@@ -447,12 +382,12 @@
 
 
 class KeyValueSend:
-    def __init__(self, refs, reach):
-        self.held, self.window = refs.kv.held, refs.window
+    def __init__(self, refs, reach, stretch):
+        self.held, self.zeros, self.window = refs.kv.held, refs.kv.zeros, refs.window
         self.copy_sem, self.send_sem, self.land_sem = refs.kv.copy, refs.kv.send, refs.kv.land
         self.chunks = self.copy_sem.shape[0]
         self.rows = self.held.shape[0] // self.chunks
-        self.reach = reach
+        self.reach, self.stretch = reach, stretch
         self.place = lax.axis_index("seq")
         self.count = lax.axis_size("seq")
 
@@ -461,6 +396,7 @@
         held = max(reach, 1)
         return dict(
             held=pltpu.VMEM((rows, width), BF),
+            zeros=pltpu.VMEM((rows // chunks, width), BF),
             copy=pltpu.SemaphoreType.DMA((chunks,)),
             send=pltpu.SemaphoreType.DMA((held, chunks)),
             land=pltpu.SemaphoreType.DMA((held, chunks)),
@@ -476,14 +412,25 @@
     def at(self, c):
         return pl.ds(pl.multiple_of(c * self.rows, self.rows), self.rows)
 
+    def there(self, back, c):
+        per = self.stretch // self.rows
+        chunk = ((c // per) * (self.reach + 1) + self.reach - back) * per + lax.rem(c, per)
+        return self.window.at[self.at(chunk)]
+
     def own(self, c):
-        return pltpu.make_async_copy(self.held.at[self.at(c)], self.window.at[self.reach, self.at(c)], self.copy_sem.at[c])
+        return pltpu.make_async_copy(self.held.at[self.at(c)], self.there(0, c), self.copy_sem.at[c])
+
+    def blank(self, back, c):
+        return pltpu.make_async_copy(self.zeros, self.there(back, c), self.land_sem.at[back - 1, c])
 
     def remote(self, back, c):
         return pltpu.make_async_remote_copy(
-            self.held.at[self.at(c)], self.window.at[self.reach - back, self.at(c)],
-            self.send_sem.at[back - 1, c], self.land_sem.at[back - 1, c],
+            self.held.at[self.at(c)], self.there(back, c), self.send_sem.at[back - 1, c],
+            self.land_sem.at[back - 1, c],
             device_id={"seq": jnp.minimum(self.place + back, self.count - 1)}, device_id_type=MESH)
+
+    def start(self):
+        self.zeros[...] = jnp.zeros_like(self.zeros)
 
     def send(self, c):
         self.own(c).start()
@@ -492,6 +439,10 @@
             @pl.when(self.place + back < self.count)
             def _():
                 self.remote(back, c).start()
+
+            @pl.when(self.place < back)
+            def _():
+                self.blank(back, c).start()
 
     def finish(self):
         @pl.loop(0, self.chunks)
@@ -506,6 +457,10 @@
                 @pl.when(self.place >= back)
                 def _():
                     self.remote(back, c).wait_recv()
+
+                @pl.when(self.place < back)
+                def _():
+                    self.blank(back, c).wait()
 
 
 class KeyValueReturn:
@@ -718,6 +673,61 @@
     return grad * cosine - pltpu.roll(grad, HEAD // 2, 1) * signed_sine
 
 
+def attend(r, c, stretch):
+    rows, span = r.queries_in.shape[0], r.window_in.shape[0] // (r.low.shape[1] // stretch)
+    offset = span - stretch
+    per = stretch // rows
+    length = min(WINDOW + rows, span)
+    q_start = offset + lax.rem(c, per) * rows
+    start = jnp.clip(q_start + rows - length, 0, span - length)
+    here = pl.ds(pl.multiple_of((c // per) * span + start, rows), length)
+    group = r.queries_in.shape[1] * 2 // r.window_in.shape[1]
+    low = r.low[:, pl.ds(pl.multiple_of(c * rows, rows), rows)].astype(F32)
+    low = jnp.broadcast_to(low, (HEAD, rows)).T[:, :1]
+    key_index = (start + lax.broadcasted_iota(jnp.int32, (rows, length), 1)).astype(F32)
+    q_index = (q_start + lax.broadcasted_iota(jnp.int32, (rows, 1), 0)).astype(F32)
+    mask = (key_index >= low) & (key_index <= q_index)
+    mask = jnp.concatenate([mask] * group, 0)
+    queries = heads_of(r.queries_in[...])
+    kv_heads = len(queries) // group
+    outs = []
+    for g in range(kv_heads):
+        keys = r.window_in[here, g * HEAD : (g + 1) * HEAD]
+        values = r.window_in[here, (kv_heads + g) * HEAD : (kv_heads + g + 1) * HEAD]
+        s = dot(jnp.concatenate(queries[g * group : (g + 1) * group], 0), keys, NT) * (SCALE * LOG2E)
+        p = jnp.where(mask, jnp.exp2(s), 0.0)
+        part = p[:, :HEAD]
+        for k in range(1, length // HEAD):
+            part = part + p[:, k * HEAD : (k + 1) * HEAD]
+        total = jnp.sum(part, 1, keepdims=True)
+        o = (dot(p.astype(BF), values) / total).astype(BF)
+        log_total = jnp.broadcast_to(jnp.log2(total), (group * rows, HEAD))
+        for h in range(group):
+            outs.append(o[h * rows : (h + 1) * rows])
+            r.lse[g, h : h + 1, :] = log_total[h * rows : (h + 1) * rows].T[0:1, :]
+    context = jnp.concatenate(outs, 1)
+    r.context[...] = context
+    return context
+
+
+def attend_ins(a, low, when):
+    return dict(
+        queries_in=(a.queries, when),
+        window_in=(a.window, WHOLE),
+        low=(low, WHOLE),
+    )
+
+
+def attend_outs(a, when):
+    kv_heads = a.window.shape[1] // (2 * HEAD)
+    rows, width = a.queries.shape
+    shape = (kv_heads, width // (kv_heads * HEAD), rows)
+    return dict(
+        context=((rows, width), BF, when),
+        lse=(shape, F32, pl.BlockSpec(shape[:2] + (rows // when[2],), lambda s: (0, 0, chunk_index(when, s)))),
+    )
+
+
 def project(r, hidden, kv, c):
     hat, _ = norm_parts(hidden)
     low = (hat * r.attn_gain[...].astype(F32)).astype(BF)
@@ -738,14 +748,14 @@
     kv.send(c)
 
 
-def project_outs(rows, width, w, reach, when):
+def project_outs(rows, width, w, stretch, reach, when):
     q_width, k_width = w.w_q.shape[2], w.w_k.shape[2]
     return dict(
         attn_low=((rows, width), BF, when),
         q_raw=((rows, q_width), F32, when),
         k_raw=((rows, k_width), F32, when),
         queries=((rows, q_width), BF, when),
-        window=((reach + 1, rows, k_width + w.w_v.shape[2]), BF, HBM),
+        window=((rows // stretch * (reach + 1) * stretch, k_width + w.w_v.shape[2]), BF, HBM),
     )
 
 
@@ -754,15 +764,13 @@
         return (array, Late(layer)) if late else of_layer(array, layer)
 
     return dict(
-        attn_gain=of_layer(w.attn_gain, layer),
+        attn_gain=(w.attn_gain, Row(layer)),
         w_q=weight(w.w_q),
         w_k=weight(w.w_k),
         w_v=weight(w.w_v),
-        q_gain=of_layer(w.q_gain, layer),
-        k_gain=of_layer(w.k_gain, layer),
-        cosine=(tables[0], when),
-        sine=(tables[1], when),
-    )
+        q_gain=(w.q_gain, Row(layer)),
+        k_gain=(w.k_gain, Row(layer)),
+    ) | (dict(cosine=(tables[0], when), sine=(tables[1], when)) if tables else {})
 
 
 def mlp_gates(r, low):
@@ -779,32 +787,96 @@
     return d_gate, d_up, dot(d_gate, r.w_gate[...], NT) + dot(d_up, r.w_up[...], NT)
 
 
-def first_projection(hidden, w, tables, reach, chunks, collective_id):
+def first_projection(hidden, segments, positions, w, stretch, reach, chunks, collective_id):
     rows, width = hidden.shape
     when = (1, 0, chunks)
     kv_width = w.w_k.shape[2] + w.w_v.shape[2]
 
+    held = max(reach, 1)
+    seqs = rows // stretch
+
     def body(r, s):
-        kv = KeyValueSend(r, reach)
+        kv = KeyValueSend(r, reach, stretch)
+
+        def documents(back):
+            return pltpu.make_async_remote_copy(
+                r.segments, r.docs.at[back - 1], r.doc_send.at[back - 1], r.doc_land.at[back - 1],
+                device_id={"seq": jnp.minimum(kv.place + back, kv.count - 1)}, device_id_type=MESH)
 
         @pl.when(s == 0)
         def _():
+            r.docs[...] = jnp.full_like(r.docs, -1)
             enter(kv.neighbours())
-
+            kv.start()
+            for back in range(1, reach + 1):
+
+                @pl.when(kv.place + back < kv.count)
+                def _():
+                    documents(back).start()
+
+        angle = jnp.broadcast_to(r.positions[...].astype(F32), (HEAD, rows // chunks)).T * r.frequency[...]
+        lane = lax.broadcasted_iota(jnp.int32, angle.shape, 1)
+        sine = jnp.sin(angle)
+        r.cosine[...] = jnp.cos(angle)
+        r.sine[...] = jnp.where(lane < HEAD // 2, -sine, sine)
         project(r, r.hidden[...].astype(F32), kv, s)
 
         @pl.when(s == chunks - 1)
         def _():
             kv.finish()
-
+            for back in range(1, reach + 1):
+
+                @pl.when(kv.place + back < kv.count)
+                def _():
+                    documents(back).wait_send()
+
+                @pl.when(kv.place >= back)
+                def _():
+                    documents(back).wait_recv()
+
+            for q in range(seqs):
+                here = slice(q * stretch, (q + 1) * stretch)
+                own = r.segments[:, here]
+                docs = [r.docs[back - 1, :, here] for back in range(1, reach + 1)]
+
+                def first_of(document):
+                    counts = [jnp.sum((d < document).astype(jnp.int32), 1, keepdims=True) for d in docs + [own]]
+                    return functools.reduce(jnp.add, counts)
+
+                low = jnp.broadcast_to(first_of(0), own.shape)
+                for document in range(1, 4):
+                    low = jnp.where(own >= document, first_of(document), low)
+                index = lax.broadcasted_iota(jnp.int32, own.shape, 1)
+                r.low[:, here] = jnp.maximum(low, reach * stretch + index - (WINDOW - 1))
+
+    frequency = THETA ** (-(jnp.arange(HEAD // 2, dtype=F32) * 2.0) / HEAD)
     return step_kernel(
         first_projection, body, chunks,
-        dict(hidden=(hidden, when)) | project_ins(w, 0, tables, when, False),
-        project_outs(rows, width, w, reach, when),
-        dict(kv=KeyValueSend.scratch(rows, kv_width, chunks, reach)), collective_id)
-
-
-def between_forward(context, hidden, w, layer, tables, reach, chunks, collective_id):
+        dict(
+            hidden=(hidden, when),
+            segments=(segments.reshape(1, rows), WHOLE),
+            positions=(
+                positions.reshape(1, rows), pl.BlockSpec((1, rows // chunks), lambda s: (0, chunk_index(when, s)))),
+            frequency=(jnp.concatenate([frequency, frequency])[None], WHOLE),
+        )
+        | project_ins(w, 0, None, when, False),
+        project_outs(rows, width, w, stretch, reach, when)
+        | dict(
+            cosine=((rows, HEAD), F32, when),
+            sine=((rows, HEAD), F32, when),
+            low=((1, rows), jnp.int32, WHOLE),
+        ),
+        dict(
+            kv=KeyValueSend.scratch(rows, kv_width, chunks, reach),
+            docs=pltpu.VMEM((held, 1, rows), jnp.int32),
+            doc_send=pltpu.SemaphoreType.DMA((held,)),
+            doc_land=pltpu.SemaphoreType.DMA((held,)),
+        ),
+        collective_id)
+
+
+def between_forward(a, low, w, layer, tables, stretch, reach, chunks, collective_id):
+    hidden = a.hidden
     rows, width = hidden.shape
     kv_width = w.w_k.shape[2] + w.w_v.shape[2]
     ff = w.w_gate.shape[2]
@@ -814,15 +886,16 @@
     chunk = rows // chunks
 
     def body(r, s):
-        kv = KeyValueSend(r, reach)
+        kv = KeyValueSend(r, reach, stretch)
         attn, mlp = LineSum(r.attn), LineSum(r.mlp)
 
         @pl.when(s == 0)
         def _():
             enter(attn.neighbours() + kv.neighbours())
+            kv.start()
 
         def send_attn(c):
-            attn.put(c, dot(r.context[...], r.w_o[...]))
+            attn.put(c, dot(attend(r, c, stretch), r.w_o[...]))
 
         def feed_forward(c):
             middle = r.hidden[...].astype(F32) + attn.total(c, chunk)
@@ -861,17 +934,18 @@
 
     return step_kernel(
         between_forward, body, steps,
-        dict(
-            context=(context, first),
+        attend_ins(a, low, first)
+        | dict(
             w_o=of_layer(w.w_o, layer),
             hidden=(hidden, second),
-            mlp_gain=of_layer(w.mlp_gain, layer),
+            mlp_gain=(w.mlp_gain, Row(layer)),
             w_gate=(w.w_gate, Late(layer)),
             w_up=(w.w_up, Late(layer)),
             w_down=(w.w_down, Late(layer)),
         )
         | project_ins(w, layer + 1, tables, third, True),
-        dict(
+        attend_outs(a, first)
+        | dict(
             hidden_mid=((rows, width), F32, second),
             mlp_low=((rows, width), BF, second),
             gate=((rows, ff), F32, second),
@@ -879,7 +953,7 @@
             act=((rows, ff), BF, second),
             hidden_next=((rows, width), F32, third),
         )
-        | project_outs(rows, width, w, reach, third),
+        | project_outs(rows, width, w, stretch, reach, third),
         dict(
             attn=LineSum.scratch(rows, width, pieces),
             mlp=LineSum.scratch(rows, width, pieces),
@@ -889,7 +963,8 @@
         collective_id)
 
 
-def turn_around(context, hidden, cotangent, w, layer, chunks, collective_id):
+def turn_around(a, low, cotangent, w, layer, stretch, chunks, collective_id):
+    hidden = a.hidden
     rows, width = hidden.shape
     ff = w.w_gate.shape[2]
     pieces = chunks * PIECES
@@ -906,7 +981,7 @@
             r.gain_grad[...] = jnp.zeros_like(r.gain_grad)
 
         def send_attn(c):
-            attn.put(c, dot(r.context[...], r.w_o[...]))
+            attn.put(c, dot(attend(r, c, stretch), r.w_o[...]))
 
         def feed_forward(c):
             middle = r.hidden[...] + attn.total(c, chunk)
@@ -922,7 +997,15 @@
             r.d_up[...] = d_up
             act = (gate * sigma * up).astype(BF)
             r.act[...] = act
-            r.mlp_part[...] = dot(act, r.w_down[...]).astype(BF)
+            part = dot(act, r.w_down[...]).astype(BF)
+
+            @pl.when(c < chunks // 2)
+            def _():
+                r.lower_part[...] = part
+
+            @pl.when(c >= chunks // 2)
+            def _():
+                r.upper_part[...] = part
 
         def middle_grad(c):
             hat, inverse = norm_parts(r.mid_held[back.at(c, chunk), :])
@@ -950,27 +1033,29 @@
 
     return step_kernel(
         turn_around, body, steps,
-        dict(
-            context=(context, first),
+        attend_ins(a, low, first)
+        | dict(
             w_o=of_layer(w.w_o, layer),
             hidden=(hidden, second),
             cotangent=(cotangent, second),
             cotangent_late=(cotangent, third),
-            mlp_gain=of_layer(w.mlp_gain, layer),
+            mlp_gain=(w.mlp_gain, Row(layer)),
             w_gate=(w.w_gate, Late(layer)),
             w_up=(w.w_up, Late(layer)),
             w_down=(w.w_down, Late(layer)),
         ),
-        dict(
+        attend_outs(a, first)
+        | dict(
             mlp_low=((rows, width), BF, second),
             act=((rows, ff), BF, second),
             hidden_mid=((rows, width), F32, second),
-            mlp_part=((rows, width), BF, second),
+            lower_part=((rows // 2, width), BF, (PIECES, second[1], chunks // 2)),
+            upper_part=((rows // 2, width), BF, (PIECES, second[1] + PIECES * (chunks // 2), chunks // 2)),
             d_gate=((rows, ff), BF, second),
             d_up=((rows, ff), BF, second),
             g_mid=((rows, width), F32, third),
             mid_low=((rows, width), BF, third),
-            d_context=(context.shape, BF, third),
+            d_context=(a.queries.shape, BF, third),
             gain_grad=((8, width), F32, WHOLE),
         ),
         dict(
@@ -1170,9 +1255,9 @@
         w_q=of_layer(w.w_q, layer),
         w_k=of_layer(w.w_k, layer),
         w_v=of_layer(w.w_v, layer),
-        q_gain=of_layer(w.q_gain, layer),
-        k_gain=of_layer(w.k_gain, layer),
-        attn_gain=of_layer(w.attn_gain, layer),
+        q_gain=(w.q_gain, Row(layer)),
+        k_gain=(w.k_gain, Row(layer)),
+        attn_gain=(w.attn_gain, Row(layer)),
     )
 
 
@@ -1185,10 +1270,10 @@
     chunk = rows // chunks
     after = PIECES * (chunks - 1) + 1
     plan = types.SimpleNamespace(
-        slabs=(PIECES, 4, slab_count(chunks)),
-        early=lambda k: min(after - 2 + 6 * k, steps - 2),
-        late_slabs=(after, after + 2),
-        late=lambda k: min(after + 5 + 2 * k, steps - 2),
+        slabs=(PIECES, 2, slab_count(chunks)),
+        early=lambda k: min(after - 3 + 4 * k, steps - 2),
+        late_slabs=(after, after + 1),
+        late=lambda k: min(after + 3 + 2 * k, steps - 2),
     )
 
     def body(r, s):
@@ -1232,12 +1317,12 @@
 
         at_chunk(s, first, send_attn)
         grads.late_slabs(s)
-        at_chunk(s, (1, 2, pieces), attn.relay)
-        at_chunk(s, (1, 3, pieces), attn.meet)
+        at_chunk(s, (1, 1, pieces), attn.relay)
+        at_chunk(s, (1, 2, pieces), attn.meet)
         r.arrived(second[1], *MLP_WEIGHTS)
         at_chunk(s, second, feed_forward)
-        at_chunk(s, (1, 7, pieces), mlp.relay)
-        at_chunk(s, (1, 8, pieces), mlp.meet)
+        at_chunk(s, (1, 6, pieces), mlp.relay)
+        at_chunk(s, (1, 7, pieces), mlp.meet)
         r.arrived(third[1], "w_o")
         at_chunk(s, third, middle_grad)
         grads.run(s)
@@ -1260,7 +1345,7 @@
             gate=(below.gate, second),
             up=(below.up, second),
             hidden_mid=(below.hidden_mid, third),
-            mlp_gain=of_layer(w.mlp_gain, layer - 1),
+            mlp_gain=(w.mlp_gain, Row(layer - 1)),
             w_gate=(w.w_gate, Late(layer - 1)),
             w_up=(w.w_up, Late(layer - 1)),
             w_down=(w.w_down, Late(layer - 1)),
@@ -1287,7 +1372,8 @@
         collective_id)
 
 
-def last_backward(a, top, top_total, g_mid, gain_parts, w, tables, reach, chunks, collective_id):
+def last_backward(a, top, top_halves, above, w, tables, reach, chunks, collective_id):
+    g_mid = above.g_mid
     rows, width = g_mid.shape
     q_width, k_width, ff = w.w_q.shape[2], w.w_k.shape[2], w.w_gate.shape[2]
     layer = 0
@@ -1308,7 +1394,7 @@
 
     def body(r, s):
         back = KeyValueReturn(r, reach)
-        attn, upper, lower = LineSum(r.attn), LineSum(r.upper, r.upper_part), Spread(r.lower, r.lower_total)
+        attn, upper, lower = LineSum(r.attn), LineSum(r.upper, r.upper_part), Spread(r.lower, r.lower_here)
         grads = WeightGrads(r, plan)
         sums = Butterfly(r.sums)
 
@@ -1316,7 +1402,7 @@
         def _():
             enter(attn.neighbours() + back.neighbours() + sums.neighbours())
             back.start()
-            lower.start()
+            lower.start(r.lower_there)
             r.head_gain[...] = jnp.zeros_like(r.head_gain)
             r.gain_held[...] = jnp.zeros_like(r.gain_held)
 
@@ -1355,9 +1441,14 @@
         @pl.when(s == after)
         def _():
             row = lax.broadcasted_iota(jnp.int32, (8, width), 0)
-            pad = jnp.zeros((1, width - 2 * HEAD), F32)
-            heads = jnp.concatenate([r.head_gain[0:1, :], pad], 1)
-            packet = r.gain_parts[...] + jnp.where(row == 0, r.gain_held[...], 0.0) + jnp.where(row == 4, heads, 0.0)
+            once = jnp.where(lax.axis_index("tensor") == 0, 1.0, 0.0)
+            heads = [r.head_gain[0:1, :], r.above_head_gain[0:1, :], jnp.zeros((1, width - 4 * HEAD), F32)]
+            packet = jnp.zeros((8, width), F32)
+            for place, part in enumerate([
+                r.gain_held[...], r.above_gain[0:1, :] * once, r.above_gain[1:2, :] * once, r.top_gain[0:1, :] * once,
+                jnp.concatenate(heads, 1),
+            ]):
+                packet = jnp.where(row == place, part, packet)
             sums.put(packet)
 
         for k in range(len(sums.axes)):
@@ -1385,9 +1476,12 @@
             hidden=(a.hidden, first),
             hidden_late=(a.hidden, second),
             g_above=(g_mid, second),
-            gain_parts=(gain_parts, WHOLE),
-            upper_part=(top.mlp_part, pl.BlockSpec((half, width), lambda s: (1, 0), pipeline_mode=pl.Buffered(1))),
-            lower_total=(top_total, WHOLE),
+            above_gain=(above.gain_grad, WHOLE),
+            above_head_gain=(above.head_gain, WHOLE),
+            top_gain=(top.gain_grad, WHOLE),
+            upper_part=(top.upper_part, WHOLE),
+            lower_here=(top_halves[0], WHOLE),
+            lower_there=(top_halves[1], WHOLE),
             hidden_mid=(top.hidden_mid, third),
         ),
         dict(
@@ -1409,47 +1503,78 @@
         collective_id)
 
 
-def shifted(array, axis, by):
-    devices = lax.axis_size(axis)
-    pairs = [(i, i + by) for i in range(devices) if 0 <= i + by < devices]
-    return lax.ppermute(array, axis, pairs)
-
-
-def middle_sum(part):
+def collect_kernel(count, output_in, input_in, gains, *refs):
+    ins, (output, input_grad, attn, mlp, q_gain, k_gain), outs = refs[: 2 * count], refs[2 * count : 2 * count + 6], refs[2 * count + 6 :]
+    output[...] = output_in[...]
+    input_grad[...] = input_in[...]
+    s = pl.program_id(0)
+
+    @pl.when(s == 0)
+    def _():
+        attn[...] = gains[0:2, :]
+        mlp[...] = gains[2:4, :]
+        for layer in range(2):
+            at = 2 * layer * HEAD
+            q_gain[layer : layer + 1, :] = gains[4:5, at : at + HEAD]
+            k_gain[layer : layer + 1, :] = gains[4:5, at + HEAD : at + 2 * HEAD]
+
+    for g in range(count):
+        for layer in range(2):
+            value = ins[2 * g + layer]
+            if outs[g].shape[1] == value.shape[0]:
+                outs[g][layer] = value[...]
+            else:
+
+                @pl.when(s == 0)
+                def _():
+                    outs[g][layer] = value[...].T
+
+
+def collect(end, above):
+    rows, width = end.output.shape
+    straight = [(k.grad_q, k.grad_k, k.grad_v, k.grad_gate, k.grad_up) for k in (end, above)]
+    turned = [(k.grad_o, k.grad_down) for k in (end, above)]
+    per = straight[0][0].shape[0]
+    steps = max(1, min(8, per // 8))
+    whole = pl.BlockSpec(memory_space=pltpu.VMEM)
+
+    def blocks(array):
+        return pl.BlockSpec((array.shape[0] // steps, array.shape[1]), lambda s: (s, 0))
+
+    ins = [end.output, end.input_grad, end.gains]
+    in_specs = [blocks(end.output), blocks(end.input_grad), whole]
+    outs = [
+        ((rows, width), BF, blocks(end.output)), ((rows, width), F32, blocks(end.input_grad)),
+        ((2, width), F32, whole), ((2, width), F32, whole), ((2, HEAD), F32, whole), ((2, HEAD), F32, whole),
+    ]
+    for pair in zip(*straight):
+        ins += pair
+        in_specs += [blocks(a) for a in pair]
+        shape = pair[0].shape
+        outs.append(((2,) + shape, F32, pl.BlockSpec((2, per // steps, shape[1]), lambda s: (0, s, 0))))
+    for pair in zip(*turned):
+        ins += pair
+        in_specs += [whole, whole]
+        outs.append(((2,) + pair[0].shape[::-1], F32, whole))
+    return pl.pallas_call(
+        functools.partial(collect_kernel, 7),
+        grid=(steps,),
+        in_specs=in_specs,
+        out_specs=[o[2] for o in outs],
+        out_shape=[jax.ShapeDtypeStruct(o[0], o[1]) for o in outs],
+        name=collect.__name__,
+        compiler_params=pltpu.CompilerParams(vmem_limit_bytes=62 << 20),
+    )(*ins)
+
+
+def middle_terms(part):
     n = lax.axis_size("tensor")
     half = n // 2
     total = part
     for hop in range(half - 1):
         moved = lax.ppermute(total, "tensor", [(hop, hop + 1), (n - 1 - hop, n - 2 - hop)])
         total = (part.astype(F32) + moved.astype(F32)).astype(BF)
-    if n > 1:
-        moved = lax.ppermute(total, "tensor", [(half - 1, half), (half, half - 1)])
-        total = (total.astype(F32) + moved.astype(F32)).astype(BF)
-    return total
-
-
-def rope_tables(places):
-    halves = HEAD // 2
-    frequency = THETA ** (-(jnp.arange(halves, dtype=F32) * 2.0) / HEAD)
-    angle = places.astype(F32)[:, None] * frequency
-    cosine, sine = jnp.cos(angle), jnp.sin(angle)
-    return jnp.concatenate([cosine, cosine], -1), jnp.concatenate([-sine, sine], -1)
-
-
-def lowest_keys(segments, reach):
-    seqs_here, stretch = segments.shape
-    place = lax.axis_index("seq")
-    docs = [segments]
-    for back in range(1, reach + 1):
-        docs.insert(0, jnp.where(place >= back, shifted(segments, "seq", back), -1))
-    docs = jnp.concatenate(docs, 1)
-    start = jnp.sum((docs < 0).astype(jnp.int32), 1, keepdims=True)
-    low = jnp.broadcast_to(start, segments.shape)
-    for d in range(1, 4):
-        start = jnp.sum((docs < d).astype(jnp.int32), 1, keepdims=True)
-        low = jnp.where(segments >= d, start, low)
-    index = jnp.arange(stretch, dtype=jnp.int32)
-    return jnp.maximum(low, reach * stretch + index - (WINDOW - 1)).reshape(-1)
+    return total, lax.ppermute(total, "tensor", [(half - 1, half), (half, half - 1)])
 
 
 def per_device(
@@ -1462,55 +1587,39 @@
     chunks = rows // min(CHUNK, stretch)
 
     w = types.SimpleNamespace(
-        attn_gain=attn_gain[:, None], mlp_gain=mlp_gain[:, None], q_gain=query_gain[:, None], k_gain=key_gain[:, None],
+        attn_gain=attn_gain, mlp_gain=mlp_gain, q_gain=query_gain, k_gain=key_gain,
         w_q=w_query, w_k=key_projection, w_v=value_projection, w_o=w_output, w_gate=w_gate, w_up=w_up, w_down=w_down,
     )
-    tables = rope_tables(positions.reshape(rows))
-    low = lowest_keys(segments, reach)
-    block = min(512, stretch)
-    first = low[::block]
     tokens = tokens.reshape(rows, width)
     cotangent = cotangent.reshape(rows, width)
 
-    a0 = first_projection(tokens, w, tables, reach, chunks, 1)
+    a0 = first_projection(tokens, segments, positions, w, stretch, reach, chunks, 1)
+    tables, low = (a0.cosine, a0.sine), a0.low
     a0.hidden = tokens
-    a0.context, a0.lse = attn_fwd(a0.queries, a0.window, first, low, stretch, block, block)
-    mid = between_forward(a0.context, tokens, w, 0, tables, reach, chunks, 2)
+    mid = between_forward(a0, low, w, 0, tables, stretch, reach, chunks, 2)
+    a0.context, a0.lse = mid.context, mid.lse
     a1 = types.SimpleNamespace(
         attn_low=mid.attn_low, q_raw=mid.q_raw, k_raw=mid.k_raw, queries=mid.queries, window=mid.window,
         hidden=mid.hidden_next)
-    a1.context, a1.lse = attn_fwd(a1.queries, a1.window, first, low, stretch, block, block)
-    turn = turn_around(a1.context, a1.hidden, cotangent, w, 1, chunks, 3)
-    top_total = middle_sum(turn.mlp_part[: rows // 2])
+    turn = turn_around(a1, low, cotangent, w, 1, stretch, chunks, 3)
+    a1.context, a1.lse = turn.context, turn.lse
+    top_halves = middle_terms(turn.lower_part)
     a1.mlp_low, a1.act, a1.d_gate, a1.d_up = turn.mlp_low, turn.act, turn.d_gate, turn.d_up
     a1.mid_low, a1.g_low = turn.mid_low, cotangent
     a1.d_q, a1.d_own, a1.d_prev = attn_bwd(
-        a1.queries, turn.d_context, a1.context, a1.window, first, low, a1.lse, stretch, block, block)
+        a1.queries, turn.d_context, a1.context, a1.window, low, a1.lse, stretch)
     down = between_backward(a1, mid, turn.g_mid, w, 1, tables, reach, chunks, 4)
     a0.mlp_low, a0.act, a0.d_gate, a0.d_up = mid.mlp_low, mid.act, down.d_gate, down.d_up
     a0.mid_low, a0.g_low = down.mid_low, down.g_low
     a0.d_q, a0.d_own, a0.d_prev = attn_bwd(
-        a0.queries, down.d_context, a0.context, a0.window, first, low, a0.lse, stretch, block, block)
-
-    once = lax.axis_index("tensor") == 0
-    shared = jnp.concatenate([
-        jnp.zeros((1, width), F32), down.gain_grad[0:1], down.gain_grad[1:2], turn.gain_grad[0:1],
-        jnp.zeros((4, width), F32)], 0)
-    heads = jnp.pad(down.head_gain[0:1], ((4, 3), (2 * HEAD, width - 4 * HEAD)))
-    gain_parts = jnp.where(once, shared, 0.0) + heads
-    end = last_backward(a0, turn, top_total, down.g_mid, gain_parts, w, tables, reach, chunks, 5)
-    gains = end.gains
-
-    def both(pick, turned=False):
-        lower, upper = pick(end), pick(down)
-        return jnp.stack([lower.T, upper.T] if turned else [lower, upper])
-
-    head_rows = gains[4, : 4 * HEAD].reshape(2, 2, HEAD)
+        a0.queries, down.d_context, a0.context, a0.window, low, a0.lse, stretch)
+
+    end = last_backward(a0, turn, top_halves, down, w, tables, reach, chunks, 5)
+    output, input_grad, attn, mlp, q_gain, k_gain, d_q, d_k, d_v, d_gate, d_up, d_o, d_down = collect(end, down)
     shape = (seqs_here, stretch, width)
     return (
-        end.output.reshape(shape), end.input_grad.reshape(shape), gains[0:2], both(lambda k: k.grad_q), both(lambda k: k.grad_k),
-        both(lambda k: k.grad_v), head_rows[:, 0], head_rows[:, 1], both(lambda k: k.grad_o, True), gains[2:4], both(lambda k: k.grad_gate),
-        both(lambda k: k.grad_up), both(lambda k: k.grad_down, True),
+        output.reshape(shape), input_grad.reshape(shape), attn, d_q, d_k, d_v, q_gain, k_gain, d_o, mlp, d_gate, d_up,
+        d_down,
     )
 
 

time: 589 us -> 526 us (0.89); the launches traced: 580 us -> 524 us
  Pallas kernels: 535 us -> 517 us
  other arithmetic: 20.2 us -> 2.54 us
  local copies, waits for them, and re-layouts: 17.5 us -> 0.01 us
    pallas_call x5, Pallas kernels: 477 us -> 466 us  [step_kernel(): pl.pallas_call(kernel, grid=(steps,), in_specs=[spec(a.shape, w, True) fo...]
    another operation x8 -> x0, other arithmetic: 7.77 us -> none  [the longest x7 5.17 us: both(): return jnp.stack([lower.T, upper.T] if turned else [lower, upper])]
    unnamed x46 -> x2, local copies, waits for them, and re-layouts: 7.18 us -> 0.01 us
    pallas_call x4 -> x3, Pallas kernels: 57.7 us -> 50.7 us  [the longest x2 40.2 us: attn_bwd(): pl.pallas_call(functools.partial(attn_bwd_kernel, reach * stretch), grid=...]
    slice x8 -> x0, local copies, waits for them, and re-layouts: 6.9 us -> none  [the longest x1 1.44 us: per_device(): gains[2:4]]
  transfers between devices with their start and end apart: 3 -> 2, of which waited for: 0 -> 0; matrix products, arithmetic and copies ran while one was open for 2% -> 0% of each run, Pallas kernels for 31% -> 30%
where the time goes in v3:
time: 526 us; the launch traced here: 524 us
  Pallas kernels  517 us (98%)
    pallas_call x5, Pallas kernels, step_kernel(): pl.pallas_call(kernel, grid=(steps,), in_specs=[spec(a.shape, w, True) fo...  466 us
    pallas_call x2, Pallas kernels, attn_bwd(): pl.pallas_call(functools.partial(attn_bwd_kernel, reach * stretch), grid=...  40.2 us
    pallas_call x1, Pallas kernels, collect(): pl.pallas_call(functools.partial(collect_kernel, 7), grid=(steps,), in_sp...  10.6 us
  transfers between devices with their start and end apart: 2, of which 0 were waited for; matrix products, arithmetic and copies ran while one was open for 0% of the time, Pallas kernels for 30%

profile of v3, /device:TPU:0, one launch (start us, length us, event | category | flops | bytes accessed | tf_op | source)
XLA Modules:
  0.0 524.3 jit_solution(65730502742262021)
XLA Ops:
  0.7 0.6 maximum_bitcast_fusion.refs_3_
  1.2 12.8 %first_projection.1 = (bf16[1024,1024]{1,0:T(8,128)(2,1)}, f32[1024,512]{1,0:T(8,128)}, f32[1024,256]{1,0:T(8,128)}, bf16[1024,512]{1,0:T(8,128)(2,1)}, bf16[204...) custom-call(bf16[1024,1024]{1,0:T(8,128)(2,1)} %bitcast.6, ...), custom_call_target="tpu_custom_call" | custom-call | tf_op jit(solution)/shard_map/first_projection/pallas_call | solution.py:202
  14.1 117.5 %between_forward.1 = (bf16[1024,512]{1,0:T(8,128)(2,1)}, f32[2,2,1024]{2,1,0:T(2,128)}, f32[1024,1024]{1,0:T(8,128)}, bf16[1024,1024]{1,0:T(8,128)(2,1)}, f32[10...) custom-call(bf16[1024,512]{1,0:T(8,128)(2,1)} %get-tuple-element.92., ...), custom_call_target="tpu_custom_call" | custom-call | tf_op jit(solution)/shard_map/between_forward/pallas_call | solution.py:202
  131.6 115.3 %turn_around.1 = (bf16[1024,512]{1,0:T(8,128)(2,1)}, f32[2,2,1024]{2,1,0:T(2,128)}, bf16[1024,1024]{1,0:T(8,128)(2,1)}, bf16[1024,768]{1,0:T(8,128)(2,1)}, f32[1...) custom-call(bf16[1024,512]{1,0:T(8,128)(2,1)} %get-tuple-element.97., ...), custom_call_target="tpu_custom_call" | custom-call | tf_op jit(solution)/shard_map/turn_around/pallas_call | solution.py:202
  246.9 2.3 collective-permute-start
  249.2 20.1 %attn_bwd.2 = (f32[1024,512]{1,0:T(8,128)}, f32[2,1024,256]{2,1,0:T(8,128)}, bf16[1,2,1024,256]{3,2,1,0:T(8,128)(2,1)}) custom-call(s32[1,1024]{1,0:T(1,128)} %get-tuple-element.91.refs_2_.low_ref, f32[2,2,1024]{2,1,0:T(2,128)} %get-tuple-element.100.lse_ref, bf16[1024,512]{1,0:T(8,128)(2,1)} %get-tuple-element.97.refs_0_.q_ref, ...), custom_call_target="tpu_custom_call" | custom-call | flops 30000001024 | bytes 12582912 | tf_op jit(solution)/shard_map/attn_bwd/pallas_call | solution.py:93
  269.3 118.7 %between_backward.1 = (bf16[1024,1024]{1,0:T(8,128)(2,1)}, bf16[1024,768]{1,0:T(8,128)(2,1)}, bf16[1024,768]{1,0:T(8,128)(2,1)}, f32[1024,1024]{1,0:T(8,128)}, b...) custom-call(f32[1024,512]{1,0:T(8,128)} %get-tuple-element.103.refs_, ...), custom_call_target="tpu_custom_call" | custom-call | tf_op jit(solution)/shard_map/between_backward/pallas_call | solution.py:202
  388.0 0.0 collective-permute-done
  388.0 1.9 add_convert_fusion.refs_28_
  389.9 0.0 copy-start
  389.9 1.9 collective-permute-start.1
  391.8 20.1 %attn_bwd.3 = (f32[1024,512]{1,0:T(8,128)}, f32[2,1024,256]{2,1,0:T(8,128)}, bf16[1,2,1024,256]{3,2,1,0:T(8,128)(2,1)}) custom-call(s32[1,1024]{1,0:T(1,128)} %get-tuple-element.91.refs_2_.low_ref, f32[2,2,1024]{2,1,0:T(2,128)} %get-tuple-element.96.lse_ref, bf16[1024,512]{1,0:T(8,128)(2,1)} %get-tuple-element.92.refs_0_.q_ref, ...), custom_call_target="tpu_custom_call" | custom-call | flops 30000001024 | bytes 12582912 | tf_op jit(solution)/shard_map/attn_bwd/pallas_call | solution.py:93
  411.9 0.0 copy-done
  411.9 0.0 collective-permute-done.1.refs_29_
  411.9 101.6 %last_backward.1 = (f32[1024,1024]{1,0:T(8,128)}, bf16[1024,1024]{1,0:T(8,128)(2,1)}, f32[8,1024]{1,0:T(8,128)}, f32[128,512]{1,0:T(8,128)}, f32[128,256]{1,0:T(...) custom-call(f32[1024,512]{1,0:T(8,128)} %get-tuple-element.120.refs_, ...), custom_call_target="tpu_custom_call" | custom-call | tf_op jit(solution)/shard_map/last_backward/pallas_call | solution.py:202
  513.5 10.6 %collect.1 = (bf16[1024,1024]{1,0:T(8,128)(2,1)}, f32[1024,1024]{1,0:T(8,128)}, f32[2,1024]{1,0:T(2,128)}, f32[2,1024]{1,0:T(2,128)}, f32[2,128]{1,0:T(2,128)}, ...) custom-call(bf16[1024,1024]{1,0:T(8,128)(2,1)} %get-tuple-element.13, ...), custom_call_target="tpu_custom_call" | custom-call | tf_op jit(solution)/shard_map/collect/pallas_call | solution.py:1559
  (1 shorter events, 0.0 us)
Async XLA Ops:
  246.9 141.1 %collective-permute-start = (bf16[512,1024]{1,0:T(8,128)(2,1)}, bf16[512,1024]{1,0:T(8,128)(2,1)}, u32[]{:S(2)}, u32[]{:S(2)}) collective-permute-start(bf16[512,1024]{1,0:T(8,128)(2,1)} %get-tuple-element.137), channel_id=1, source_target_pairs={{0,1},{3,2},{4,5},{7,6},{8,9},{11,10},{12,13},{15,14},{16,17},{19,... | collective-permute-start | bytes 3145736 | tf_op jit(solution)/shard_map/ppermute | solution.py:1575
  389.9 22.0 %copy-start = (bf16[512,1024]{1,0:T(8,128)(2,1)}, bf16[512,1024]{1,0:T(8,128)(2,1)S(1)}, u32[]{:S(2)}) copy-start(bf16[512,1024]{1,0:T(8,128)(2,1)S(1)} %add_convert_fusion.refs_28_) | copy-start | bytes 3145732
  389.9 22.0 %collective-permute-start.1 = (bf16[512,1024]{1,0:T(8,128)(2,1)S(1)}, bf16[512,1024]{1,0:T(8,128)(2,1)}, u32[]{:S(2)}, u32[]{:S(2)}) collective-permute-start(bf16[512,1024]{1,0:T(8,128)(2,1)S(1)} %add_convert_fusion.refs_28_), channel_id=1, source_target_pairs={{1,2},{2,1},{5,6},{6,5},{9,10},{10,9},{13,14},{14,13},{17,18},{18,... | collective-permute-start | bytes 3145736 | tf_op jit(solution)/shard_map/ppermute | solution.py:1577

commit v4 on v3

--- a/solution.py
+++ b/solution.py
@@ -3,6 +3,7 @@
 
 import jax
 import jax.numpy as jnp
+import numpy as np
 from jax import lax
 from jax.experimental import pallas as pl
 from jax.experimental.pallas import tpu as pltpu
@@ -17,6 +18,7 @@
 SCALE = HEAD ** (-0.5)
 CHUNK = 128
 PIECES = 2
+FINE = 4
 MESH = pl.DeviceIdType.MESH
 BF = jnp.bfloat16
 F32 = jnp.float32
@@ -30,95 +32,6 @@
     return lax.dot_general(a, b, dims, preferred_element_type=F32)
 
 
-def attn_bwd_kernel(offset, low_ref, lse_ref, q_ref, do_ref, o_ref, k_ref, v_ref, dq_ref, own_ref, prev_ref,
-                    dk_ref, dv_ref):
-    step = pl.program_id(2)
-    qb = q_ref.shape[0]
-    heads = q_ref.shape[1] // HEAD
-    span = k_ref.shape[0]
-    length = min(WINDOW + qb, span)
-    q_start = step * qb + offset
-    start = jnp.clip(q_start + qb - length, 0, span - length)
-    here = pl.ds(pl.multiple_of(start, HEAD), length)
-
-    @pl.when(step == 0)
-    def _():
-        dk_ref[...] = jnp.zeros_like(dk_ref)
-        dv_ref[...] = jnp.zeros_like(dv_ref)
-
-    def stack(ref):
-        return jnp.concatenate([ref[:, h * HEAD : (h + 1) * HEAD] for h in range(heads)], 0)
-
-    queries = stack(q_ref)
-    d_out = stack(do_ref)
-    lse = jnp.concatenate([lse_ref[h : h + 1, :] for h in range(heads)], 1)
-    product = d_out.astype(F32) * stack(o_ref).astype(F32)
-    delta = jnp.sum(product.T, 0, keepdims=True)
-    keys = k_ref[here, :]
-    values = v_ref[here, :]
-    key_index = start + lax.broadcasted_iota(jnp.int32, (length, qb), 0)
-    q_index = q_start + lax.broadcasted_iota(jnp.int32, (1, qb), 1)
-    mask = (key_index >= low_ref[...]) & (key_index <= q_index)
-    mask = jnp.concatenate([mask] * heads, 1)
-    s = dot(keys, queries, NT) * (SCALE * LOG2E) - lse
-    p = jnp.where(mask, jnp.exp2(s), 0.0)
-    ds = (p * (dot(values, d_out, NT) - delta)).astype(BF)
-    dv_ref[here, :] += dot(p.astype(BF), d_out)
-    dk_ref[here, :] += dot(ds, queries)
-    dq = dot(ds, keys, TN) * SCALE
-    for h in range(heads):
-        dq_ref[:, h * HEAD : (h + 1) * HEAD] = dq[h * qb : (h + 1) * qb]
-
-    @pl.when(step == pl.num_programs(2) - 1)
-    def _():
-        own_ref[0] = dk_ref[offset:, :] * SCALE
-        own_ref[1] = dv_ref[offset:, :]
-        stretch = own_ref.shape[1]
-        for j in range(offset // stretch):
-            prev_ref[j, 0] = (dk_ref[j * stretch : (j + 1) * stretch, :] * SCALE).astype(BF)
-            prev_ref[j, 1] = dv_ref[j * stretch : (j + 1) * stretch, :].astype(BF)
-
-
-def attn_bwd(q, d_out, o, window, low, lse, stretch):
-    rows = q.shape[0]
-    kv_heads = window.shape[1] // (2 * HEAD)
-    width = q.shape[1] // kv_heads
-    group = width // HEAD
-    qb = min(2 * CHUNK, stretch)
-    steps = stretch // qb
-    span = window.shape[0] // (rows // stretch)
-    reach = span // stretch - 1
-    held = max(reach, 1)
-    row_spec = pl.BlockSpec((qb, width), lambda s, g, i: (s * steps + i, g))
-    return pl.pallas_call(
-        functools.partial(attn_bwd_kernel, reach * stretch),
-        grid=(rows // stretch, kv_heads, steps),
-        in_specs=[
-            pl.BlockSpec((1, qb), lambda s, g, i: (0, s * steps + i)),
-            pl.BlockSpec((None, group, qb), lambda s, g, i: (g, 0, s * steps + i)),
-            row_spec,
-            row_spec,
-            row_spec,
-            pl.BlockSpec((span, HEAD), lambda s, g, i: (s, g)),
-            pl.BlockSpec((span, HEAD), lambda s, g, i: (s, kv_heads + g)),
-        ],
-        out_specs=[
-            row_spec,
-            pl.BlockSpec((2, stretch, HEAD), lambda s, g, i: (0, s, g)),
-            pl.BlockSpec((held, 2, stretch, HEAD), lambda s, g, i: (0, 0, s, g)),
-        ],
-        out_shape=[
-            jax.ShapeDtypeStruct(q.shape, F32),
-            jax.ShapeDtypeStruct((2, rows, kv_heads * HEAD), F32),
-            jax.ShapeDtypeStruct((held, 2, rows, kv_heads * HEAD), BF),
-        ],
-        scratch_shapes=[pltpu.VMEM((span, HEAD), F32), pltpu.VMEM((span, HEAD), F32)],
-        name=attn_bwd.__name__,
-        cost_estimate=pl.CostEstimate(flops=3 * 10**10, bytes_accessed=12 * 2**20, transcendentals=4 * 2**20),
-        compiler_params=pltpu.CompilerParams(vmem_limit_bytes=62 << 20),
-    )(low, lse, q, d_out, o, window, window)
-
-
 def chunk_index(schedule, s):
     rate, lag, count = schedule
     return jnp.clip((s - lag) // rate, 0, count - 1)
@@ -131,13 +44,7 @@
 WHOLE, HBM = object(), object()
 MLP_WEIGHTS = ("w_gate", "w_up", "w_down")
 QKV_WEIGHTS = ("w_q", "w_k", "w_v")
-GRAD_OPERANDS = ("d_gate_all", "d_up_all", "context_all", "act_all")
-
-
-def of_layer(array, layer):
-    shape = array.shape[1:]
-    zeros = (0,) * len(shape)
-    return array, pl.BlockSpec((None,) + shape, lambda s: (layer,) + zeros, pipeline_mode=pl.Buffered(1))
+GRAD_OPERANDS = ("d_gates_all", "context_all", "act_all")
 
 
 class Row:
@@ -259,9 +166,9 @@
         self.slot = jnp.where(self.middle, 1, 0)
 
     @staticmethod
-    def scratch(rows, width, pieces):
-        return dict(
-            x=pltpu.VMEM((rows, width), BF),
+    def scratch(rows, width, pieces, own=True):
+        held = dict(x=pltpu.VMEM((rows, width), BF)) if own else {}
+        return held | dict(
             land=pltpu.VMEM((2, rows, width), BF),
             send=pltpu.SemaphoreType.DMA((pieces,)),
             arrive=pltpu.SemaphoreType.DMA((2, pieces)),
@@ -348,37 +255,6 @@
             @pl.loop(0, self.pieces)
             def _(j):
                 self.inward(self.x, j, self.slot).wait_send()
-
-
-class Spread(LineSum):
-    @staticmethod
-    def scratch(rows, width, pieces):
-        return dict(
-            land=pltpu.VMEM((2, rows, width), BF),
-            send=pltpu.SemaphoreType.DMA((pieces,)),
-            arrive=pltpu.SemaphoreType.DMA((2, pieces)),
-            out=pltpu.SemaphoreType.DMA((pieces,)),
-        )
-
-    def start(self, other):
-        @pl.when(self.middle)
-        def _():
-            @pl.loop(0, self.pieces)
-            def _(j):
-                self.land[1, self.at(j), :] = (
-                    self.x[self.at(j), :].astype(F32) + other[self.at(j), :].astype(F32)
-                ).astype(BF)
-
-                @pl.when(self.has_outer)
-                def _():
-                    self.outward(j).start()
-
-    def finish(self):
-        @pl.when(self.has_outer)
-        def _():
-            @pl.loop(0, self.pieces)
-            def _(j):
-                self.outward(j).wait_send()
 
 
 class KeyValueSend:
@@ -713,7 +589,7 @@
 def attend_ins(a, low, when):
     return dict(
         queries_in=(a.queries, when),
-        window_in=(a.window, WHOLE),
+        window_in=(a.window, Late()),
         low=(low, WHOLE),
     )
 
@@ -735,9 +611,8 @@
     q_raw = dot(low, r.w_q[...])
     k_raw = dot(low, r.w_k[...])
     values = dot(low, r.w_v[...])
-    r.q_raw[...] = q_raw
-    r.k_raw[...] = k_raw
-    cosine, sine = r.cosine[...], r.sine[...]
+    r.raw[...] = jnp.concatenate([q_raw, k_raw], 1)
+    cosine, sine = r.tables[:, :HEAD], r.tables[:, HEAD:]
 
     def turned(raw, gain):
         return jnp.concatenate(
@@ -752,16 +627,18 @@
     q_width, k_width = w.w_q.shape[2], w.w_k.shape[2]
     return dict(
         attn_low=((rows, width), BF, when),
-        q_raw=((rows, q_width), F32, when),
-        k_raw=((rows, k_width), F32, when),
+        raw=((rows, q_width + k_width), F32, when),
         queries=((rows, q_width), BF, when),
         window=((rows // stretch * (reach + 1) * stretch, k_width + w.w_v.shape[2]), BF, HBM),
     )
 
 
-def project_ins(w, layer, tables, when, late):
+def project_ins(w, layer, tables, when):
     def weight(array):
-        return (array, Late(layer)) if late else of_layer(array, layer)
+        if tables is not None:
+            return array, Late(layer)
+        shape = array.shape[1:]
+        return array, pl.BlockSpec((None,) + shape, lambda s: (layer, 0, 0), pipeline_mode=pl.Buffered(1))
 
     return dict(
         attn_gain=(w.attn_gain, Row(layer)),
@@ -770,7 +647,7 @@
         w_v=weight(w.w_v),
         q_gain=(w.q_gain, Row(layer)),
         k_gain=(w.k_gain, Row(layer)),
-    ) | (dict(cosine=(tables[0], when), sine=(tables[1], when)) if tables else {})
+    ) | ({} if tables is None else dict(tables=(tables, when)))
 
 
 def mlp_gates(r, low):
@@ -784,7 +661,7 @@
     d_act = dot(g_low, r.w_down[...], NT)
     d_gate = (d_act * up * sigma * (1.0 + gate * (1.0 - sigma))).astype(BF)
     d_up = (d_act * gate * sigma).astype(BF)
-    return d_gate, d_up, dot(d_gate, r.w_gate[...], NT) + dot(d_up, r.w_up[...], NT)
+    return jnp.concatenate([d_gate, d_up], 1), dot(d_gate, r.w_gate[...], NT) + dot(d_up, r.w_up[...], NT)
 
 
 def first_projection(hidden, segments, positions, w, stretch, reach, chunks, collective_id):
@@ -817,8 +694,7 @@
         angle = jnp.broadcast_to(r.positions[...].astype(F32), (HEAD, rows // chunks)).T * r.frequency[...]
         lane = lax.broadcasted_iota(jnp.int32, angle.shape, 1)
         sine = jnp.sin(angle)
-        r.cosine[...] = jnp.cos(angle)
-        r.sine[...] = jnp.where(lane < HEAD // 2, -sine, sine)
+        r.tables[...] = jnp.concatenate([jnp.cos(angle), jnp.where(lane < HEAD // 2, -sine, sine)], 1)
         project(r, r.hidden[...].astype(F32), kv, s)
 
         @pl.when(s == chunks - 1)
@@ -849,7 +725,7 @@
                 index = lax.broadcasted_iota(jnp.int32, own.shape, 1)
                 r.low[:, here] = jnp.maximum(low, reach * stretch + index - (WINDOW - 1))
 
-    frequency = THETA ** (-(jnp.arange(HEAD // 2, dtype=F32) * 2.0) / HEAD)
+    frequency = (THETA ** (-np.arange(0, HEAD, 2) / HEAD)).astype(np.float32)
     return step_kernel(
         first_projection, body, chunks,
         dict(
@@ -857,13 +733,12 @@
             segments=(segments.reshape(1, rows), WHOLE),
             positions=(
                 positions.reshape(1, rows), pl.BlockSpec((1, rows // chunks), lambda s: (0, chunk_index(when, s)))),
-            frequency=(jnp.concatenate([frequency, frequency])[None], WHOLE),
+            frequency=(jnp.asarray(np.concatenate([frequency, frequency])[None]), WHOLE),
         )
-        | project_ins(w, 0, None, when, False),
+        | project_ins(w, 0, None, when),
         project_outs(rows, width, w, stretch, reach, when)
         | dict(
-            cosine=((rows, HEAD), F32, when),
-            sine=((rows, HEAD), F32, when),
+            tables=((rows, 2 * HEAD), F32, when),
             low=((1, rows), jnp.int32, WHOLE),
         ),
         dict(
@@ -880,9 +755,9 @@
     rows, width = hidden.shape
     kv_width = w.w_k.shape[2] + w.w_v.shape[2]
     ff = w.w_gate.shape[2]
-    pieces = chunks * PIECES
-    first, second, third = (PIECES, 0, chunks), (PIECES, 4, chunks), (PIECES, 8, chunks)
-    steps = PIECES * (chunks - 1) + third[1] + 1
+    pieces = chunks * FINE
+    first, second, third = (FINE, 0, chunks), (FINE, 8, chunks), (FINE, 17, chunks)
+    steps = FINE * (chunks - 1) + third[1] + 1
     chunk = rows // chunks
 
     def body(r, s):
@@ -905,8 +780,7 @@
             low = (hat * r.mlp_gain[...].astype(F32)).astype(BF)
             r.mlp_low[...] = low
             gate, up, sigma = mlp_gates(r, low)
-            r.gate[...] = gate
-            r.up[...] = up
+            r.gates[...] = jnp.concatenate([gate, up], 1)
             act = (gate * sigma * up).astype(BF)
             r.act[...] = act
             mlp.put(c, dot(act, r.w_down[...]))
@@ -916,13 +790,14 @@
             r.hidden_next[...] = hidden_next
             project(r, hidden_next, kv, c)
 
+        r.arrived(0, "window_in", "w_o")
         at_chunk(s, first, send_attn)
-        at_chunk(s, (1, 1, pieces), attn.relay)
-        at_chunk(s, (1, 2, pieces), attn.meet)
+        at_chunk(s, (1, 2, pieces), attn.relay)
+        at_chunk(s, (1, 4, pieces), attn.meet)
         r.arrived(second[1], *MLP_WEIGHTS)
         at_chunk(s, second, feed_forward)
-        at_chunk(s, (1, 6, pieces), mlp.relay)
-        at_chunk(s, (1, 7, pieces), mlp.meet)
+        at_chunk(s, (1, 12, pieces), mlp.relay)
+        at_chunk(s, (1, 14, pieces), mlp.meet)
         r.arrived(third[1], *QKV_WEIGHTS)
         at_chunk(s, third, next_layer)
 
@@ -936,20 +811,19 @@
         between_forward, body, steps,
         attend_ins(a, low, first)
         | dict(
-            w_o=of_layer(w.w_o, layer),
+            w_o=(w.w_o, Late(layer)),
             hidden=(hidden, second),
             mlp_gain=(w.mlp_gain, Row(layer)),
             w_gate=(w.w_gate, Late(layer)),
             w_up=(w.w_up, Late(layer)),
             w_down=(w.w_down, Late(layer)),
         )
-        | project_ins(w, layer + 1, tables, third, True),
+        | project_ins(w, layer + 1, tables, third),
         attend_outs(a, first)
         | dict(
             hidden_mid=((rows, width), F32, second),
             mlp_low=((rows, width), BF, second),
-            gate=((rows, ff), F32, second),
-            up=((rows, ff), F32, second),
+            gates=((rows, 2 * ff), F32, second),
             act=((rows, ff), BF, second),
             hidden_next=((rows, width), F32, third),
         )
@@ -967,9 +841,9 @@
     hidden = a.hidden
     rows, width = hidden.shape
     ff = w.w_gate.shape[2]
-    pieces = chunks * PIECES
-    first, second, third = (PIECES, 0, chunks), (PIECES, 6, chunks), (PIECES, 12, chunks)
-    steps = PIECES * (chunks - 1) + third[1] + 1
+    pieces = chunks * FINE
+    first, second, third = (FINE, 0, chunks), (FINE, 9, chunks), (FINE, 17, chunks)
+    steps = FINE * (chunks - 1) + third[1] + 1
     chunk = rows // chunks
 
     def body(r, s):
@@ -991,10 +865,9 @@
             low = (hat * r.mlp_gain[...].astype(F32)).astype(BF)
             r.mlp_low[...] = low
             gate, up, sigma = mlp_gates(r, low)
-            d_gate, d_up, part = mlp_back(r, r.cotangent[...], gate, up, sigma)
+            d_gates, part = mlp_back(r, r.cotangent[...], gate, up, sigma)
             back.put(c, part)
-            r.d_gate[...] = d_gate
-            r.d_up[...] = d_up
+            r.d_gates[...] = d_gates
             act = (gate * sigma * up).astype(BF)
             r.act[...] = act
             part = dot(act, r.w_down[...]).astype(BF)
@@ -1017,13 +890,14 @@
             r.mid_low[...] = mid_low
             r.d_context[...] = dot(mid_low, r.w_o[...], NT).astype(BF)
 
+        r.arrived(0, "window_in", "w_o")
         at_chunk(s, first, send_attn)
-        at_chunk(s, (1, 3, pieces), attn.relay)
+        at_chunk(s, (1, 2, pieces), attn.relay)
         at_chunk(s, (1, 4, pieces), attn.meet)
         r.arrived(second[1], *MLP_WEIGHTS)
         at_chunk(s, second, feed_forward)
-        at_chunk(s, (1, 9, pieces), back.relay)
-        at_chunk(s, (1, 10, pieces), back.meet)
+        at_chunk(s, (1, 12, pieces), back.relay)
+        at_chunk(s, (1, 14, pieces), back.meet)
         at_chunk(s, third, middle_grad)
 
         @pl.when(s == steps - 1)
@@ -1035,7 +909,7 @@
         turn_around, body, steps,
         attend_ins(a, low, first)
         | dict(
-            w_o=of_layer(w.w_o, layer),
+            w_o=(w.w_o, Late(layer)),
             hidden=(hidden, second),
             cotangent=(cotangent, second),
             cotangent_late=(cotangent, third),
@@ -1049,10 +923,9 @@
             mlp_low=((rows, width), BF, second),
             act=((rows, ff), BF, second),
             hidden_mid=((rows, width), F32, second),
-            lower_part=((rows // 2, width), BF, (PIECES, second[1], chunks // 2)),
-            upper_part=((rows // 2, width), BF, (PIECES, second[1] + PIECES * (chunks // 2), chunks // 2)),
-            d_gate=((rows, ff), BF, second),
-            d_up=((rows, ff), BF, second),
+            lower_part=((rows // 2, width), BF, (FINE, second[1], chunks // 2)),
+            upper_part=((rows // 2, width), BF, (FINE, second[1] + FINE * (chunks // 2), chunks // 2)),
+            d_gates=((rows, 2 * ff), BF, second),
             g_mid=((rows, width), F32, third),
             mid_low=((rows, width), BF, third),
             d_context=(a.queries.shape, BF, third),
@@ -1066,8 +939,125 @@
         collective_id)
 
 
+def attention_backward(a, d_context, low, part, quarter, stretch, pieces, collective_id):
+    rows = a.queries.shape[0]
+    kv_heads = a.window.shape[1] // (2 * HEAD)
+    width = a.queries.shape[1] // kv_heads
+    group = width // HEAD
+    qb = min(2 * CHUNK, stretch)
+    count = stretch // qb
+    seqs = rows // stretch
+    span = a.window.shape[0] // seqs
+    reach = span // stretch - 1
+    held = max(reach, 1)
+    offset = reach * stretch
+    length = min(WINDOW + qb, span)
+    steps = seqs * kv_heads * count
+
+    def places(s):
+        return s // (kv_heads * count), lax.rem(s // count, kv_heads), lax.rem(s, count)
+
+    def block(shape, index):
+        return pl.BlockSpec(shape, lambda s: index(*places(s)))
+
+    def body(r, s):
+        seq, g, i = places(s)
+        line = LineSum(r.line, r.part)
+        q_start = i * qb + offset
+        start = jnp.clip(q_start + qb - length, 0, span - length)
+        here = pl.ds(pl.multiple_of(start, HEAD), length)
+
+        @pl.when(s == 0)
+        def _():
+            enter(line.neighbours())
+            line.push(0, line.x.shape[0])
+
+        @pl.when(i == 0)
+        def _():
+            r.d_keys[...] = jnp.zeros_like(r.d_keys)
+            r.d_values[...] = jnp.zeros_like(r.d_values)
+
+        for j in range(pieces):
+
+            @pl.when(s == min(2 + j // 2, steps - 1))
+            def _():
+                line.relay(j)
+
+        for j in range(pieces):
+
+            @pl.when(s == min(4 + j // 2, steps - 1))
+            def _():
+                line.meet(j)
+
+        def stack(ref):
+            return jnp.concatenate([ref[:, h * HEAD : (h + 1) * HEAD] for h in range(group)], 0)
+
+        queries = stack(r.queries)
+        d_out = stack(r.d_context)
+        lse = jnp.concatenate([r.lse[h : h + 1, :] for h in range(group)], 1)
+        product = d_out.astype(F32) * stack(r.context).astype(F32)
+        delta = jnp.sum(product.T, 0, keepdims=True)
+        keys = r.keys[here, :]
+        values = r.values[here, :]
+        key_index = start + lax.broadcasted_iota(jnp.int32, (length, qb), 0)
+        q_index = q_start + lax.broadcasted_iota(jnp.int32, (1, qb), 1)
+        mask = (key_index >= r.low[...]) & (key_index <= q_index)
+        mask = jnp.concatenate([mask] * group, 1)
+        scores = dot(keys, queries, NT) * (SCALE * LOG2E) - lse
+        p = jnp.where(mask, jnp.exp2(scores), 0.0)
+        ds = (p * (dot(values, d_out, NT) - delta)).astype(BF)
+        r.d_values[here, :] += dot(p.astype(BF), d_out)
+        r.d_keys[here, :] += dot(ds, queries)
+        dq = (dot(keys, ds, TN) * SCALE).T
+        for h in range(group):
+            r.d_q[:, h * HEAD : (h + 1) * HEAD] = dq[h * qb : (h + 1) * qb]
+
+        @pl.when(i == count - 1)
+        def _():
+            r.d_own[0] = r.d_keys[offset:, :] * SCALE
+            r.d_own[1] = r.d_values[offset:, :]
+            for j in range(reach):
+                r.d_prev[j, 0] = (r.d_keys[j * stretch : (j + 1) * stretch, :] * SCALE).astype(BF)
+                r.d_prev[j, 1] = r.d_values[j * stretch : (j + 1) * stretch, :].astype(BF)
+
+        @pl.when(s == steps - 1)
+        def _():
+            r.total[...] = line.total(0, line.x.shape[0]).astype(BF)
+            line.finish()
+
+    by_rows = block((qb, width), lambda seq, g, i: (seq * count + i, g))
+    part_rows = part.shape[0] // 2
+    return step_kernel(
+        attention_backward, body, steps,
+        dict(
+            low=(low, block((1, qb), lambda seq, g, i: (0, seq * count + i))),
+            lse=(a.lse, block((None, group, qb), lambda seq, g, i: (g, 0, seq * count + i))),
+            queries=(a.queries, by_rows),
+            d_context=(d_context, by_rows),
+            context=(a.context, by_rows),
+            keys=(a.window, block((span, HEAD), lambda seq, g, i: (seq, g))),
+            values=(a.window, block((span, HEAD), lambda seq, g, i: (seq, kv_heads + g))),
+            part=(part, pl.BlockSpec(
+                (part_rows, part.shape[1]), lambda s: (quarter, 0), pipeline_mode=pl.Buffered(1))),
+        ),
+        dict(
+            d_q=(a.queries.shape, F32, by_rows),
+            d_own=((2, rows, kv_heads * HEAD), F32, block((2, stretch, HEAD), lambda seq, g, i: (0, seq, g))),
+            d_prev=(
+                (held, 2, rows, kv_heads * HEAD), BF,
+                block((held, 2, stretch, HEAD), lambda seq, g, i: (0, 0, seq, g))),
+            total=((part_rows, part.shape[1]), BF, WHOLE),
+        ),
+        dict(
+            line=LineSum.scratch(part_rows, part.shape[1], pieces, False),
+            d_keys=pltpu.VMEM((span, HEAD), F32),
+            d_values=pltpu.VMEM((span, HEAD), F32),
+        ),
+        collective_id)
+
+
 def attention_grads(r, back, line, c):
-    cosine, sine = r.cosine[...], r.sine[...]
+    cosine, sine = r.tables[:, :HEAD], r.tables[:, HEAD:]
     both = back.add(r.d_own[...], c)
 
     def raw_back(grads, raws, gain):
@@ -1079,8 +1069,9 @@
             lows.append(norm_back(grad, gain, hat, inverse).astype(BF))
         return jnp.concatenate(lows, 1), gains
 
-    d_q, q_gain = raw_back(r.d_q[...], r.q_raw[...], r.q_gain[...].astype(F32))
-    d_k, k_gain = raw_back(both[0], r.k_raw[...], r.k_gain[...].astype(F32))
+    q_width = r.d_q.shape[1]
+    d_q, q_gain = raw_back(r.d_q[...], r.raw[:, :q_width], r.q_gain[...].astype(F32))
+    d_k, k_gain = raw_back(both[0], r.raw[:, q_width:], r.k_gain[...].astype(F32))
     d_v = both[1].astype(BF)
     r.head_gain[0:1, 0:HEAD] += q_gain
     r.head_gain[0:1, HEAD : 2 * HEAD] += k_gain
@@ -1121,25 +1112,22 @@
 
     def mlp_slab(self, slab):
         r = self.r
-        ff = r.d_gate_all.shape[1]
+        ff = r.act_all.shape[1]
         q_width = r.context_all.shape[1]
-        mlp_low = r.mlp_low_slab[...]
-        self.put(self.early[0], slab, slice(0, ff), dot(mlp_low, r.d_gate_all[...], TN))
+        both = dot(r.mlp_low_slab[...], r.d_gates_all[...], TN)
+        self.put(self.early[0], slab, slice(0, ff), both[:, :ff])
         self.put(self.early[0], slab, slice(ff, ff + q_width), dot(r.mid_low_slab[...], r.context_all[...], TN))
-        self.put(self.early[1], slab, slice(0, ff), dot(mlp_low, r.d_up_all[...], TN))
+        self.put(self.early[1], slab, slice(0, ff), both[:, ff:])
         self.put(self.early[1], slab, slice(ff, 2 * ff), dot(r.g_low_slab[...], r.act_all[...], TN))
 
-    def qkv_slabs(self, begin, end):
+    def qkv_slab(self, slab):
         r = self.r
         slab_width = r.attn_low_all.shape[1] // self.slabs
         q_width = r.d_q.shape[1]
-
-        @pl.loop(begin, end)
-        def _(slab):
-            columns = pl.ds(pl.multiple_of(slab * slab_width, slab_width), slab_width)
-            value = dot(r.attn_low_all[:, columns], r.d_held[...], TN)
-            self.put(self.late[0], slab, slice(None), value[:, :q_width])
-            self.put(self.late[1], slab, slice(None), value[:, q_width:])
+        columns = pl.ds(pl.multiple_of(slab * slab_width, slab_width), slab_width)
+        value = dot(r.attn_low_all[:, columns], r.d_held[...], TN)
+        self.put(self.late[0], slab, slice(None), value[:, :q_width])
+        self.put(self.late[1], slab, slice(None), value[:, q_width:])
 
     def each(self, scatters, work):
         for scatter in scatters:
@@ -1148,8 +1136,8 @@
     def store(self):
         r = self.r
         last = len(block_axes()) - 1
-        ff = r.d_gate_all.shape[1]
-        k_width = r.k_raw.shape[1]
+        ff = r.act_all.shape[1]
+        k_width = r.grad_k.shape[1]
 
         def store_a(total):
             r.grad_gate[...] = total[:, :ff]
@@ -1172,14 +1160,11 @@
         self.late[1].fold(last, store_kv)
 
     def late_slabs(self, s):
-        for i in range(2):
-            self.r.arrived(self.plan.late_slabs[0], "attn_low_all") if i == 0 else None
-
-            @pl.when(s == self.plan.late_slabs[i])
-            def _():
-                self.qkv_slabs(i * self.slabs // 2, (i + 1) * self.slabs // 2)
-
-        @pl.when(s == self.plan.late_slabs[1])
+        _, lag, count = self.plan.late_slabs
+        self.r.arrived(lag, "attn_low_all")
+        at_chunk(s, self.plan.late_slabs, self.qkv_slab)
+
+        @pl.when(s == lag + count - 1)
         def _():
             self.each(self.late, lambda scatter: scatter.send(0))
 
@@ -1221,8 +1206,7 @@
         mid_low_slab=(a.mid_low, slab),
         g_low_slab=(a.g_low, slab),
         attn_low_all=(a.attn_low, Late()),
-        d_gate_all=(a.d_gate, Late()),
-        d_up_all=(a.d_up, Late()),
+        d_gates_all=(a.d_gates, Late()),
         context_all=(a.context, Late()),
         act_all=(a.act, Late()),
     )
@@ -1242,19 +1226,17 @@
 
 
 def attention_grads_ins(a, w, layer, tables, when):
-    rows, k_width = a.k_raw.shape
+    rows, k_width = a.raw.shape[0], w.w_k.shape[2]
     own = pl.BlockSpec((2, rows // when[2], k_width), lambda s: (0, chunk_index(when, s), 0))
     return dict(
         d_q=(a.d_q, when),
         d_own=(a.d_own, own),
         d_prev=(a.d_prev, HBM),
-        q_raw=(a.q_raw, when),
-        k_raw=(a.k_raw, when),
-        cosine=(tables[0], when),
-        sine=(tables[1], when),
-        w_q=of_layer(w.w_q, layer),
-        w_k=of_layer(w.w_k, layer),
-        w_v=of_layer(w.w_v, layer),
+        raw=(a.raw, when),
+        tables=(tables, when),
+        w_q=(w.w_q, Late(layer)),
+        w_k=(w.w_k, Late(layer)),
+        w_v=(w.w_v, Late(layer)),
         q_gain=(w.q_gain, Row(layer)),
         k_gain=(w.k_gain, Row(layer)),
         attn_gain=(w.attn_gain, Row(layer)),
@@ -1272,8 +1254,8 @@
     plan = types.SimpleNamespace(
         slabs=(PIECES, 2, slab_count(chunks)),
         early=lambda k: min(after - 3 + 4 * k, steps - 2),
-        late_slabs=(after, after + 1),
-        late=lambda k: min(after + 3 + 2 * k, steps - 2),
+        late_slabs=(1, after, slab_count(chunks)),
+        late=lambda k: min(after + slab_count(chunks) + 2 * k, steps - 2),
     )
 
     def body(r, s):
@@ -1299,10 +1281,9 @@
             r.g_held[lax.rem(c, 4)] = g
             g_low = g.astype(BF)
             r.g_low[...] = g_low
-            gate = r.gate[...]
-            d_gate, d_up, part = mlp_back(r, g_low, gate, r.up[...], jax.nn.sigmoid(gate))
-            r.d_gate[...] = d_gate
-            r.d_up[...] = d_up
+            gate, up = r.gates[:, :ff], r.gates[:, ff:]
+            d_gates, part = mlp_back(r, g_low, gate, up, jax.nn.sigmoid(gate))
+            r.d_gates[...] = d_gates
             mlp.put(c, part)
 
         def middle_grad(c):
@@ -1315,6 +1296,7 @@
             r.mid_low[...] = mid_low
             r.d_context[...] = dot(mid_low, r.w_o[...], NT).astype(BF)
 
+        r.arrived(first[1], *QKV_WEIGHTS)
         at_chunk(s, first, send_attn)
         grads.late_slabs(s)
         at_chunk(s, (1, 1, pieces), attn.relay)
@@ -1342,8 +1324,7 @@
         | dict(
             hidden=(a.hidden, second),
             g_above=(g_mid, second),
-            gate=(below.gate, second),
-            up=(below.up, second),
+            gates=(below.gates, second),
             hidden_mid=(below.hidden_mid, third),
             mlp_gain=(w.mlp_gain, Row(layer - 1)),
             w_gate=(w.w_gate, Late(layer - 1)),
@@ -1353,8 +1334,7 @@
         ),
         dict(
             g_low=((rows, width), BF, second),
-            d_gate=((rows, ff), BF, second),
-            d_up=((rows, ff), BF, second),
+            d_gates=((rows, 2 * ff), BF, second),
             g_mid=((rows, width), F32, third),
             mid_low=((rows, width), BF, third),
             d_context=((rows, q_width), BF, third),
@@ -1372,7 +1352,7 @@
         collective_id)
 
 
-def last_backward(a, top, top_halves, above, w, tables, reach, chunks, collective_id):
+def last_backward(a, top, quarters, above, w, tables, reach, chunks, collective_id):
     g_mid = above.g_mid
     rows, width = g_mid.shape
     q_width, k_width, ff = w.w_q.shape[2], w.w_k.shape[2], w.w_gate.shape[2]
@@ -1381,20 +1361,24 @@
     pairs = max(1, chunks // 2)
     half = rows // 2
     half_pieces = pieces // 2
-    first, second, third = (PIECES, 0, pairs), (PIECES, 8, chunks), (PIECES, 5, chunks)
+    out_chunk = min(rows // chunks, half // 2)
+    out_count = rows // out_chunk
+    first, second = (2, 2, pairs), (PIECES, 15, chunks)
+    third = (PIECES * chunks // out_count, 12, out_count)
     steps = PIECES * (chunks - 1) + second[1] + 1
     chunk = rows // chunks
-    after = PIECES * pairs
+    after = 2 * pairs
+    slabs = slab_count(chunks)
     plan = types.SimpleNamespace(
-        slabs=(PIECES, 1, slab_count(chunks)),
-        early=lambda k: min(after + 1 + 4 * k, steps - 2),
-        late_slabs=(after, after + 1),
-        late=lambda k: min(after + 5 + 5 * k, steps - 2),
+        slabs=(1, 9, slabs),
+        early=lambda k: min(slabs + 12 + 7 * k, steps - 2),
+        late_slabs=(1, after + 8, slabs),
+        late=lambda k: min(after + 10 + slabs + 5 * k, steps - 2),
     )
 
     def body(r, s):
         back = KeyValueReturn(r, reach)
-        attn, upper, lower = LineSum(r.attn), LineSum(r.upper, r.upper_part), Spread(r.lower, r.lower_here)
+        attn, upper = LineSum(r.attn), LineSum(r.upper, r.upper_part)
         grads = WeightGrads(r, plan)
         sums = Butterfly(r.sums)
 
@@ -1402,7 +1386,7 @@
         def _():
             enter(attn.neighbours() + back.neighbours() + sums.neighbours())
             back.start()
-            lower.start(r.lower_there)
+            upper.push(0, half)
             r.head_gain[...] = jnp.zeros_like(r.head_gain)
             r.gain_held[...] = jnp.zeros_like(r.gain_held)
 
@@ -1412,33 +1396,35 @@
             r.gain_held[...] += row_sums(part * hat)
 
         def give_output(c):
-            @pl.when(c < chunks // 2)
+            per = out_count // 4
+            for q in range(2):
+
+                @pl.when((c >= q * per) & (c < (q + 1) * per))
+                def _():
+                    here = pl.ds(pl.multiple_of(jnp.clip(c - q * per, 0, per - 1) * out_chunk, out_chunk), out_chunk)
+                    total = (r.quarter_0, r.quarter_1)[q][here, :].astype(F32)
+                    r.output[...] = (r.hidden_mid[...] + total).astype(BF)
+
+            @pl.when(c >= 2 * per)
             def _():
-                r.output[...] = (r.hidden_mid[...] + lower.total(c, chunk)).astype(BF)
-
-            @pl.when(c >= chunks // 2)
-            def _():
-                r.output[...] = (r.hidden_mid[...] + upper.total(c - chunks // 2, chunk)).astype(BF)
-
-        def push_upper(j):
-            upper.push(j, 2 * upper.rows)
+                r.output[...] = (r.hidden_mid[...] + upper.total(c - 2 * per, out_chunk)).astype(BF)
 
         def give_input(c):
             hat, inverse = norm_parts(r.hidden_late[...].astype(F32))
             r.input_grad[...] = r.g_above[...] + norm_back(attn.total(c, chunk), r.attn_gain[...].astype(F32), hat, inverse)
 
-        at_chunk(s, (1, 0, half_pieces // 2), push_upper)
+        r.arrived(first[1], *QKV_WEIGHTS)
         at_chunk(s, first, send_attn)
         grads.late_slabs(s)
-        at_chunk(s, (1, 3, half_pieces), upper.relay)
-        at_chunk(s, (1, 3, pieces), attn.relay)
-        at_chunk(s, (1, 5, half_pieces), upper.meet)
-        at_chunk(s, (1, 5, pieces), attn.meet)
+        at_chunk(s, (1, 2, half_pieces), upper.relay)
+        at_chunk(s, (1, 9, pieces), attn.relay)
+        at_chunk(s, (1, 4, half_pieces), upper.meet)
+        at_chunk(s, (1, 12, pieces), attn.meet)
         at_chunk(s, third, give_output)
         at_chunk(s, second, give_input)
         grads.run(s)
 
-        @pl.when(s == after)
+        @pl.when(s == after + 1)
         def _():
             row = lax.broadcasted_iota(jnp.int32, (8, width), 0)
             once = jnp.where(lax.axis_index("tensor") == 0, 1.0, 0.0)
@@ -1453,7 +1439,7 @@
 
         for k in range(len(sums.axes)):
 
-            @pl.when(s == min(after + 2 + 2 * k, steps - 1))
+            @pl.when(s == max(steps - len(sums.axes) - 4 + k, after + 2))
             def _():
                 sums.fold(k)
 
@@ -1463,7 +1449,6 @@
             r.gains[...] = sums.total()
             attn.finish()
             upper.finish()
-            lower.finish()
             back.finish()
             grads.finish()
             sums.finish()
@@ -1480,8 +1465,8 @@
             above_head_gain=(above.head_gain, WHOLE),
             top_gain=(top.gain_grad, WHOLE),
             upper_part=(top.upper_part, WHOLE),
-            lower_here=(top_halves[0], WHOLE),
-            lower_there=(top_halves[1], WHOLE),
+            quarter_0=(quarters[0], WHOLE),
+            quarter_1=(quarters[1], WHOLE),
             hidden_mid=(top.hidden_mid, third),
         ),
         dict(
@@ -1492,8 +1477,7 @@
         | grads_outs(width, q_width, k_width, ff),
         dict(
             attn=LineSum.scratch(rows, width, pieces),
-            upper=Spread.scratch(half, width, half_pieces),
-            lower=Spread.scratch(half, width, half_pieces),
+            upper=LineSum.scratch(half, width, half_pieces, False),
             kr=KeyValueReturn.scratch(rows, k_width, pairs, reach),
             **WeightGrads.scratch(rows, width, q_width, k_width, ff),
             sums=Butterfly.scratch((8, width)),
@@ -1535,7 +1519,7 @@
     straight = [(k.grad_q, k.grad_k, k.grad_v, k.grad_gate, k.grad_up) for k in (end, above)]
     turned = [(k.grad_o, k.grad_down) for k in (end, above)]
     per = straight[0][0].shape[0]
-    steps = max(1, min(8, per // 8))
+    steps = max(1, min(2, per // 8))
     whole = pl.BlockSpec(memory_space=pltpu.VMEM)
 
     def blocks(array):
@@ -1567,16 +1551,6 @@
     )(*ins)
 
 
-def middle_terms(part):
-    n = lax.axis_size("tensor")
-    half = n // 2
-    total = part
-    for hop in range(half - 1):
-        moved = lax.ppermute(total, "tensor", [(hop, hop + 1), (n - 1 - hop, n - 2 - hop)])
-        total = (part.astype(F32) + moved.astype(F32)).astype(BF)
-    return total, lax.ppermute(total, "tensor", [(half - 1, half), (half, half - 1)])
-
-
 def per_device(
     tokens, cotangent, segments, positions, attn_gain, w_query, key_projection, value_projection, query_gain, key_gain,
     w_output, mlp_gain, w_gate, w_up, w_down,
@@ -1593,28 +1567,29 @@
     tokens = tokens.reshape(rows, width)
     cotangent = cotangent.reshape(rows, width)
 
-    a0 = first_projection(tokens, segments, positions, w, stretch, reach, chunks, 1)
-    tables, low = (a0.cosine, a0.sine), a0.low
+    a0 = first_projection(tokens, segments, positions, w, stretch, reach, rows // min(2 * CHUNK, stretch), 1)
+    tables, low = a0.tables, a0.low
     a0.hidden = tokens
     mid = between_forward(a0, low, w, 0, tables, stretch, reach, chunks, 2)
     a0.context, a0.lse = mid.context, mid.lse
     a1 = types.SimpleNamespace(
-        attn_low=mid.attn_low, q_raw=mid.q_raw, k_raw=mid.k_raw, queries=mid.queries, window=mid.window,
+        attn_low=mid.attn_low, raw=mid.raw, queries=mid.queries, window=mid.window,
         hidden=mid.hidden_next)
     turn = turn_around(a1, low, cotangent, w, 1, stretch, chunks, 3)
     a1.context, a1.lse = turn.context, turn.lse
-    top_halves = middle_terms(turn.lower_part)
-    a1.mlp_low, a1.act, a1.d_gate, a1.d_up = turn.mlp_low, turn.act, turn.d_gate, turn.d_up
+    a1.mlp_low, a1.act, a1.d_gates = turn.mlp_low, turn.act, turn.d_gates
     a1.mid_low, a1.g_low = turn.mid_low, cotangent
-    a1.d_q, a1.d_own, a1.d_prev = attn_bwd(
-        a1.queries, turn.d_context, a1.context, a1.window, low, a1.lse, stretch)
+    pieces = chunks * FINE // 4
+    back = attention_backward(a1, turn.d_context, low, turn.lower_part, 0, stretch, pieces, 6)
+    a1.d_q, a1.d_own, a1.d_prev = back.d_q, back.d_own, back.d_prev
+    quarters = [back.total]
     down = between_backward(a1, mid, turn.g_mid, w, 1, tables, reach, chunks, 4)
-    a0.mlp_low, a0.act, a0.d_gate, a0.d_up = mid.mlp_low, mid.act, down.d_gate, down.d_up
+    a0.mlp_low, a0.act, a0.d_gates = mid.mlp_low, mid.act, down.d_gates
     a0.mid_low, a0.g_low = down.mid_low, down.g_low
-    a0.d_q, a0.d_own, a0.d_prev = attn_bwd(
-        a0.queries, down.d_context, a0.context, a0.window, low, a0.lse, stretch)
-
-    end = last_backward(a0, turn, top_halves, down, w, tables, reach, chunks, 5)
+    back = attention_backward(a0, down.d_context, low, turn.lower_part, 1, stretch, pieces, 7)
+    a0.d_q, a0.d_own, a0.d_prev = back.d_q, back.d_own, back.d_prev
+    quarters.append(back.total)
+    end = last_backward(a0, turn, quarters, down, w, tables, reach, chunks, 5)
     output, input_grad, attn, mlp, q_gain, k_gain, d_q, d_k, d_v, d_gate, d_up, d_o, d_down = collect(end, down)
     shape = (seqs_here, stretch, width)
     return (

time: 526 us -> 516 us (0.981)
    pallas_call x2 -> x0, Pallas kernels: 40.2 us -> none  [attn_bwd(): pl.pallas_call(functools.partial(attn_bwd_kernel, reach * stretch), grid=...]
    pallas_call x5 -> x7, Pallas kernels: 466 us -> 506 us  [step_kernel(): pl.pallas_call(kernel, grid=(steps,), in_specs=[spec(a.shape, w, True) fo...]
  transfers between devices with their start and end apart: 2 -> 0, of which waited for: 0 -> 0; matrix products, arithmetic and copies ran while one was open for 0% -> 0% of each run, Pallas kernels for 30% -> 0%
where the time goes in v4:
time: 516 us; the launch traced here: 515 us
  Pallas kernels  514 us (100%)
    pallas_call x7, Pallas kernels, step_kernel(): pl.pallas_call(kernel, grid=(steps,), in_specs=[spec(a.shape, w, True) fo...  506 us

profile of v4, /device:TPU:0, one launch (start us, length us, event | category | flops | bytes accessed | tf_op | source)
XLA Modules:
  0.0 514.7 jit_solution(14754906363690602862)
XLA Ops:
  0.6 10.8 %first_projection.1 = (bf16[1024,1024]{1,0:T(8,128)(2,1)}, f32[1024,768]{1,0:T(8,128)}, bf16[1024,512]{1,0:T(8,128)(2,1)}, bf16[2048,512]{1,0:T(8,128)(2,1)}, f32[1024,256]{1,0:T(8,128)}, /*index=5*/s32[1,1024]{1,0:T(1,128)}) custom-call(bf16[1024,1024]{1,0:T(8,128)(2,1)} %bitcast.4, s32[1,1024]{1,0:T(1,128)} %refs_1_.1, s32[1,1024]{1,0:T(1,128)} %refs_2_.1, ...), custom_call_target="tpu_custom_call" | custom-call | tf_op jit(solution)/shard_map/first_projection/pallas_call | solution.py:109
  11.5 116.0 %between_forward.1 = (bf16[1024,512]{1,0:T(8,128)(2,1)}, f32[2,2,1024]{2,1,0:T(2,128)}, f32[1024,1024]{1,0:T(8,128)}, bf16[1024,1024]{1,0:T(8,128)(2,1)}, f32[10...) custom-call(bf16[1024,512]{1,0:T(8,128)(2,1)} %get-tuple-element.88., ...), custom_call_target="tpu_custom_call" | custom-call | tf_op jit(solution)/shard_map/between_forward/pallas_call | solution.py:109
  127.5 115.8 %turn_around.1 = (bf16[1024,512]{1,0:T(8,128)(2,1)}, f32[2,2,1024]{2,1,0:T(2,128)}, bf16[1024,1024]{1,0:T(8,128)(2,1)}, bf16[1024,768]{1,0:T(8,128)(2,1)}, f32[1...) custom-call(bf16[1024,512]{1,0:T(8,128)(2,1)} %get-tuple-element.92., ...), custom_call_target="tpu_custom_call" | custom-call | tf_op jit(solution)/shard_map/turn_around/pallas_call | solution.py:109
  243.3 24.8 %attention_backward.2 = (f32[1024,512]{1,0:T(8,128)}, f32[2,1024,256]{2,1,0:T(8,128)}, bf16[1,2,1024,256]{3,2,1,0:T(8,128)(2,1)}, bf16[256,1024]{1,0:T(8,128)(2,1)}) custom-call(s32[1,1024]{1,0:T(1,128)} %get-tuple-element.87.refs_2_.refs_0_, f32[2,2,1024]{2,1,0:T(2,128)} %get-tuple-element.95.refs_1_, bf16[1024,512]{1,0:T(8,128)(2,1)} %get-tuple-element.92.refs_0_.refs_2_, ...), custom_call_target="tpu_custom_call" | custom-call | tf_op jit(solution)/shard_map/attention_backward/pallas_call | solution.py:109
  268.1 118.2 %between_backward.1 = (bf16[1024,1024]{1,0:T(8,128)(2,1)}, bf16[1024,1536]{1,0:T(8,128)(2,1)}, f32[1024,1024]{1,0:T(8,128)}, bf16[1024,1024]{1,0:T(8,128)(2,1)},...) custom-call(f32[1024,512]{1,0:T(8,128)} %get-tuple-element.99.refs_0, ...), custom_call_target="tpu_custom_call" | custom-call | tf_op jit(solution)/shard_map/between_backward/pallas_call | solution.py:109
  386.3 25.4 %attention_backward.3 = (f32[1024,512]{1,0:T(8,128)}, f32[2,1024,256]{2,1,0:T(8,128)}, bf16[1,2,1024,256]{3,2,1,0:T(8,128)(2,1)}, bf16[256,1024]{1,0:T(8,128)(2,1)}) custom-call(s32[1,1024]{1,0:T(1,128)} %get-tuple-element.87.refs_2_.refs_0_, f32[2,2,1024]{2,1,0:T(2,128)} %get-tuple-element.91.refs_1_, bf16[1024,512]{1,0:T(8,128)(2,1)} %get-tuple-element.88.refs_0_.refs_2_, ...), custom_call_target="tpu_custom_call" | custom-call | tf_op jit(solution)/shard_map/attention_backward/pallas_call | solution.py:109
  411.7 94.8 %last_backward.1 = (f32[1024,1024]{1,0:T(8,128)}, bf16[1024,1024]{1,0:T(8,128)(2,1)}, f32[8,1024]{1,0:T(8,128)}, f32[128,512]{1,0:T(8,128)}, f32[128,256]{1,0:T(...) custom-call(f32[1024,512]{1,0:T(8,128)} %get-tuple-element.113.refs_, ...), custom_call_target="tpu_custom_call" | custom-call | tf_op jit(solution)/shard_map/last_backward/pallas_call | solution.py:109
  506.6 8.0 %collect.1 = (bf16[1024,1024]{1,0:T(8,128)(2,1)}, f32[1024,1024]{1,0:T(8,128)}, f32[2,1024]{1,0:T(2,128)}, f32[2,1024]{1,0:T(2,128)}, f32[2,128]{1,0:T(2,128)}, ...) custom-call(bf16[1024,1024]{1,0:T(8,128)(2,1)} %get-tuple-element.13, ...), custom_call_target="tpu_custom_call" | custom-call | tf_op jit(solution)/shard_map/collect/pallas_call | solution.py:1543

commit v5 on v4

--- a/solution.py
+++ b/solution.py
@@ -1247,15 +1247,16 @@
     rows, width = g_mid.shape
     q_width, k_width, ff = w.w_q.shape[2], w.w_k.shape[2], w.w_gate.shape[2]
     pieces = chunks * PIECES
-    first, second, third = (PIECES, 0, chunks), (PIECES, 4, chunks), (PIECES, 10, chunks)
+    first, second, third = (PIECES, 0, chunks), (PIECES, 5, chunks), (PIECES, 11, chunks)
     steps = PIECES * (chunks - 1) + third[1] + 1
     chunk = rows // chunks
     after = PIECES * (chunks - 1) + 1
+    slabs = slab_count(chunks)
     plan = types.SimpleNamespace(
-        slabs=(PIECES, 2, slab_count(chunks)),
-        early=lambda k: min(after - 3 + 4 * k, steps - 2),
-        late_slabs=(1, after, slab_count(chunks)),
-        late=lambda k: min(after + slab_count(chunks) + 2 * k, steps - 2),
+        slabs=(2, 2, slabs),
+        early=lambda k: min(4 + 2 * slabs + 4 * k, steps - 2),
+        late_slabs=(1, after, slabs),
+        late=lambda k: min(after + slabs + 2 * k, steps - 2),
     )
 
     def body(r, s):
@@ -1299,12 +1300,12 @@
         r.arrived(first[1], *QKV_WEIGHTS)
         at_chunk(s, first, send_attn)
         grads.late_slabs(s)
-        at_chunk(s, (1, 1, pieces), attn.relay)
-        at_chunk(s, (1, 2, pieces), attn.meet)
+        at_chunk(s, (1, 2, pieces), attn.relay)
+        at_chunk(s, (1, 3, pieces), attn.meet)
         r.arrived(second[1], *MLP_WEIGHTS)
         at_chunk(s, second, feed_forward)
-        at_chunk(s, (1, 6, pieces), mlp.relay)
-        at_chunk(s, (1, 7, pieces), mlp.meet)
+        at_chunk(s, (1, 7, pieces), mlp.relay)
+        at_chunk(s, (1, 8, pieces), mlp.meet)
         r.arrived(third[1], "w_o")
         at_chunk(s, third, middle_grad)
         grads.run(s)
@@ -1363,17 +1364,17 @@
     half_pieces = pieces // 2
     out_chunk = min(rows // chunks, half // 2)
     out_count = rows // out_chunk
-    first, second = (2, 2, pairs), (PIECES, 15, chunks)
-    third = (PIECES * chunks // out_count, 12, out_count)
-    steps = PIECES * (chunks - 1) + second[1] + 1
+    first, second = (4, 0, pairs), (PIECES, 13, chunks)
+    third = (PIECES * chunks // out_count, 13, out_count)
+    steps = max(PIECES * (chunks - 1) + second[1], third[0] * (out_count - 1) + third[1]) + 1
     chunk = rows // chunks
-    after = 2 * pairs
+    after = 4 * (pairs - 1)
     slabs = slab_count(chunks)
     plan = types.SimpleNamespace(
-        slabs=(1, 9, slabs),
-        early=lambda k: min(slabs + 12 + 7 * k, steps - 2),
-        late_slabs=(1, after + 8, slabs),
-        late=lambda k: min(after + 10 + slabs + 5 * k, steps - 2),
+        slabs=(2, 0, slabs),
+        early=lambda k: min(2 * slabs + 1 + 7 * k, steps - 2),
+        late_slabs=(1, after + 3, slabs),
+        late=lambda k: min(after + 5 + slabs + 5 * k, steps - 2),
     )
 
     def body(r, s):
@@ -1416,10 +1417,10 @@
         r.arrived(first[1], *QKV_WEIGHTS)
         at_chunk(s, first, send_attn)
         grads.late_slabs(s)
-        at_chunk(s, (1, 2, half_pieces), upper.relay)
-        at_chunk(s, (1, 9, pieces), attn.relay)
-        at_chunk(s, (1, 4, half_pieces), upper.meet)
-        at_chunk(s, (1, 12, pieces), attn.meet)
+        at_chunk(s, (1, 0, half_pieces), upper.relay)
+        at_chunk(s, (1, 8, pieces), attn.relay)
+        at_chunk(s, (1, 2, half_pieces), upper.meet)
+        at_chunk(s, (1, 10, pieces), attn.meet)
         at_chunk(s, third, give_output)
         at_chunk(s, second, give_input)
         grads.run(s)

time: 516 us -> 512 us (level)
  no operation moved by 1% of the time
where the time goes in v5:
time: 512 us; the launch traced here: 510 us
  Pallas kernels  509 us (99%)
    pallas_call x7, Pallas kernels, step_kernel(): pl.pallas_call(kernel, grid=(steps,), in_specs=[spec(a.shape, w, True) fo...  501 us

profile of v5, /device:TPU:0, one launch (start us, length us, event | category | flops | bytes accessed | tf_op | source)
XLA Modules:
  0.0 510.3 jit_solution(13839730017731352640)
XLA Ops:
  0.6 10.8 %first_projection.1 = (bf16[1024,1024]{1,0:T(8,128)(2,1)}, f32[1024,768]{1,0:T(8,128)}, bf16[1024,512]{1,0:T(8,128)(2,1)}, bf16[2048,512]{1,0:T(8,128)(2,1)}, f32[1024,256]{1,0:T(8,128)}, /*index=5*/s32[1,1024]{1,0:T(1,128)}) custom-call(bf16[1024,1024]{1,0:T(8,128)(2,1)} %bitcast.4, s32[1,1024]{1,0:T(1,128)} %refs_1_.1, s32[1,1024]{1,0:T(1,128)} %refs_2_.1, ...), custom_call_target="tpu_custom_call" | custom-call | tf_op jit(solution)/shard_map/first_projection/pallas_call | solution.py:109
  11.5 116.0 %between_forward.1 = (bf16[1024,512]{1,0:T(8,128)(2,1)}, f32[2,2,1024]{2,1,0:T(2,128)}, f32[1024,1024]{1,0:T(8,128)}, bf16[1024,1024]{1,0:T(8,128)(2,1)}, f32[10...) custom-call(bf16[1024,512]{1,0:T(8,128)(2,1)} %get-tuple-element.88., ...), custom_call_target="tpu_custom_call" | custom-call | tf_op jit(solution)/shard_map/between_forward/pallas_call | solution.py:109
  127.5 115.8 %turn_around.1 = (bf16[1024,512]{1,0:T(8,128)(2,1)}, f32[2,2,1024]{2,1,0:T(2,128)}, bf16[1024,1024]{1,0:T(8,128)(2,1)}, bf16[1024,768]{1,0:T(8,128)(2,1)}, f32[1...) custom-call(bf16[1024,512]{1,0:T(8,128)(2,1)} %get-tuple-element.92., ...), custom_call_target="tpu_custom_call" | custom-call | tf_op jit(solution)/shard_map/turn_around/pallas_call | solution.py:109
  243.3 24.8 %attention_backward.2 = (f32[1024,512]{1,0:T(8,128)}, f32[2,1024,256]{2,1,0:T(8,128)}, bf16[1,2,1024,256]{3,2,1,0:T(8,128)(2,1)}, bf16[256,1024]{1,0:T(8,128)(2,1)}) custom-call(s32[1,1024]{1,0:T(1,128)} %get-tuple-element.87.refs_2_.refs_0_, f32[2,2,1024]{2,1,0:T(2,128)} %get-tuple-element.95.refs_1_, bf16[1024,512]{1,0:T(8,128)(2,1)} %get-tuple-element.92.refs_0_.refs_2_, ...), custom_call_target="tpu_custom_call" | custom-call | tf_op jit(solution)/shard_map/attention_backward/pallas_call | solution.py:109
  268.1 117.9 %between_backward.1 = (bf16[1024,1024]{1,0:T(8,128)(2,1)}, bf16[1024,1536]{1,0:T(8,128)(2,1)}, f32[1024,1024]{1,0:T(8,128)}, bf16[1024,1024]{1,0:T(8,128)(2,1)},...) custom-call(f32[1024,512]{1,0:T(8,128)} %get-tuple-element.99.refs_0, ...), custom_call_target="tpu_custom_call" | custom-call | tf_op jit(solution)/shard_map/between_backward/pallas_call | solution.py:109
  386.0 25.1 %attention_backward.3 = (f32[1024,512]{1,0:T(8,128)}, f32[2,1024,256]{2,1,0:T(8,128)}, bf16[1,2,1024,256]{3,2,1,0:T(8,128)(2,1)}, bf16[256,1024]{1,0:T(8,128)(2,1)}) custom-call(s32[1,1024]{1,0:T(1,128)} %get-tuple-element.87.refs_2_.refs_0_, f32[2,2,1024]{2,1,0:T(2,128)} %get-tuple-element.91.refs_1_, bf16[1024,512]{1,0:T(8,128)(2,1)} %get-tuple-element.88.refs_0_.refs_2_, ...), custom_call_target="tpu_custom_call" | custom-call | tf_op jit(solution)/shard_map/attention_backward/pallas_call | solution.py:109
  411.1 91.0 %last_backward.1 = (f32[1024,1024]{1,0:T(8,128)}, bf16[1024,1024]{1,0:T(8,128)(2,1)}, f32[8,1024]{1,0:T(8,128)}, f32[128,512]{1,0:T(8,128)}, f32[128,256]{1,0:T(...) custom-call(f32[1024,512]{1,0:T(8,128)} %get-tuple-element.113.refs_, ...), custom_call_target="tpu_custom_call" | custom-call | tf_op jit(solution)/shard_map/last_backward/pallas_call | solution.py:109
  502.1 8.0 %collect.1 = (bf16[1024,1024]{1,0:T(8,128)(2,1)}, f32[1024,1024]{1,0:T(8,128)}, f32[2,1024]{1,0:T(2,128)}, f32[2,1024]{1,0:T(2,128)}, f32[2,128]{1,0:T(2,128)}, ...) custom-call(bf16[1024,1024]{1,0:T(8,128)(2,1)} %get-tuple-element.13, ...), custom_call_target="tpu_custom_call" | custom-call | tf_op jit(solution)/shard_map/collect/pallas_call | solution.py:1544

commit v6 on v5

--- a/solution.py
+++ b/solution.py
@@ -1005,8 +1005,9 @@
         mask = jnp.concatenate([mask] * group, 1)
         scores = dot(keys, queries, NT) * (SCALE * LOG2E) - lse
         p = jnp.where(mask, jnp.exp2(scores), 0.0)
-        ds = (p * (dot(values, d_out, NT) - delta)).astype(BF)
-        r.d_values[here, :] += dot(p.astype(BF), d_out)
+        p = p.astype(BF)
+        ds = p * (dot(values, d_out, NT) - delta).astype(BF)
+        r.d_values[here, :] += dot(p, d_out)
         r.d_keys[here, :] += dot(ds, queries)
         dq = (dot(keys, ds, TN) * SCALE).T
         for h in range(group):

time: 512 us -> 511 us (level)
  no operation moved by 1% of the time
where the time goes in v6:
time: 511 us; the launch traced here: 510 us
  Pallas kernels  509 us (100%)
    pallas_call x7, Pallas kernels, step_kernel(): pl.pallas_call(kernel, grid=(steps,), in_specs=[spec(a.shape, w, True) fo...  501 us

profile of v6, /device:TPU:0, one launch (start us, length us, event | category | flops | bytes accessed | tf_op | source)
XLA Modules:
  0.0 509.9 jit_solution(15905198006421459760)
XLA Ops:
  0.6 10.8 %first_projection.1 = (bf16[1024,1024]{1,0:T(8,128)(2,1)}, f32[1024,768]{1,0:T(8,128)}, bf16[1024,512]{1,0:T(8,128)(2,1)}, bf16[2048,512]{1,0:T(8,128)(2,1)}, f32[1024,256]{1,0:T(8,128)}, /*index=5*/s32[1,1024]{1,0:T(1,128)}) custom-call(bf16[1024,1024]{1,0:T(8,128)(2,1)} %bitcast.4, s32[1,1024]{1,0:T(1,128)} %refs_1_.1, s32[1,1024]{1,0:T(1,128)} %refs_2_.1, ...), custom_call_target="tpu_custom_call" | custom-call | tf_op jit(solution)/shard_map/first_projection/pallas_call | solution.py:109
  11.5 116.0 %between_forward.1 = (bf16[1024,512]{1,0:T(8,128)(2,1)}, f32[2,2,1024]{2,1,0:T(2,128)}, f32[1024,1024]{1,0:T(8,128)}, bf16[1024,1024]{1,0:T(8,128)(2,1)}, f32[10...) custom-call(bf16[1024,512]{1,0:T(8,128)(2,1)} %get-tuple-element.88., ...), custom_call_target="tpu_custom_call" | custom-call | tf_op jit(solution)/shard_map/between_forward/pallas_call | solution.py:109
  127.5 115.8 %turn_around.1 = (bf16[1024,512]{1,0:T(8,128)(2,1)}, f32[2,2,1024]{2,1,0:T(2,128)}, bf16[1024,1024]{1,0:T(8,128)(2,1)}, bf16[1024,768]{1,0:T(8,128)(2,1)}, f32[1...) custom-call(bf16[1024,512]{1,0:T(8,128)(2,1)} %get-tuple-element.92., ...), custom_call_target="tpu_custom_call" | custom-call | tf_op jit(solution)/shard_map/turn_around/pallas_call | solution.py:109
  243.3 24.6 %attention_backward.2 = (f32[1024,512]{1,0:T(8,128)}, f32[2,1024,256]{2,1,0:T(8,128)}, bf16[1,2,1024,256]{3,2,1,0:T(8,128)(2,1)}, bf16[256,1024]{1,0:T(8,128)(2,1)}) custom-call(s32[1,1024]{1,0:T(1,128)} %get-tuple-element.87.refs_2_.refs_0_, f32[2,2,1024]{2,1,0:T(2,128)} %get-tuple-element.95.refs_1_, bf16[1024,512]{1,0:T(8,128)(2,1)} %get-tuple-element.92.refs_0_.refs_2_, ...), custom_call_target="tpu_custom_call" | custom-call | tf_op jit(solution)/shard_map/attention_backward/pallas_call | solution.py:109
  267.9 117.9 %between_backward.1 = (bf16[1024,1024]{1,0:T(8,128)(2,1)}, bf16[1024,1536]{1,0:T(8,128)(2,1)}, f32[1024,1024]{1,0:T(8,128)}, bf16[1024,1024]{1,0:T(8,128)(2,1)},...) custom-call(f32[1024,512]{1,0:T(8,128)} %get-tuple-element.99.refs_0, ...), custom_call_target="tpu_custom_call" | custom-call | tf_op jit(solution)/shard_map/between_backward/pallas_call | solution.py:109
  385.7 24.9 %attention_backward.3 = (f32[1024,512]{1,0:T(8,128)}, f32[2,1024,256]{2,1,0:T(8,128)}, bf16[1,2,1024,256]{3,2,1,0:T(8,128)(2,1)}, bf16[256,1024]{1,0:T(8,128)(2,1)}) custom-call(s32[1,1024]{1,0:T(1,128)} %get-tuple-element.87.refs_2_.refs_0_, f32[2,2,1024]{2,1,0:T(2,128)} %get-tuple-element.91.refs_1_, bf16[1024,512]{1,0:T(8,128)(2,1)} %get-tuple-element.88.refs_0_.refs_2_, ...), custom_call_target="tpu_custom_call" | custom-call | tf_op jit(solution)/shard_map/attention_backward/pallas_call | solution.py:109
  410.6 91.0 %last_backward.1 = (f32[1024,1024]{1,0:T(8,128)}, bf16[1024,1024]{1,0:T(8,128)(2,1)}, f32[8,1024]{1,0:T(8,128)}, f32[128,512]{1,0:T(8,128)}, f32[128,256]{1,0:T(...) custom-call(f32[1024,512]{1,0:T(8,128)} %get-tuple-element.113.refs_, ...), custom_call_target="tpu_custom_call" | custom-call | tf_op jit(solution)/shard_map/last_backward/pallas_call | solution.py:109
  501.7 8.0 %collect.1 = (bf16[1024,1024]{1,0:T(8,128)(2,1)}, f32[1024,1024]{1,0:T(8,128)}, f32[2,1024]{1,0:T(2,128)}, f32[2,1024]{1,0:T(2,128)}, f32[2,128]{1,0:T(2,128)}, ...) custom-call(bf16[1024,1024]{1,0:T(8,128)(2,1)} %get-tuple-element.13, ...), custom_call_target="tpu_custom_call" | custom-call | tf_op jit(solution)/shard_map/collect/pallas_call | solution.py:1545
